TPU v7x, 32 devices: a whole 2x2x4 slice. The times are simulated.
32 devices in a mesh: groups: 2 (over y), grid: 16 (over z, x, core).
Axes of the slice: x: 2, y: 2, z: 4, core: 2. Of those that a mesh axis runs over, the one named last changes fastest.
Arguments:
- tile_values: bfloat16 [1536, 4, 128, 128], P(('groups', 'grid')), parts along dimension 0, may hold values from -64 to 64
- tile_columns: int32 [192, 8, 4], P('groups'), parts along dimension 0, may hold values from 0 to 11, as said below
- keep_tiles: int32 [1536, 3], P(('groups', 'grid')), parts along dimension 0, may hold values 0 or 1
Outputs:
- inflated: float32 [1536, 3, 128, 128], P(('groups', 'grid')), parts along dimension 0
There are 2 independent parts, one for each index of `groups`. A program takes and returns all parts, laid end to end along the dimension named above; each array names one. Nothing has to cross between parts.
Inputs may be any that keep to these rules, and one draw needn't show every extreme that they name: `tile_columns`: for each block row and column strip the 4 entries are distinct; at most 3 of them are below 3, and in every block of 48 block rows of one grid row, within each column strip, some block row has exactly 3 such entries.
All inputs are finite; a program needn't handle non-finite values. No bound on the sum of `keep_tiles` on one device may be relied on, other than what follows from the above.
Results may differ from a plain program's by a relative error of at most 0.0003.
Values may be sent and summed in bfloat16 or wider, within the bound.
No kernel may reach another device: no remote copies, remote signals or barrier semaphores. Data moves between devices by JAX's collectives and lax.ppermute only.
A program may use at most 256 MiB of HBM per device.

v0:
```python
import jax
import jax.numpy as jnp
from jax import lax
from jax.sharding import PartitionSpec as P

GC = 8
CB = 12


def swapped(array, axis, bit):
    return lax.ppermute(array, axis, [(i, i ^ 1 << bit) for i in range(lax.axis_size(axis))])


def panel_from(tiles, columns, panel_width):
    matches = (columns[..., None] == jnp.arange(panel_width, dtype=jnp.int32)).astype(jnp.bfloat16)
    dense_panel = jnp.einsum(
        "qrtp,qrtab->qrpab", matches, tiles, preferred_element_type=jnp.float32
    )
    return dense_panel.astype(jnp.bfloat16)


def shards(tile_values, tile_columns, keep_tiles):
    devices = lax.axis_size("grid")
    device = lax.axis_index("grid")
    grid_rows = devices // GC
    row_strip = device // GC
    col_strip = device % GC
    block_rows = tile_values.shape[0]
    tile_width = tile_values.shape[-1]
    panel_width = CB // 4
    low_bits = GC.bit_length() - 1
    all_bits = devices.bit_length() - 1
    strip_rows = lax.dynamic_slice_in_dim(tile_columns, row_strip * block_rows, block_rows, 0)
    tier_ids = jnp.bitwise_xor(row_strip, jnp.arange(grid_rows, dtype=jnp.int32))
    row_ids = (
        tier_ids[:, None] * block_rows + jnp.arange(block_rows, dtype=jnp.int32)[None, :]
    ).reshape(-1)
    column_rows = jnp.take(tile_columns, row_ids, axis=0)
    column_pattern = lax.dynamic_index_in_dim(column_rows, col_strip, 1, keepdims=False).reshape(
        grid_rows, block_rows, -1
    )
    collected = tile_values[None]
    for bit_index in range(low_bits, all_bits):
        collected = jnp.concatenate([collected, swapped(collected, "grid", bit_index)], axis=0)
    panel = panel_from(collected, column_pattern, panel_width)
    panel_flat = panel.reshape(grid_rows * block_rows, panel_width, tile_width, tile_width)
    row_blocks = tile_values[None]
    for bit_index in range(low_bits):
        row_blocks = jnp.concatenate([row_blocks, swapped(row_blocks, "grid", bit_index)], axis=0)
    arrived_count = row_blocks.shape[0]
    strips = jnp.bitwise_xor(col_strip, jnp.arange(arrived_count, dtype=jnp.int32))
    pattern = jnp.take(strip_rows, strips, axis=1)
    columns = strips[None, :, None] * CB + pattern
    source = jnp.bitwise_xor(columns // block_rows, row_strip) * block_rows + columns % block_rows
    row_major = jnp.transpose(row_blocks, (1, 0, 2, 3, 4))

    def one_row(pair):
        row_tiles, row_source = pair
        gathered = jnp.take(panel_flat, row_source, axis=0)
        return jnp.einsum(
            "mtab,mtpbc->pac", row_tiles, gathered, preferred_element_type=jnp.float32
        )

    expanded = lax.map(one_row, (row_major, source))
    keep = keep_tiles.astype(jnp.float32)
    squared = expanded * expanded * keep[:, :, None, None]
    column_sums = jnp.sum(squared, axis=(0, 2))
    for bit_index in range(low_bits, all_bits):
        column_sums = column_sums + swapped(column_sums, "grid", bit_index)
    column_mean = column_sums / (CB * GC * tile_width)
    return squared / (column_mean[None, :, None, :] + 1e-06)


def solution(mesh):
    return jax.shard_map(
        shards,
        mesh=mesh,
        in_specs=(
            P(("groups", "grid"), None, None, None),
            P("groups", None, None),
            P(("groups", "grid"), None),
        ),
        out_specs=P(("groups", "grid"), None, None, None),
        check_vma=False,
    )
```

profile of v0, /device:TPU:0, one launch (start us, length us, event | category | flops | bytes accessed | tf_op | source)
XLA Modules:
  0.0 1720.5 jit_solution(37728409759888275)
XLA Ops:
  0.0 11.6 copy.39
  12.0 10.0 collective-permute-done.1
  22.0 11.0 pad_maximum_fusion.1
  36.0 270.7 %collective-permute-done.2 = bf16[2,48,4,128,128]{4,2,3,1,0:T(4,128)(2,1)} collective-permute-done((bf16[2,48,4,128,128]{4,2,3,1,0:T(4,128)(2,1)S(1)}, bf16[2,48,4,128,128]{4,2,3,1,0:T(4,128)(2,1)}, u32[]{:S(2)}, u32[]{:S(2)}) %collective-permute-start.2) | collective-permute-done | bytes 12582944 | tf_op jit(solution)/shard_map/ppermute | solution.py:11
  306.8 21.1 %pad_maximum_fusion = bf16[4,48,4,128,128]{4,2,3,1,0:T(4,128)(2,1)} fusion(bf16[2,48,4,128,128]{4,2,3,1,0:T(4,128)(2,1)} %collective-permute-done.2, bf16[1,48,4,128,128]{4,2,3,1,0:T(4,128)(2,1)S(1)} %collective-permute-done.1, bf16[1,48,4,128,128]{4,2,3,1,0:T(4,128)(2,1)} %bitcast.60), kind=kLoop, calls=%fused_computation.18 | loop fusion | flops 25165824 | bytes 50331648 | tf_op jit(solution)/shard_map/concatenate | solution.py:49
  336.5 667.2 %collective-permute-done = bf16[1,48,4,128,128]{4,2,3,1,0:T(4,128)(2,1)} collective-permute-done((bf16[1,48,4,128,128]{4,2,3,1,0:T(4,128)(2,1)}, bf16[1,48,4,128,128]{4,2,3,1,0:T(4,128)(2,1)}, u32[]{:S(2)}, u32[]{:S(2)}) %collective-permute-start) | collective-permute-done | bytes 6291488 | tf_op jit(solution)/shard_map/ppermute | solution.py:11
  1003.6 13.7 fusion.12
  1017.3 11.1 copy.21
  1028.4 40.2 %maximum_bitcast_fusion = bf16[48,8,4,128,128]{4,2,3,0,1:T(4,128)(2,1)} fusion(bf16[4,48,4,128,128]{4,2,3,1,0:T(4,128)(2,1)} %collective-permute-done.3, bf16[2,48,4,128,128]{4,2,3,1,0:T(4,128)(2,1)} %collective-permute-done.2, bf16[1,48,4,128,128]{4,2,3,1,0:T(4,128)(2,1)} %copy-done, bf16[1,48,4,128,128]{4,2,3,1,0:T(4,128)(2,1)} %bitcast.60), kind=kLoop, calls=%fused_computation.17 | loop fusion | flops 75497472 | bytes 100663296 | tf_op jit(solution)/shard_map/transpose | solution.py:55
  1068.6 636.7 %while.10 = (s32[]{:T(128)}, f32[48,3,128,128]{3,2,1,0:T(8,128)}, s32[48,8,4]{1,2,0:T(4,128)S(1)}, bf16[96,3,128,128]{3,2,1,0:T(8,128)(2,1)}, bf16[48,8,4,128,128]{4,2,3,0,1:T(4,128)(2,1)}, /*index=5*/s32[]{:T(128)}) while((s32[]{:T(128)}, f32[48,3,128,128]{3,2,1,0:T(8,128)}, s32[48,8,4]{1,2,0:T(4,128)S(1)}, ...), condition=%wide.region_1.2_spmd, body=%wide.region_0.1_spmd.sunk | while | flops 404227360 | bytes 19863376 | solution.py:64
  1068.8 4.8 gather_fusion
  1095.4 4.8 gather_fusion
  1135.2 4.8 gather_fusion
  1148.4 4.8 gather_fusion
  1175.0 4.8 gather_fusion
  1188.2 4.8 gather_fusion
  1228.0 4.8 gather_fusion
  1267.8 4.8 gather_fusion
  1281.1 4.8 gather_fusion
  1307.6 4.8 gather_fusion
  1320.9 4.8 gather_fusion
  1360.7 4.8 gather_fusion
  1387.2 4.8 gather_fusion
  1400.5 4.8 gather_fusion
  1413.7 4.8 gather_fusion
  1440.3 4.8 gather_fusion
  1493.3 4.8 gather_fusion
  1519.9 4.8 gather_fusion
  1533.1 4.8 gather_fusion
  1546.4 4.8 gather_fusion
  1705.4 5.2 fusion.14
  1715.6 4.9 fusion.13
  (593 shorter events, 555.8 us)
Async XLA Ops:
  11.6 10.4 collective-permute-start.1
  22.0 284.7 %copy-start = (bf16[1,48,4,128,128]{4,2,3,1,0:T(4,128)(2,1)}, bf16[1,48,4,128,128]{4,2,3,1,0:T(4,128)(2,1)S(1)}, u32[]{:S(2)}) copy-start(bf16[1,48,4,128,128]{4,2,3,1,0:T(4,128)(2,1)S(1)} %collective-permute-done.1) | copy-start | bytes 18874372
  33.1 299.5 %copy-start.2 = (s32[96,8,4]{0,2,1:T(4,128)S(1)}, s32[96,8,4]{0,2,1:T(4,128)}, u32[]{:S(2)}) copy-start(s32[96,8,4]{0,2,1:T(4,128)} %param.6) | copy-start | bytes 36868
  33.1 300.6 %copy-start.3 = (s32[48,3]{0,1:T(4,128)S(1)}, s32[48,3]{0,1:T(4,128)}, u32[]{:S(2)}) copy-start(s32[48,3]{0,1:T(4,128)} %param.7) | copy-start | bytes 1732
  33.1 273.7 %collective-permute-start.2 = (bf16[2,48,4,128,128]{4,2,3,1,0:T(4,128)(2,1)S(1)}, bf16[2,48,4,128,128]{4,2,3,1,0:T(4,128)(2,1)}, u32[]{:S(2)}, u32[]{:S(2)}) collective-permute-start(bf16[2,48,4,128,128]{4,2,3,1,0:T(4,128)(2,1)S(1)} %pad_maximum_fusion.1), channel_id=1, source_target_pairs={{0,2},{1,3},{2,0},{3,1},{4,6},{5,7},{6,4},{7,5},{8,10},{9,11},{10,... | collective-permute-start | bytes 37748744 | tf_op jit(solution)/shard_map/ppermute | solution.py:11
  327.9 700.5 %collective-permute-start.3 = (bf16[4,48,4,128,128]{4,2,3,1,0:T(4,128)(2,1)}, bf16[4,48,4,128,128]{4,2,3,1,0:T(4,128)(2,1)}, u32[]{:S(2)}, u32[]{:S(2)}) collective-permute-start(bf16[4,48,4,128,128]{4,2,3,1,0:T(4,128)(2,1)} %pad_maximum_fusion), channel_id=1, source_target_pairs={{0,4},{1,5},{2,6},{3,7},{4,0},{5,1},{6,2},{7,3},{8,12},{9,13},{10,... | collective-permute-start | bytes 75497480 | tf_op jit(solution)/shard_map/ppermute | solution.py:11
  329.8 673.9 %collective-permute-start = (bf16[1,48,4,128,128]{4,2,3,1,0:T(4,128)(2,1)}, bf16[1,48,4,128,128]{4,2,3,1,0:T(4,128)(2,1)}, u32[]{:S(2)}, u32[]{:S(2)}) collective-permute-start(bf16[1,48,4,128,128]{4,2,3,1,0:T(4,128)(2,1)} %bitcast.60), channel_id=1, source_target_pairs={{0,8},{1,9},{2,10},{3,11},{4,12},{5,13},{6,14},{7,15},{8,0},{9,1},... | collective-permute-start | bytes 18874376 | tf_op jit(solution)/shard_map/ppermute | solution.py:11
  1705.4 10.2 copy-start.1
  1710.6 5.0 collective-permute-start.4
where the time goes:
time: 1730 us; the launch traced here: 1720 us
  waiting for transfers between devices  949 us (55%)
  local copies, waits for them, and re-layouts  520 us (30%)
  matrix products  153 us (9%)
  other arithmetic  85.5 us (5%)
    ppermute x5, waiting for transfers between devices, swapped(): lax.ppermute(array, axis, [(i, i ^ 1 << bit) for i in range(lax.axis_size...  949 us
    gather x96, local copies, waits for them, and re-layouts, one_row(): gathered = jnp.take(panel_flat, row_source, axis=0)  367 us
    dot_general x48, matrix products, one_row(): jnp.einsum('mtab,mtpbc->pac', row_tiles, gathered, preferred_element_type...  140 us
    dynamic_slice x48, local copies, waits for them, and re-layouts, shards(): expanded = lax.map(one_row, (row_major, source))  76.2 us
    transpose x1, other arithmetic, shards(): row_major = jnp.transpose(row_blocks, (1, 0, 2, 3, 4))  40.2 us
    dynamic_update_slice x96, local copies, waits for them, and re-layouts, shards(): expanded = lax.map(one_row, (row_major, source))  39.6 us
  transfers between devices with their start and end apart: 5, of which 4 were waited for; matrix products, arithmetic and copies ran while one was open for 2% of the time, Pallas kernels for 0%

commit v1 on v0

v1 whole, which is shorter than its diff:
```python
import functools
import math

import jax
import jax.numpy as jnp
from jax import lax
from jax.experimental import pallas as pl
from jax.experimental.pallas import tpu as pltpu
from jax.sharding import PartitionSpec as P

GC = 8
CB = 12
PC = CB // 4
STRIPS = GC // 2
MIB = 1 << 20


def swapped(array, mask):
    return lax.ppermute(array, "grid", [(i, i ^ mask) for i in range(lax.axis_size("grid"))])


def panel_kernel(slot_ref, tiles_ref, panel_ref):
    rows, _, width, _ = tiles_ref.shape
    first = pl.program_id(0) * rows

    @pl.loop(0, rows)
    def _(r):
        for p in range(PC):
            slot = slot_ref[(first + r) * PC + p]
            tile = tiles_ref[r, jnp.maximum(slot, 0)]
            panel_ref[r, :, p * width : (p + 1) * width] = jnp.where(
                slot >= 0, tile, jnp.zeros_like(tile)
            )


def make_panel(tile_values, slots):
    block_rows, slots_per_row, width, _ = tile_values.shape
    step = math.gcd(block_rows, 12)
    return pl.pallas_call(
        panel_kernel,
        grid_spec=pltpu.PrefetchScalarGridSpec(
            num_scalar_prefetch=1,
            grid=(block_rows // step,),
            in_specs=[pl.BlockSpec((step, slots_per_row, width, width), lambda i, s: (i, 0, 0, 0))],
            out_specs=pl.BlockSpec((step, width, PC * width), lambda i, s: (i, 0, 0)),
        ),
        out_shape=jax.ShapeDtypeStruct((block_rows, width, PC * width), jnp.bfloat16),
        compiler_params=pltpu.CompilerParams(vmem_limit_bytes=40 * MIB),
        cost_estimate=pl.CostEstimate(flops=0, bytes_accessed=11_000_000, transcendentals=0),
        name="panel",
    )(slots.reshape(-1), tile_values)


def expand_kernel(chunks, parts, where_ref, index_ref, *refs):
    chunk_refs = refs[: chunks * STRIPS]
    panel_refs = refs[chunks * STRIPS : chunks * STRIPS + 2 * parts]
    mine_ref, other_ref, panel, tiles, sums, panel_sem, tile_sem, sum_sem = refs[
        chunks * STRIPS + 2 * parts :
    ]
    rows, slots, width, _ = chunk_refs[0].shape
    part_rows = panel_refs[0].shape[0]
    unit = math.gcd(CB, part_rows)
    units = CB // unit
    half = PC * width

    for q in range(STRIPS):
        for u in range(units):
            part = where_ref[2 * (q * units + u)]
            offset = where_ref[2 * (q * units + u) + 1]
            for n in range(parts):

                @pl.when(part == n)
                def _():
                    for side in range(2):
                        pltpu.make_async_copy(
                            panel_refs[side * parts + n].at[pl.ds(offset, unit)],
                            panel.at[
                                pl.ds(q * CB + u * unit, unit), :, pl.ds(side * half, half)
                            ],
                            panel_sem.at[side],
                        ).start()

    def fetch(k):
        return [
            pltpu.make_async_copy(
                chunk_refs[k * STRIPS + q], tiles.at[k % 2, q], tile_sem.at[k % 2, q]
            )
            for q in range(STRIPS)
        ]

    for copy in fetch(0):
        copy.start()
    for side in range(2):
        pltpu.make_async_copy(
            panel.at[:, :, pl.ds(side * half, half)],
            panel.at[:, :, pl.ds(side * half, half)],
            panel_sem.at[side],
        ).wait()

    def stores(row, slot):
        return [
            pltpu.make_async_copy(
                sums.at[slot, :, pl.ds(side * half, half)], out.at[row], sum_sem.at[slot, side]
            )
            for side, out in enumerate((mine_ref, other_ref))
        ]

    for k in range(chunks):
        if k + 1 < chunks:
            for copy in fetch(k + 1):
                copy.start()
        for copy in fetch(k):
            copy.wait()

        @pl.loop(0, rows)
        def _(r):
            row = k * rows + r
            slot = lax.rem(row, 2)

            @pl.when(row >= 2)
            def _():
                for copy in stores(row - 2, slot):
                    copy.wait()

            total = None
            for q in range(STRIPS):
                for t in range(0, slots, 2):
                    base = row * (STRIPS * slots) + q * slots + t
                    left = jnp.concatenate(
                        [tiles[k % 2, q, r, t], tiles[k % 2, q, r, t + 1]], axis=1
                    )
                    right = jnp.concatenate(
                        [panel[index_ref[base]], panel[index_ref[base + 1]]], axis=0
                    )
                    term = jnp.dot(left, right, preferred_element_type=jnp.float32)
                    total = term if total is None else total + term
            sums[slot] = total
            for copy in stores(row, slot):
                copy.start()

    for row in range(max(chunks * rows - 2, 0), chunks * rows):
        for copy in stores(row, row % 2):
            copy.wait()


def expand(chunk_list, panels, others, where, index):
    chunks = len(chunk_list)
    parts = len(panels)
    rows, slots, width, _ = chunk_list[0][0].shape
    total_rows = chunks * rows
    half = jax.ShapeDtypeStruct((total_rows, width, PC * width), jnp.float32)
    anywhere = pl.BlockSpec(memory_space=pl.ANY)
    smem = pl.BlockSpec(memory_space=pltpu.SMEM)
    operands = [a for chunk in chunk_list for a in chunk] + list(panels) + list(others)
    return pl.pallas_call(
        functools.partial(expand_kernel, chunks, parts),
        out_shape=(half, half),
        in_specs=[smem, smem] + [anywhere] * len(operands),
        out_specs=(anywhere, anywhere),
        scratch_shapes=[
            pltpu.VMEM((STRIPS * CB, width, 2 * PC * width), jnp.bfloat16),
            pltpu.VMEM((2, STRIPS, rows, slots, width, width), jnp.bfloat16),
            pltpu.VMEM((2, width, 2 * PC * width), jnp.float32),
            pltpu.SemaphoreType.DMA((2,)),
            pltpu.SemaphoreType.DMA((2, STRIPS)),
            pltpu.SemaphoreType.DMA((2, 2)),
        ],
        compiler_params=pltpu.CompilerParams(vmem_limit_bytes=48 * MIB),
        cost_estimate=pl.CostEstimate(
            flops=2 * total_rows * STRIPS * slots * width * width * 2 * PC * width * 2,
            bytes_accessed=30_000_000,
            transcendentals=0,
        ),
        name="expand",
    )(where, index.reshape(-1), *operands)


def square_kernel(keep_ref, mine_ref, got_ref, squared_ref, sums_ref):
    rows, width, _ = mine_ref.shape
    first = pl.program_id(0) * rows

    @pl.when(pl.program_id(0) == 0)
    def _():
        sums_ref[...] = jnp.zeros_like(sums_ref)

    @pl.loop(0, rows)
    def _(r):
        for p in range(PC):
            keep = keep_ref[(first + r) * PC + p].astype(jnp.float32)
            cols = slice(p * width, (p + 1) * width)
            value = mine_ref[r, :, cols] + got_ref[r, :, cols]
            value = value * value * keep
            squared_ref[r, :, cols] = value
            sums_ref[:, cols] += jnp.sum(value.reshape(width // 8, 8, width), axis=0)


def square(keep, mine, got):
    rows, width, half = mine.shape
    step = math.gcd(rows, 6)
    block = pl.BlockSpec((step, width, half), lambda i, s: (i, 0, 0))
    return pl.pallas_call(
        square_kernel,
        grid_spec=pltpu.PrefetchScalarGridSpec(
            num_scalar_prefetch=1,
            grid=(rows // step,),
            in_specs=[block, block],
            out_specs=(block, pl.BlockSpec((8, half), lambda i, s: (0, 0))),
        ),
        out_shape=(
            jax.ShapeDtypeStruct(mine.shape, jnp.float32),
            jax.ShapeDtypeStruct((8, half), jnp.float32),
        ),
        compiler_params=pltpu.CompilerParams(vmem_limit_bytes=40 * MIB),
        name="square",
    )(keep.reshape(-1), mine, got)


def scale_kernel(bounds, mean_ref, *refs):
    pieces, out_ref = refs[:-1], refs[-1]
    step, width, _ = pieces[0].shape
    at = pl.program_id(0) * step
    for n, piece in enumerate(pieces):

        @pl.when((at >= bounds[n]) & (at < bounds[n + 1]))
        def _():
            for p in range(PC):
                cols = slice(p * width, (p + 1) * width)
                inverse = 1.0 / (mean_ref[0:1, cols] + 1e-6)
                for r in range(step):
                    out_ref[r, p] = piece[r, :, cols] * inverse


def scale(mean, pieces):
    _, width, half = pieces[0].shape
    step = functools.reduce(math.gcd, [p.shape[0] for p in pieces])
    bounds = [0]
    for p in pieces:
        bounds.append(bounds[-1] + p.shape[0])

    def block_of(n):
        low, count = bounds[n] // step, pieces[n].shape[0] // step
        return pl.BlockSpec(
            (step, width, half), lambda i: (jnp.clip(i - low, 0, count - 1), 0, 0)
        )

    return pl.pallas_call(
        functools.partial(scale_kernel, tuple(bounds)),
        grid=(bounds[-1] // step,),
        in_specs=[pl.BlockSpec((1, half), lambda i: (0, 0))]
        + [block_of(n) for n in range(len(pieces))],
        out_specs=pl.BlockSpec((step, PC, width, width), lambda i: (i, 0, 0, 0)),
        out_shape=jax.ShapeDtypeStruct((bounds[-1], PC, width, width), jnp.float32),
        compiler_params=pltpu.CompilerParams(vmem_limit_bytes=48 * MIB),
        name="scale",
    )(mean, *pieces)


class Lane:
    def __init__(self, window):
        self.window = window
        self.sent = []

    def send(self, array, mask):
        if len(self.sent) >= self.window:
            array, _ = lax.optimization_barrier((array, self.sent[-self.window]))
        out = swapped(array, mask)
        self.sent.append(out)
        return out


def shards(tile_values, tile_columns, keep_tiles):
    devices = lax.axis_size("grid")
    device = lax.axis_index("grid")
    all_bits = devices.bit_length() - 1
    low_bits = GC.bit_length() - 1
    row_strip = device // GC
    col_strip = device % GC
    block_rows, slots, width, _ = tile_values.shape
    chunks = math.gcd(block_rows, 8)
    rows = block_rows // chunks

    strip_rows = lax.dynamic_slice_in_dim(tile_columns, row_strip * block_rows, block_rows, 0)
    strips = jnp.bitwise_xor(col_strip, 2 * jnp.arange(STRIPS, dtype=jnp.int32))
    pattern = jnp.take(strip_rows, strips, axis=1)
    own = pattern[:, 0]
    match = own[:, :, None] == jnp.arange(PC, dtype=jnp.int32)
    slot = jnp.max(
        jnp.where(match, jnp.arange(slots, dtype=jnp.int32)[None, :, None], -1), axis=1
    )
    index = pattern + CB * jnp.arange(STRIPS, dtype=jnp.int32)[None, :, None]
    index = index.reshape(block_rows, STRIPS * slots)
    unit = math.gcd(CB, block_rows)
    unit_rows = strips[:, None] * CB + unit * jnp.arange(CB // unit, dtype=jnp.int32)
    where = jnp.stack(
        [jnp.bitwise_xor(unit_rows // block_rows, row_strip), unit_rows % block_rows], axis=-1
    ).reshape(-1)

    panels = [make_panel(tile_values, slot)]
    for bit in range(low_bits, all_bits):
        panels = panels + [swapped(p, 1 << bit) for p in panels]
    others = [swapped(p, 1) for p in panels]

    own_chunks = [lax.slice_in_dim(tile_values, k * rows, (k + 1) * rows) for k in range(chunks)]
    x_lane, z_lane = Lane(2), Lane(2)
    from_x, from_z, from_xz = [], [], []
    for k in range(chunks):
        from_x.append(x_lane.send(own_chunks[k], 2))
        from_z.append(z_lane.send(own_chunks[k], 4))
        if k > 0:
            from_xz.append(x_lane.send(from_z[k - 1], 2))
    from_xz.append(z_lane.send(from_x[chunks - 1], 4))

    squares, sums = [], []
    first = 0
    for count in (chunks - 3, 2, 1) if chunks > 3 else (chunks,):
        ks = range(first, first + count)
        lo, hi = first * rows, (first + count) * rows
        mine, other = expand(
            [(own_chunks[k], from_x[k], from_z[k], from_xz[k]) for k in ks],
            panels,
            others,
            where,
            index[lo:hi],
        )
        squared, total = square(keep_tiles[lo:hi], mine, swapped(other, 1))
        squares.append(squared)
        sums.append(jnp.sum(total, axis=0, keepdims=True))
        first += count
    column_sums = functools.reduce(jnp.add, sums)
    for bit in range(low_bits, all_bits):
        column_sums = column_sums + swapped(column_sums, 1 << bit)
    column_mean = column_sums / (CB * GC * width)
    return scale(column_mean, squares)


def solution(mesh):
    return jax.shard_map(
        shards,
        mesh=mesh,
        in_specs=(
            P(("groups", "grid"), None, None, None),
            P("groups", None, None),
            P(("groups", "grid"), None),
        ),
        out_specs=P(("groups", "grid"), None, None, None),
        check_vma=False,
    )
```

time: 1730 us -> 563 us (0.33)
  waiting for transfers between devices: 949 us -> 410 us
  local copies, waits for them, and re-layouts: 520 us -> 39.4 us
  matrix products: 153 us -> 0 us
  other arithmetic: 85.5 us -> 2.65 us
  Pallas kernels: 0 us -> 70 us
  starting transfers between devices: 11.3 us -> 39.7 us
    ppermute x5 -> x31, waiting for transfers between devices: 949 us -> 410 us  [swapped(): lax.ppermute(array, 'grid', [(i, i ^ mask) for i in range(lax.axis_size('...]
    gather x97 -> x0, local copies, waits for them, and re-layouts: 367 us -> none  [the longest x96 367 us: one_row(): gathered = jnp.take(panel_flat, row_source, axis=0)]
    dot_general x49 -> x0, matrix products: 153 us -> none  [the longest x48 140 us: one_row(): jnp.einsum('mtab,mtpbc->pac', row_tiles, gathered, preferred_element_type...]
    dynamic_slice x48 -> x0, local copies, waits for them, and re-layouts: 76.2 us -> none  [shards(): expanded = lax.map(one_row, (row_major, source))]
    pallas_call x0 -> x8, Pallas kernels: none -> 70 us  [the longest x3 47.7 us: expand(): pl.pallas_call(functools.partial(expand_kernel, chunks, parts), out_shape...]
    transpose x1 -> x0, other arithmetic: 40.2 us -> none  [shards(): row_major = jnp.transpose(row_blocks, (1, 0, 2, 3, 4))]
    dynamic_update_slice x96 -> x0, local copies, waits for them, and re-layouts: 39.6 us -> none  [shards(): expanded = lax.map(one_row, (row_major, source))]
    concatenate x2 -> x0, other arithmetic: 32.1 us -> none  [shards(): jnp.concatenate([row_blocks, swapped(row_blocks, 'grid', bit_index)], axi...]
  transfers between devices with their start and end apart: 5 -> 31, of which waited for: 4 -> 18; matrix products, arithmetic and copies ran while one was open for 2% -> 1% of each run, Pallas kernels for 0% -> 5%
where the time goes in v1:
time: 563 us; the launch traced here: 562 us
  waiting for transfers between devices  410 us (73%)
  Pallas kernels  70 us (12%)
  starting transfers between devices  39.7 us (7%)
  local copies, waits for them, and re-layouts  39.4 us (7%)
    ppermute x31, waiting for transfers between devices, swapped(): lax.ppermute(array, 'grid', [(i, i ^ mask) for i in range(lax.axis_size('...  410 us
    pallas_call x3, Pallas kernels, expand(): pl.pallas_call(functools.partial(expand_kernel, chunks, parts), out_shape...  47.7 us
    ppermute x31, starting transfers between devices, swapped(): lax.ppermute(array, 'grid', [(i, i ^ mask) for i in range(lax.axis_size('...  39.7 us
    unnamed x86, local copies, waits for them, and re-layouts  34.5 us
  transfers between devices with their start and end apart: 31, of which 18 were waited for; matrix products, arithmetic and copies ran while one was open for 1% of the time, Pallas kernels for 5%

profile of v1, /device:TPU:0, one launch (start us, length us, event | category | flops | bytes accessed | tf_op | source)
XLA Modules:
  0.0 561.9 jit_solution(12735628333194780805)
XLA Ops:
  1.7 2.8 copy-done.2
  4.5 3.9 panel.1.refs_20_.refs_8_.refs_4_
  8.4 4.0 collective-permute-start.15
  12.4 2.4 fusion.7
  14.8 1.6 collective-permute-start.1
  17.9 197.7 %collective-permute-done.15.refs_21_.refs_9_.refs_5_ = bf16[48,128,384]{2,1,0:T(8,128)(2,1)} collective-permute-done((bf16[48,128,384]{2,1,0:T(8,128)(2,1)}, bf16[48,128,384]{2,1,0:T(8,128)(2,1)}, u32[]{:S(2)}, u32[]{:S(2)}) %collective-permute-start.15) | collective-permute-done | bytes 4718624 | tf_op jit(solution)/shard_map/ppermute | solution.py:19
  221.1 14.5 %collective-permute-done.4.refs_6_ = bf16[6,4,128,128]{3,2,1,0:T(8,128)(2,1)S(1)} collective-permute-done((bf16[6,4,128,128]{3,2,1,0:T(8,128)(2,1)S(1)}, bf16[6,4,128,128]{3,2,1,0:T(8,128)(2,1)S(1)}, u32[]{:S(2)}, u32[]{:S(2)}) %collective-permute-start.4) | collective-permute-done | bytes 786464 | tf_op jit(solution)/shard_map/ppermute | solution.py:19
  240.9 13.6 %collective-permute-done.3.refs_5_ = bf16[6,4,128,128]{3,2,1,0:T(8,128)(2,1)S(1)} collective-permute-done((bf16[6,4,128,128]{3,2,1,0:T(8,128)(2,1)S(1)}, bf16[6,4,128,128]{3,2,1,0:T(8,128)(2,1)S(1)}, u32[]{:S(2)}, u32[]{:S(2)}) %collective-permute-start.3) | collective-permute-done | bytes 786464 | tf_op jit(solution)/shard_map/ppermute | solution.py:19
  258.3 13.1 %collective-permute-done.5.refs_7_ = bf16[6,4,128,128]{3,2,1,0:T(8,128)(2,1)S(1)} collective-permute-done((bf16[6,4,128,128]{3,2,1,0:T(8,128)(2,1)S(1)}, bf16[6,4,128,128]{3,2,1,0:T(8,128)(2,1)S(1)}, u32[]{:S(2)}, u32[]{:S(2)}) %collective-permute-start.5) | collective-permute-done | bytes 786464 | tf_op jit(solution)/shard_map/ppermute | solution.py:19
  272.9 15.4 %collective-permute-done.6.refs_9_ = bf16[6,4,128,128]{3,2,1,0:T(8,128)(2,1)S(1)} collective-permute-done((bf16[6,4,128,128]{3,2,1,0:T(8,128)(2,1)S(1)}, bf16[6,4,128,128]{3,2,1,0:T(8,128)(2,1)S(1)}, u32[]{:S(2)}, u32[]{:S(2)}) %collective-permute-start.6) | collective-permute-done | bytes 786464 | tf_op jit(solution)/shard_map/ppermute | solution.py:19
  291.1 14.0 %collective-permute-done.8.refs_11_ = bf16[6,4,128,128]{3,2,1,0:T(8,128)(2,1)S(1)} collective-permute-done((bf16[6,4,128,128]{3,2,1,0:T(8,128)(2,1)S(1)}, bf16[6,4,128,128]{3,2,1,0:T(8,128)(2,1)S(1)}, u32[]{:S(2)}, u32[]{:S(2)}) %collective-permute-start.8) | collective-permute-done | bytes 786464 | tf_op jit(solution)/shard_map/ppermute | solution.py:19
  306.6 15.4 %collective-permute-done.9.refs_13_ = bf16[6,4,128,128]{3,2,1,0:T(8,128)(2,1)S(1)} collective-permute-done((bf16[6,4,128,128]{3,2,1,0:T(8,128)(2,1)S(1)}, bf16[6,4,128,128]{3,2,1,0:T(8,128)(2,1)S(1)}, u32[]{:S(2)}, u32[]{:S(2)}) %collective-permute-start.9) | collective-permute-done | bytes 786464 | tf_op jit(solution)/shard_map/ppermute | solution.py:19
  323.4 15.4 %collective-permute-done.11.refs_15_ = bf16[6,4,128,128]{3,2,1,0:T(8,128)(2,1)S(1)} collective-permute-done((bf16[6,4,128,128]{3,2,1,0:T(8,128)(2,1)S(1)}, bf16[6,4,128,128]{3,2,1,0:T(8,128)(2,1)S(1)}, u32[]{:S(2)}, u32[]{:S(2)}) %collective-permute-start.11) | collective-permute-done | bytes 786464 | tf_op jit(solution)/shard_map/ppermute | solution.py:19
  340.8 14.9 %collective-permute-done.12.refs_17_ = bf16[6,4,128,128]{3,2,1,0:T(8,128)(2,1)} collective-permute-done((bf16[6,4,128,128]{3,2,1,0:T(8,128)(2,1)}, bf16[6,4,128,128]{3,2,1,0:T(8,128)(2,1)}, u32[]{:S(2)}, u32[]{:S(2)}) %collective-permute-start.12) | collective-permute-done | bytes 786464 | tf_op jit(solution)/shard_map/ppermute | solution.py:19
  355.7 16.1 %collective-permute-done.14.refs_19_ = bf16[6,4,128,128]{3,2,1,0:T(8,128)(2,1)} collective-permute-done((bf16[6,4,128,128]{3,2,1,0:T(8,128)(2,1)}, bf16[6,4,128,128]{3,2,1,0:T(8,128)(2,1)}, u32[]{:S(2)}, u32[]{:S(2)}) %collective-permute-start.14) | collective-permute-done | bytes 786464 | tf_op jit(solution)/shard_map/ppermute | solution.py:19
  378.7 25.0 %expand.3 = (f32[30,128,384]{2,1,0:T(8,128)}, f32[30,128,384]{2,1,0:T(8,128)}) custom-call(s32[8]{0:T(128)S(1)} %reshape.155.where_ref, s32[480]{0:T(512)S(1)} %reshape.156.index_ref, bf16[6,4,128,128]{3,2,1,0:T(8,128)(2,1)S(1)} %get-tuple-element.71.refs_0_, bf16[6,4,128,128]{3,2,1,0:T(8,128)(2,1)S(1)} %copy-done.17, ...), custom_call_target="tpu_custom_call" | custom-call | flops 24159191040 | bytes 30000000 | tf_op jit(solution)/shard_map/expand/pallas_call | solution.py:155
  403.8 1.6 collective-permute-start.19
  406.7 17.0 %collective-permute-done.19.refs_1_ = bf16[6,4,128,128]{3,2,1,0:T(8,128)(2,1)S(1)} collective-permute-done((bf16[6,4,128,128]{3,2,1,0:T(8,128)(2,1)S(1)}, bf16[6,4,128,128]{3,2,1,0:T(8,128)(2,1)S(1)}, u32[]{:S(2)}, u32[]{:S(2)}) %collective-permute-start.19) | collective-permute-done | bytes 786464 | tf_op jit(solution)/shard_map/ppermute | solution.py:19
  428.8 16.2 %collective-permute-done.22.refs_5_ = bf16[6,4,128,128]{3,2,1,0:T(8,128)(2,1)S(1)} collective-permute-done((bf16[6,4,128,128]{3,2,1,0:T(8,128)(2,1)S(1)}, bf16[6,4,128,128]{3,2,1,0:T(8,128)(2,1)S(1)}, u32[]{:S(2)}, u32[]{:S(2)}) %collective-permute-start.22) | collective-permute-done | bytes 786464 | tf_op jit(solution)/shard_map/ppermute | solution.py:19
  447.5 14.5 %collective-permute-done.21.refs_3_ = bf16[6,4,128,128]{3,2,1,0:T(8,128)(2,1)S(1)} collective-permute-done((bf16[6,4,128,128]{3,2,1,0:T(8,128)(2,1)S(1)}, bf16[6,4,128,128]{3,2,1,0:T(8,128)(2,1)S(1)}, u32[]{:S(2)}, u32[]{:S(2)}) %collective-permute-start.21) | collective-permute-done | bytes 786464 | tf_op jit(solution)/shard_map/ppermute | solution.py:19
  466.1 12.8 %collective-permute-done.26.refs_1_ = bf16[6,4,128,128]{3,2,1,0:T(8,128)(2,1)} collective-permute-done((bf16[6,4,128,128]{3,2,1,0:T(8,128)(2,1)S(1)}, bf16[6,4,128,128]{3,2,1,0:T(8,128)(2,1)}, u32[]{:S(2)}, u32[]{:S(2)}) %collective-permute-start.26) | collective-permute-done | bytes 786464 | tf_op jit(solution)/shard_map/ppermute | solution.py:19
  480.2 14.1 %collective-permute-done.24.refs_7_ = bf16[6,4,128,128]{3,2,1,0:T(8,128)(2,1)S(1)} collective-permute-done((bf16[6,4,128,128]{3,2,1,0:T(8,128)(2,1)}, bf16[6,4,128,128]{3,2,1,0:T(8,128)(2,1)S(1)}, u32[]{:S(2)}, u32[]{:S(2)}) %collective-permute-start.24) | collective-permute-done | bytes 786464 | tf_op jit(solution)/shard_map/ppermute | solution.py:19
  499.8 13.1 %expand.4 = (f32[12,128,384]{2,1,0:T(8,128)}, f32[12,128,384]{2,1,0:T(8,128)}) custom-call(s32[8]{0:T(128)S(1)} %reshape.155.where_ref, s32[192]{0:T(256)S(1)} %reshape.159.index_ref, bf16[6,4,128,128]{3,2,1,0:T(8,128)(2,1)S(1)} %get-tuple-element.52.refs_0_, bf16[6,4,128,128]{3,2,1,0:T(8,128)(2,1)S(1)} %copy-done.25, ...), custom_call_target="tpu_custom_call" | custom-call | flops 9663676416 | bytes 30000000 | tf_op jit(solution)/shard_map/expand/pallas_call | solution.py:155
  513.3 9.6 %expand.5 = (f32[6,128,384]{2,1,0:T(8,128)S(1)}, f32[6,128,384]{2,1,0:T(8,128)}) custom-call(s32[8]{0:T(128)S(1)} %reshape.155.where_ref, s32[96]{0:T(128)S(1)} %reshape.161.index_ref, bf16[6,4,128,128]{3,2,1,0:T(8,128)(2,1)S(1)} %get-tuple-element.61.refs_0_, bf16[6,4,128,128]{3,2,1,0:T(8,128)(2,1)} %collective-permute-done.26.refs_1_, ...), custom_call_target="tpu_custom_call" | custom-call | flops 4831838208 | bytes 30000000 | tf_op jit(solution)/shard_map/expand/pallas_call | solution.py:155
  525.1 2.1 collective-permute-done.29.got_ref
  528.5 2.0 square.5
  532.2 2.4 square.4
  536.6 2.7 copy-done.3
  539.3 5.4 square.3
  544.7 2.5 copy-done.4
  548.5 3.4 collective-permute-start.30
  553.4 8.5 %scale.1 = f32[48,3,128,128]{3,2,1,0:T(8,128)} custom-call(f32[1,384]{1,0:T(1,128)S(1)} %add_multiply_fusion.mean_ref, f32[30,128,384]{2,1,0:T(8,128)} %copy-done.4, f32[12,128,384]{2,1,0:T(8,128)S(1)} %copy-done.7, f32[6,128,384]{2,1,0:T(8,128)S(1)} %copy-done.9), custom_call_target="tpu_custom_call" | custom-call | tf_op jit(solution)/shard_map/scale/pallas_call | solution.py:246
  (161 shorter events, 63.8 us)
Async XLA Ops:
  8.4 207.3 %collective-permute-start.15 = (bf16[48,128,384]{2,1,0:T(8,128)(2,1)}, bf16[48,128,384]{2,1,0:T(8,128)(2,1)}, u32[]{:S(2)}, u32[]{:S(2)}) collective-permute-start(bf16[48,128,384]{2,1,0:T(8,128)(2,1)} %panel.1.refs_20_.refs_8_.refs_4_), channel_id=1, source_target_pairs={{0,8},{1,9},{2,10},{3,11},{4,12},{5,13},{6,14},{7,15},{8,0},{9,1},... | collective-permute-start | bytes 14155784 | tf_op jit(solution)/shard_map/ppermute | solution.py:19
  14.8 325.5 %copy-start.33 = (bf16[6,4,128,128]{3,2,1,0:T(8,128)(2,1)}, bf16[6,4,128,128]{3,2,1,0:T(8,128)(2,1)S(1)}, u32[]{:S(2)}) copy-start(bf16[6,4,128,128]{3,2,1,0:T(8,128)(2,1)S(1)} %get-tuple-element.40.refs_8_) | copy-start | bytes 2359300
  14.8 201.6 %collective-permute-start.1 = (bf16[6,4,128,128]{3,2,1,0:T(8,128)(2,1)S(1)}, bf16[6,4,128,128]{3,2,1,0:T(8,128)(2,1)S(1)}, u32[]{:S(2)}, u32[]{:S(2)}) collective-permute-start(bf16[6,4,128,128]{3,2,1,0:T(8,128)(2,1)S(1)} %get-tuple-element.71.refs_0_), channel_id=1, source_target_pairs={{0,4},{1,5},{2,6},{3,7},{4,0},{5,1},{6,2},{7,3},{8,12},{9,13},{10,... | collective-permute-start | bytes 2359304 | tf_op jit(solution)/shard_map/ppermute | solution.py:19
  16.4 200.0 %collective-permute-start = (bf16[6,4,128,128]{3,2,1,0:T(8,128)(2,1)S(1)}, bf16[6,4,128,128]{3,2,1,0:T(8,128)(2,1)S(1)}, u32[]{:S(2)}, u32[]{:S(2)}) collective-permute-start(bf16[6,4,128,128]{3,2,1,0:T(8,128)(2,1)S(1)} %get-tuple-element.71.refs_0_), channel_id=1, source_target_pairs={{0,2},{1,3},{2,0},{3,1},{4,6},{5,7},{6,4},{7,5},{8,10},{9,11},{10,... | collective-permute-start | bytes 2359304 | tf_op jit(solution)/shard_map/ppermute | solution.py:19
  17.9 337.8 %collective-permute-start.16 = (bf16[48,128,384]{2,1,0:T(8,128)(2,1)}, bf16[48,128,384]{2,1,0:T(8,128)(2,1)}, u32[]{:S(2)}, u32[]{:S(2)}) collective-permute-start(bf16[48,128,384]{2,1,0:T(8,128)(2,1)} %panel.1.refs_20_.refs_8_.refs_4_), channel_id=1, source_target_pairs={{0,1},{1,0},{2,3},{3,2},{4,5},{5,4},{6,7},{7,6},{8,9},{9,8},{10,11... | collective-permute-start | bytes 14155784 | tf_op jit(solution)/shard_map/ppermute | solution.py:19
  215.7 156.2 %collective-permute-start.17 = (bf16[48,128,384]{2,1,0:T(8,128)(2,1)}, bf16[48,128,384]{2,1,0:T(8,128)(2,1)}, u32[]{:S(2)}, u32[]{:S(2)}) collective-permute-start(bf16[48,128,384]{2,1,0:T(8,128)(2,1)} %collective-permute-done.15.refs_21_.refs_9_.refs_5_), channel_id=1, source_target_pairs={{0,1},{1,0},{2,3},{3,2},{4,5},{5,4},{6,7},{7,6},{8,9},{9,8},{10,11... | collective-permute-start | bytes 14155784 | tf_op jit(solution)/shard_map/ppermute | solution.py:19
  215.7 20.0 %collective-permute-start.4 = (bf16[6,4,128,128]{3,2,1,0:T(8,128)(2,1)S(1)}, bf16[6,4,128,128]{3,2,1,0:T(8,128)(2,1)S(1)}, u32[]{:S(2)}, u32[]{:S(2)}) collective-permute-start(bf16[6,4,128,128]{3,2,1,0:T(8,128)(2,1)S(1)} %get-tuple-element.76.refs_4_), channel_id=1, source_target_pairs={{0,4},{1,5},{2,6},{3,7},{4,0},{5,1},{6,2},{7,3},{8,12},{9,13},{10,... | collective-permute-start | bytes 2359304 | tf_op jit(solution)/shard_map/ppermute | solution.py:19
  217.3 20.4 %collective-permute-start.2 = (bf16[6,4,128,128]{3,2,1,0:T(8,128)(2,1)S(1)}, bf16[6,4,128,128]{3,2,1,0:T(8,128)(2,1)S(1)}, u32[]{:S(2)}, u32[]{:S(2)}) collective-permute-start(bf16[6,4,128,128]{3,2,1,0:T(8,128)(2,1)S(1)} %collective-permute-done.1.refs_2_), channel_id=1, source_target_pairs={{0,2},{1,3},{2,0},{3,1},{4,6},{5,7},{6,4},{7,5},{8,10},{9,11},{10,... | collective-permute-start | bytes 2359304 | tf_op jit(solution)/shard_map/ppermute | solution.py:19
  219.7 34.9 %collective-permute-start.3 = (bf16[6,4,128,128]{3,2,1,0:T(8,128)(2,1)S(1)}, bf16[6,4,128,128]{3,2,1,0:T(8,128)(2,1)S(1)}, u32[]{:S(2)}, u32[]{:S(2)}) collective-permute-start(bf16[6,4,128,128]{3,2,1,0:T(8,128)(2,1)S(1)} %get-tuple-element.76.refs_4_), channel_id=1, source_target_pairs={{0,2},{1,3},{2,0},{3,1},{4,6},{5,7},{6,4},{7,5},{8,10},{9,11},{10,... | collective-permute-start | bytes 2359304 | tf_op jit(solution)/shard_map/ppermute | solution.py:19
  235.6 21.3 %collective-permute-start.7 = (bf16[6,4,128,128]{3,2,1,0:T(8,128)(2,1)S(1)}, bf16[6,4,128,128]{3,2,1,0:T(8,128)(2,1)S(1)}, u32[]{:S(2)}, u32[]{:S(2)}) collective-permute-start(bf16[6,4,128,128]{3,2,1,0:T(8,128)(2,1)S(1)} %get-tuple-element.40.refs_8_), channel_id=1, source_target_pairs={{0,4},{1,5},{2,6},{3,7},{4,0},{5,1},{6,2},{7,3},{8,12},{9,13},{10,... | collective-permute-start | bytes 2359304 | tf_op jit(solution)/shard_map/ppermute | solution.py:19
  238.6 32.8 %collective-permute-start.5 = (bf16[6,4,128,128]{3,2,1,0:T(8,128)(2,1)S(1)}, bf16[6,4,128,128]{3,2,1,0:T(8,128)(2,1)S(1)}, u32[]{:S(2)}, u32[]{:S(2)}) collective-permute-start(bf16[6,4,128,128]{3,2,1,0:T(8,128)(2,1)S(1)} %collective-permute-done.4.refs_6_), channel_id=1, source_target_pairs={{0,2},{1,3},{2,0},{3,1},{4,6},{5,7},{6,4},{7,5},{8,10},{9,11},{10,... | collective-permute-start | bytes 2359304 | tf_op jit(solution)/shard_map/ppermute | solution.py:19
  255.4 32.8 %collective-permute-start.6 = (bf16[6,4,128,128]{3,2,1,0:T(8,128)(2,1)S(1)}, bf16[6,4,128,128]{3,2,1,0:T(8,128)(2,1)S(1)}, u32[]{:S(2)}, u32[]{:S(2)}) collective-permute-start(bf16[6,4,128,128]{3,2,1,0:T(8,128)(2,1)S(1)} %get-tuple-element.40.refs_8_), channel_id=1, source_target_pairs={{0,2},{1,3},{2,0},{3,1},{4,6},{5,7},{6,4},{7,5},{8,10},{9,11},{10,... | collective-permute-start | bytes 2359304 | tf_op jit(solution)/shard_map/ppermute | solution.py:19
  256.9 32.8 %collective-permute-start.10 = (bf16[6,4,128,128]{3,2,1,0:T(8,128)(2,1)S(1)}, bf16[6,4,128,128]{3,2,1,0:T(8,128)(2,1)S(1)}, u32[]{:S(2)}, u32[]{:S(2)}) collective-permute-start(bf16[6,4,128,128]{3,2,1,0:T(8,128)(2,1)S(1)} %get-tuple-element.43.refs_12_), channel_id=1, source_target_pairs={{0,4},{1,5},{2,6},{3,7},{4,0},{5,1},{6,2},{7,3},{8,12},{9,13},{10,... | collective-permute-start | bytes 2359304 | tf_op jit(solution)/shard_map/ppermute | solution.py:19
  271.4 33.7 %collective-permute-start.8 = (bf16[6,4,128,128]{3,2,1,0:T(8,128)(2,1)S(1)}, bf16[6,4,128,128]{3,2,1,0:T(8,128)(2,1)S(1)}, u32[]{:S(2)}, u32[]{:S(2)}) collective-permute-start(bf16[6,4,128,128]{3,2,1,0:T(8,128)(2,1)S(1)} %collective-permute-done.7.refs_10_), channel_id=1, source_target_pairs={{0,2},{1,3},{2,0},{3,1},{4,6},{5,7},{6,4},{7,5},{8,10},{9,11},{10,... | collective-permute-start | bytes 2359304 | tf_op jit(solution)/shard_map/ppermute | solution.py:19
  288.2 33.7 %collective-permute-start.9 = (bf16[6,4,128,128]{3,2,1,0:T(8,128)(2,1)S(1)}, bf16[6,4,128,128]{3,2,1,0:T(8,128)(2,1)S(1)}, u32[]{:S(2)}, u32[]{:S(2)}) collective-permute-start(bf16[6,4,128,128]{3,2,1,0:T(8,128)(2,1)S(1)} %get-tuple-element.43.refs_12_), channel_id=1, source_target_pairs={{0,2},{1,3},{2,0},{3,1},{4,6},{5,7},{6,4},{7,5},{8,10},{9,11},{10,... | collective-permute-start | bytes 2359304 | tf_op jit(solution)/shard_map/ppermute | solution.py:19
  289.7 33.7 %collective-permute-start.13 = (bf16[6,4,128,128]{3,2,1,0:T(8,128)(2,1)}, bf16[6,4,128,128]{3,2,1,0:T(8,128)(2,1)}, u32[]{:S(2)}, u32[]{:S(2)}) collective-permute-start(bf16[6,4,128,128]{3,2,1,0:T(8,128)(2,1)} %get-tuple-element.46.refs_16_), channel_id=1, source_target_pairs={{0,4},{1,5},{2,6},{3,7},{4,0},{5,1},{6,2},{7,3},{8,12},{9,13},{10,... | collective-permute-start | bytes 2359304 | tf_op jit(solution)/shard_map/ppermute | solution.py:19
  305.1 33.7 %collective-permute-start.11 = (bf16[6,4,128,128]{3,2,1,0:T(8,128)(2,1)S(1)}, bf16[6,4,128,128]{3,2,1,0:T(8,128)(2,1)S(1)}, u32[]{:S(2)}, u32[]{:S(2)}) collective-permute-start(bf16[6,4,128,128]{3,2,1,0:T(8,128)(2,1)S(1)} %collective-permute-done.10.refs_14_), channel_id=1, source_target_pairs={{0,2},{1,3},{2,0},{3,1},{4,6},{5,7},{6,4},{7,5},{8,10},{9,11},{10,... | collective-permute-start | bytes 2359304 | tf_op jit(solution)/shard_map/ppermute | solution.py:19
  321.9 33.8 %collective-permute-start.12 = (bf16[6,4,128,128]{3,2,1,0:T(8,128)(2,1)}, bf16[6,4,128,128]{3,2,1,0:T(8,128)(2,1)}, u32[]{:S(2)}, u32[]{:S(2)}) collective-permute-start(bf16[6,4,128,128]{3,2,1,0:T(8,128)(2,1)} %get-tuple-element.46.refs_16_), channel_id=1, source_target_pairs={{0,2},{1,3},{2,0},{3,1},{4,6},{5,7},{6,4},{7,5},{8,10},{9,11},{10,... | collective-permute-start | bytes 2359304 | tf_op jit(solution)/shard_map/ppermute | solution.py:19
  338.8 33.1 %collective-permute-start.14 = (bf16[6,4,128,128]{3,2,1,0:T(8,128)(2,1)}, bf16[6,4,128,128]{3,2,1,0:T(8,128)(2,1)}, u32[]{:S(2)}, u32[]{:S(2)}) collective-permute-start(bf16[6,4,128,128]{3,2,1,0:T(8,128)(2,1)} %collective-permute-done.13.refs_18_), channel_id=1, source_target_pairs={{0,2},{1,3},{2,0},{3,1},{4,6},{5,7},{6,4},{7,5},{8,10},{9,11},{10,... | collective-permute-start | bytes 2359304 | tf_op jit(solution)/shard_map/ppermute | solution.py:19
  403.7 132.9 %collective-permute-start.18 = (f32[30,128,384]{2,1,0:T(8,128)}, f32[30,128,384]{2,1,0:T(8,128)}, u32[]{:S(2)}, u32[]{:S(2)}) collective-permute-start(f32[30,128,384]{2,1,0:T(8,128)} %get-tuple-element.49), channel_id=1, source_target_pairs={{0,1},{1,0},{2,3},{3,2},{4,5},{5,4},{6,7},{7,6},{8,9},{9,8},{10,11... | collective-permute-start | bytes 17694728 | tf_op jit(solution)/shard_map/ppermute | solution.py:19
  403.8 20.0 %collective-permute-start.19 = (bf16[6,4,128,128]{3,2,1,0:T(8,128)(2,1)S(1)}, bf16[6,4,128,128]{3,2,1,0:T(8,128)(2,1)S(1)}, u32[]{:S(2)}, u32[]{:S(2)}) collective-permute-start(bf16[6,4,128,128]{3,2,1,0:T(8,128)(2,1)S(1)} %get-tuple-element.52.refs_0_), channel_id=1, source_target_pairs={{0,2},{1,3},{2,0},{3,1},{4,6},{5,7},{6,4},{7,5},{8,10},{9,11},{10,... | collective-permute-start | bytes 2359304 | tf_op jit(solution)/shard_map/ppermute | solution.py:19
  405.3 22.2 %collective-permute-start.20 = (bf16[6,4,128,128]{3,2,1,0:T(8,128)(2,1)S(1)}, bf16[6,4,128,128]{3,2,1,0:T(8,128)(2,1)S(1)}, u32[]{:S(2)}, u32[]{:S(2)}) collective-permute-start(bf16[6,4,128,128]{3,2,1,0:T(8,128)(2,1)S(1)} %get-tuple-element.52.refs_0_), channel_id=1, source_target_pairs={{0,4},{1,5},{2,6},{3,7},{4,0},{5,1},{6,2},{7,3},{8,12},{9,13},{10,... | collective-permute-start | bytes 2359304 | tf_op jit(solution)/shard_map/ppermute | solution.py:19
  424.6 20.5 %collective-permute-start.22 = (bf16[6,4,128,128]{3,2,1,0:T(8,128)(2,1)S(1)}, bf16[6,4,128,128]{3,2,1,0:T(8,128)(2,1)S(1)}, u32[]{:S(2)}, u32[]{:S(2)}) collective-permute-start(bf16[6,4,128,128]{3,2,1,0:T(8,128)(2,1)S(1)} %get-tuple-element.55.refs_4_), channel_id=1, source_target_pairs={{0,2},{1,3},{2,0},{3,1},{4,6},{5,7},{6,4},{7,5},{8,10},{9,11},{10,... | collective-permute-start | bytes 2359304 | tf_op jit(solution)/shard_map/ppermute | solution.py:19
  426.1 21.4 %collective-permute-start.23 = (bf16[6,4,128,128]{3,2,1,0:T(8,128)(2,1)S(1)}, bf16[6,4,128,128]{3,2,1,0:T(8,128)(2,1)}, u32[]{:S(2)}, u32[]{:S(2)}) collective-permute-start(bf16[6,4,128,128]{3,2,1,0:T(8,128)(2,1)S(1)} %get-tuple-element.55.refs_4_), channel_id=1, source_target_pairs={{0,4},{1,5},{2,6},{3,7},{4,0},{5,1},{6,2},{7,3},{8,12},{9,13},{10,... | collective-permute-start | bytes 2359304 | tf_op jit(solution)/shard_map/ppermute | solution.py:19
  427.5 34.4 %collective-permute-start.21 = (bf16[6,4,128,128]{3,2,1,0:T(8,128)(2,1)S(1)}, bf16[6,4,128,128]{3,2,1,0:T(8,128)(2,1)S(1)}, u32[]{:S(2)}, u32[]{:S(2)}) collective-permute-start(bf16[6,4,128,128]{3,2,1,0:T(8,128)(2,1)S(1)} %collective-permute-done.20.refs_2_), channel_id=1, source_target_pairs={{0,2},{1,3},{2,0},{3,1},{4,6},{5,7},{6,4},{7,5},{8,10},{9,11},{10,... | collective-permute-start | bytes 2359304 | tf_op jit(solution)/shard_map/ppermute | solution.py:19
  446.0 32.9 %collective-permute-start.26 = (bf16[6,4,128,128]{3,2,1,0:T(8,128)(2,1)S(1)}, bf16[6,4,128,128]{3,2,1,0:T(8,128)(2,1)}, u32[]{:S(2)}, u32[]{:S(2)}) collective-permute-start(bf16[6,4,128,128]{3,2,1,0:T(8,128)(2,1)S(1)} %get-tuple-element.61.refs_0_), channel_id=1, source_target_pairs={{0,2},{1,3},{2,0},{3,1},{4,6},{5,7},{6,4},{7,5},{8,10},{9,11},{10,... | collective-permute-start | bytes 2359304 | tf_op jit(solution)/shard_map/ppermute | solution.py:19
  462.8 31.5 %collective-permute-start.24 = (bf16[6,4,128,128]{3,2,1,0:T(8,128)(2,1)}, bf16[6,4,128,128]{3,2,1,0:T(8,128)(2,1)S(1)}, u32[]{:S(2)}, u32[]{:S(2)}) collective-permute-start(bf16[6,4,128,128]{3,2,1,0:T(8,128)(2,1)} %collective-permute-done.23.refs_6_), channel_id=1, source_target_pairs={{0,2},{1,3},{2,0},{3,1},{4,6},{5,7},{6,4},{7,5},{8,10},{9,11},{10,... | collective-permute-start | bytes 2359304 | tf_op jit(solution)/shard_map/ppermute | solution.py:19
  464.6 48.6 %collective-permute-start.27 = (bf16[6,4,128,128]{3,2,1,0:T(8,128)(2,1)S(1)}, bf16[6,4,128,128]{3,2,1,0:T(8,128)(2,1)}, u32[]{:S(2)}, u32[]{:S(2)}) collective-permute-start(bf16[6,4,128,128]{3,2,1,0:T(8,128)(2,1)S(1)} %get-tuple-element.61.refs_0_), channel_id=1, source_target_pairs={{0,4},{1,5},{2,6},{3,7},{4,0},{5,1},{6,2},{7,3},{8,12},{9,13},{10,... | collective-permute-start | bytes 2359304 | tf_op jit(solution)/shard_map/ppermute | solution.py:19
  478.9 34.4 %collective-permute-start.28 = (bf16[6,4,128,128]{3,2,1,0:T(8,128)(2,1)}, bf16[6,4,128,128]{3,2,1,0:T(8,128)(2,1)}, u32[]{:S(2)}, u32[]{:S(2)}) collective-permute-start(bf16[6,4,128,128]{3,2,1,0:T(8,128)(2,1)} %collective-permute-done.26.refs_1_), channel_id=1, source_target_pairs={{0,4},{1,5},{2,6},{3,7},{4,0},{5,1},{6,2},{7,3},{8,12},{9,13},{10,... | collective-permute-start | bytes 2359304 | tf_op jit(solution)/shard_map/ppermute | solution.py:19
  512.9 19.4 %collective-permute-start.25 = (f32[12,128,384]{2,1,0:T(8,128)}, f32[12,128,384]{2,1,0:T(8,128)}, u32[]{:S(2)}, u32[]{:S(2)}) collective-permute-start(f32[12,128,384]{2,1,0:T(8,128)} %get-tuple-element.58), channel_id=1, source_target_pairs={{0,1},{1,0},{2,3},{3,2},{4,5},{5,4},{6,7},{7,6},{8,9},{9,8},{10,11... | collective-permute-start | bytes 7077896 | tf_op jit(solution)/shard_map/ppermute | solution.py:19
  523.9 3.3 collective-permute-start.29
  548.5 4.9 collective-permute-start.30
  (42 other events, 737.3 us)

commit v2 on v1

v2 whole, which is shorter than its diff:
```python
import functools
import math

import jax
import jax.numpy as jnp
from jax import lax
from jax.experimental import pallas as pl
from jax.experimental.pallas import tpu as pltpu
from jax.sharding import PartitionSpec as P

GC = 8
CB = 12
PC = CB // 4
STRIPS = GC // 2
MIB = 1 << 20


def swapped(array, mask):
    return lax.ppermute(array, "grid", [(i, i ^ mask) for i in range(lax.axis_size("grid"))])


def panel_kernel(slot_ref, tiles_ref, panel_ref):
    rows, _, width, _ = tiles_ref.shape
    first = pl.program_id(0) * rows

    @pl.loop(0, rows)
    def _(r):
        for p in range(PC):
            slot = slot_ref[(first + r) * PC + p]
            tile = tiles_ref[r, jnp.maximum(slot, 0)]
            panel_ref[r, :, p * width : (p + 1) * width] = jnp.where(
                slot >= 0, tile, jnp.zeros_like(tile)
            )


def make_panel(tile_values, slots):
    block_rows, slots_per_row, width, _ = tile_values.shape
    step = math.gcd(block_rows, 12)
    return pl.pallas_call(
        panel_kernel,
        grid_spec=pltpu.PrefetchScalarGridSpec(
            num_scalar_prefetch=1,
            grid=(block_rows // step,),
            in_specs=[pl.BlockSpec((step, slots_per_row, width, width), lambda i, s: (i, 0, 0, 0))],
            out_specs=pl.BlockSpec((step, width, PC * width), lambda i, s: (i, 0, 0)),
        ),
        out_shape=jax.ShapeDtypeStruct((block_rows, width, PC * width), jnp.bfloat16),
        compiler_params=pltpu.CompilerParams(vmem_limit_bytes=40 * MIB),
        cost_estimate=pl.CostEstimate(flops=0, bytes_accessed=11_000_000, transcendentals=0),
        name="panel",
    )(slots.reshape(-1), tile_values)


def pack_kernel(first, parts, where_ref, *refs):
    sources, packed_ref, sem = refs[: 2 * parts], refs[-2], refs[-1]
    part_rows, _, half = sources[0].shape
    unit = math.gcd(CB, part_rows)
    for n in range(packed_ref.shape[0] // unit):
        part = where_ref[2 * (first + n)]
        offset = where_ref[2 * (first + n) + 1]
        for m in range(parts):

            @pl.when((part == m) | (parts == 1))
            def _():
                for side in range(2):
                    pltpu.make_async_copy(
                        sources[side * parts + m].at[pl.ds(offset, unit)],
                        packed_ref.at[pl.ds(n * unit, unit), :, pl.ds(side * half, half)],
                        sem.at[side],
                    ).start()
    for side in range(2):
        cols = pl.ds(side * half, half)
        pltpu.make_async_copy(
            packed_ref.at[:, :, cols], packed_ref.at[:, :, cols], sem.at[side]
        ).wait()


def pack(where, first, mine, others):
    parts = len(mine)
    _, width, half = mine[0].shape
    return pl.pallas_call(
        functools.partial(pack_kernel, first, parts),
        out_shape=jax.ShapeDtypeStruct((STRIPS // 2 * CB, width, 2 * half), jnp.bfloat16),
        in_specs=[pl.BlockSpec(memory_space=pltpu.SMEM)]
        + [pl.BlockSpec(memory_space=pl.ANY)] * (2 * parts),
        out_specs=pl.BlockSpec(memory_space=pltpu.VMEM),
        scratch_shapes=[pltpu.SemaphoreType.DMA((2,))],
        compiler_params=pltpu.CompilerParams(vmem_limit_bytes=16 * MIB),
        cost_estimate=pl.CostEstimate(flops=0, bytes_accessed=8_000_000, transcendentals=0),
        name="pack",
    )(where, *mine, *others)


def expand_kernel(chunks, order_ref, index_ref, near_ref, far_ref, *refs):
    chunk_refs = refs[: chunks * STRIPS]
    mine_ref, other_ref, tiles, sums, tile_sem, sum_sem = refs[chunks * STRIPS :]
    rows, slots, width, _ = chunk_refs[0].shape
    half = PC * width

    def fetch(k):
        return [
            pltpu.make_async_copy(
                chunk_refs[k * STRIPS + q], tiles.at[k % 2, q], tile_sem.at[k % 2, q]
            )
            for q in range(STRIPS)
        ]

    for copy in fetch(0):
        copy.start()

    def stores(row, slot):
        return [
            pltpu.make_async_copy(
                sums.at[slot, :, pl.ds(side * half, half)], out.at[row], sum_sem.at[slot, side]
            )
            for side, out in enumerate((mine_ref, other_ref))
        ]

    for k in range(chunks):
        if k + 1 < chunks:
            for copy in fetch(k + 1):
                copy.start()
        for copy in fetch(k):
            copy.wait()

        @pl.loop(0, rows)
        def _(r):
            row = k * rows + r
            slot = lax.rem(row, 2)

            @pl.when(row >= 2)
            def _():
                for copy in stores(row - 2, slot):
                    copy.wait()

            total = None
            for n in range(STRIPS):
                panel = near_ref if n < STRIPS // 2 else far_ref
                q = order_ref[n]
                for t in range(0, slots, 2):
                    base = row * (STRIPS * slots) + n * slots + t
                    left = jnp.concatenate(
                        [tiles[k % 2, q, r, t], tiles[k % 2, q, r, t + 1]], axis=1
                    )
                    right = jnp.concatenate(
                        [panel[index_ref[base]], panel[index_ref[base + 1]]], axis=0
                    )
                    term = jnp.dot(left, right, preferred_element_type=jnp.float32)
                    total = term if total is None else total + term
            sums[slot] = total
            for copy in stores(row, slot):
                copy.start()

    for row in range(max(chunks * rows - 2, 0), chunks * rows):
        for copy in stores(row, row % 2):
            copy.wait()


def expand(chunk_list, order, index, near, far):
    chunks = len(chunk_list)
    rows, slots, width, _ = chunk_list[0][0].shape
    total_rows = chunks * rows
    half = jax.ShapeDtypeStruct((total_rows, width, PC * width), jnp.float32)
    anywhere = pl.BlockSpec(memory_space=pltpu.HBM)
    smem = pl.BlockSpec(memory_space=pltpu.SMEM)
    vmem = pl.BlockSpec(memory_space=pltpu.VMEM)
    operands = [a for chunk in chunk_list for a in chunk]
    return pl.pallas_call(
        functools.partial(expand_kernel, chunks),
        out_shape=(half, half),
        in_specs=[smem, smem, vmem, vmem] + [anywhere] * len(operands),
        out_specs=(anywhere, anywhere),
        scratch_shapes=[
            pltpu.VMEM((2, STRIPS, rows, slots, width, width), jnp.bfloat16),
            pltpu.VMEM((2, width, 2 * PC * width), jnp.float32),
            pltpu.SemaphoreType.DMA((2, STRIPS)),
            pltpu.SemaphoreType.DMA((2, 2)),
        ],
        compiler_params=pltpu.CompilerParams(vmem_limit_bytes=24 * MIB),
        cost_estimate=pl.CostEstimate(
            flops=2 * total_rows * STRIPS * slots * width * width * 2 * PC * width * 2,
            bytes_accessed=30_000_000,
            transcendentals=0,
        ),
        name="expand",
    )(order, index.reshape(-1), near, far, *operands)


def square_kernel(keep_ref, before_ref, mine_ref, got_ref, squared_ref, sums_ref):
    rows, width, _ = mine_ref.shape
    first = pl.program_id(0) * rows

    @pl.when(pl.program_id(0) == 0)
    def _():
        sums_ref[...] = before_ref[...]

    @pl.loop(0, rows)
    def _(r):
        for p in range(PC):
            keep = keep_ref[(first + r) * PC + p].astype(jnp.float32)
            cols = slice(p * width, (p + 1) * width)
            value = mine_ref[r, :, cols] + got_ref[r, :, cols]
            value = value * value * keep
            squared_ref[r, :, cols] = value
            sums_ref[:, cols] += jnp.sum(value.reshape(width // 8, 8, width), axis=0)


def square(keep, before, mine, got):
    rows, width, half = mine.shape
    step = math.gcd(rows, 6)
    block = pl.BlockSpec((step, width, half), lambda i, s: (i, 0, 0))
    sums = pl.BlockSpec((8, half), lambda i, s: (0, 0))
    return pl.pallas_call(
        square_kernel,
        grid_spec=pltpu.PrefetchScalarGridSpec(
            num_scalar_prefetch=1,
            grid=(rows // step,),
            in_specs=[sums, block, block],
            out_specs=(block, sums),
        ),
        out_shape=(
            jax.ShapeDtypeStruct(mine.shape, jnp.float32),
            jax.ShapeDtypeStruct((8, half), jnp.float32),
        ),
        compiler_params=pltpu.CompilerParams(vmem_limit_bytes=24 * MIB),
        cost_estimate=pl.CostEstimate(
            flops=0, bytes_accessed=3 * mine.size * 4, transcendentals=0
        ),
        name="square",
    )(keep.reshape(-1), before, mine, got)


def scale_kernel(bounds, count, sums_ref, got_ref, *refs):
    pieces, out_ref = refs[:-1], refs[-1]
    step, width, _ = pieces[0].shape
    at = pl.program_id(0) * step
    for n, piece in enumerate(pieces):

        @pl.when((at >= bounds[n]) & (at < bounds[n + 1]))
        def _():
            for p in range(PC):
                cols = slice(p * width, (p + 1) * width)
                sums = jnp.sum(sums_ref[:, cols] + got_ref[:, cols], axis=0, keepdims=True)
                inverse = 1.0 / (sums / count + 1e-6)
                for r in range(step):
                    out_ref[r, p] = piece[r, :, cols] * inverse


def scale(count, sums, got, pieces):
    _, width, half = pieces[0].shape
    step = functools.reduce(math.gcd, [p.shape[0] for p in pieces])
    bounds = [0]
    for p in pieces:
        bounds.append(bounds[-1] + p.shape[0])

    def block_of(n):
        low, number = bounds[n] // step, pieces[n].shape[0] // step
        return pl.BlockSpec(
            (step, width, half), lambda i: (jnp.clip(i - low, 0, number - 1), 0, 0)
        )

    return pl.pallas_call(
        functools.partial(scale_kernel, tuple(bounds), count),
        grid=(bounds[-1] // step,),
        in_specs=[pl.BlockSpec((8, half), lambda i: (0, 0))] * 2
        + [block_of(n) for n in range(len(pieces))],
        out_specs=pl.BlockSpec((step, PC, width, width), lambda i: (i, 0, 0, 0)),
        out_shape=jax.ShapeDtypeStruct((bounds[-1], PC, width, width), jnp.float32),
        compiler_params=pltpu.CompilerParams(vmem_limit_bytes=40 * MIB),
        name="scale",
    )(sums, got, *pieces)


def after(array, *earlier):
    return lax.optimization_barrier((array, *earlier))[0]


class Lane:
    def __init__(self, window):
        self.window = window
        self.sent = []

    def send(self, array, mask):
        if len(self.sent) >= self.window:
            array = after(array, self.sent[-self.window])
        out = swapped(array, mask)
        self.sent.append(out)
        return out


def shards(tile_values, tile_columns, keep_tiles):
    devices = lax.axis_size("grid")
    device = lax.axis_index("grid")
    all_bits = devices.bit_length() - 1
    low_bits = GC.bit_length() - 1
    grid_rows = devices // GC
    row_strip = device // GC
    col_strip = device % GC
    block_rows, slots, width, _ = tile_values.shape
    chunks = math.gcd(block_rows, 8)
    rows = block_rows // chunks
    pair = STRIPS // 2

    strip_rows = lax.dynamic_slice_in_dim(tile_columns, row_strip * block_rows, block_rows, 0)
    far_first = 0
    if block_rows == pair * 2 * CB:
        far_first = pair * (col_strip // (pair * 2) != row_strip).astype(jnp.int32)
    order = jnp.bitwise_xor(jnp.arange(STRIPS, dtype=jnp.int32), far_first)
    strips = jnp.bitwise_xor(col_strip, 2 * order)
    own = jnp.take(strip_rows, col_strip, axis=1)
    match = own[:, :, None] == jnp.arange(PC, dtype=jnp.int32)
    slot = jnp.max(
        jnp.where(match, jnp.arange(slots, dtype=jnp.int32)[None, :, None], -1), axis=1
    )
    index = jnp.take(strip_rows, strips, axis=1)
    index = index + CB * (jnp.arange(STRIPS, dtype=jnp.int32) % pair)[None, :, None]
    index = index.reshape(block_rows, STRIPS * slots)
    unit = math.gcd(CB, block_rows)
    unit_rows = strips[:, None] * CB + unit * jnp.arange(CB // unit, dtype=jnp.int32)
    where = jnp.stack(
        [jnp.bitwise_xor(unit_rows // block_rows, row_strip), unit_rows % block_rows], axis=-1
    ).reshape(-1)

    own_chunks = [lax.slice_in_dim(tile_values, k * rows, (k + 1) * rows) for k in range(chunks)]
    x_lane, z_lane = Lane(2), Lane(1)
    from_x, from_z, from_xz = [], [], []
    for k in range(chunks):
        from_x.append(x_lane.send(own_chunks[k], 2))
        from_z.append(z_lane.send(own_chunks[k], 4))
        if k > 1:
            from_xz.append(x_lane.send(from_z[k - 2], 2))
    from_xz.append(x_lane.send(from_z[chunks - 2], 2))
    from_xz.append(z_lane.send(from_x[chunks - 1], 4))

    panels = [make_panel(tile_values, slot)]
    for bit in range(low_bits, all_bits):
        panels = panels + [swapped(p, 1 << bit) for p in panels]
    half = len(where) // 2
    if block_rows == pair * 2 * CB and grid_rows == 2:
        near_other = swapped(panels[0], 1)
        near = pack(where, 0, panels[:1], [near_other])
        far_mine = after(panels[1], from_x[-1], from_z[-1], from_xz[-4])
        far = pack(where, half // 2, [far_mine], [swapped(far_mine, 1)])
    else:
        others = [swapped(p, 1) for p in panels]
        near = pack(where, 0, panels, others)
        far = pack(where, half // 2, panels, others)

    squares = []
    sums = jnp.zeros((8, PC * width), jnp.float32)
    first = 0
    for count in (chunks - 2, 2) if chunks > 3 else (chunks,):
        ks = range(first, first + count)
        lo, hi = first * rows, (first + count) * rows
        mine, other = expand(
            [(own_chunks[k], from_x[k], from_z[k], from_xz[k]) for k in ks],
            order,
            index[lo:hi],
            near,
            far,
        )
        squared, sums = square(keep_tiles[lo:hi], sums, mine, swapped(other, 1))
        squares.append(squared)
        first += count
    for bit in range(low_bits, all_bits - 1):
        sums = sums + swapped(sums, 1 << bit)
    got = swapped(sums, 1 << (all_bits - 1))
    return scale(float(CB * GC * width), sums, got, squares)


def solution(mesh):
    return jax.shard_map(
        shards,
        mesh=mesh,
        in_specs=(
            P(("groups", "grid"), None, None, None),
            P("groups", None, None),
            P(("groups", "grid"), None),
        ),
        out_specs=P(("groups", "grid"), None, None, None),
        check_vma=False,
    )
```

time: 563 us -> 459 us (0.82)
  waiting for transfers between devices: 410 us -> 322 us
  Pallas kernels: 70 us -> 59.4 us
    ppermute x31 -> x30, waiting for transfers between devices: 410 us -> 322 us  [swapped(): lax.ppermute(array, 'grid', [(i, i ^ mask) for i in range(lax.axis_size('...]
    pallas_call x4 -> x5, Pallas kernels: 56.2 us -> 47.5 us  [the longest x2 37 us: expand(): pl.pallas_call(functools.partial(expand_kernel, chunks), out_shape=(half,...]
    unnamed x86 -> x98, local copies, waits for them, and re-layouts: 34.5 us -> 29.8 us
    ppermute x31 -> x30, starting transfers between devices: 39.7 us -> 37.9 us  [swapped(): lax.ppermute(array, 'grid', [(i, i ^ mask) for i in range(lax.axis_size('...]
  transfers between devices with their start and end apart: 31 -> 30, of which waited for: 18 -> 18; matrix products, arithmetic and copies ran while one was open for 1% -> 0% of each run, Pallas kernels for 5% -> 6%
where the time goes in v2:
time: 459 us
  waiting for transfers between devices  322 us (70%)
  Pallas kernels  59.4 us (13%)
  local copies, waits for them, and re-layouts  38.3 us (8%)
  starting transfers between devices  37.9 us (8%)
    ppermute x30, waiting for transfers between devices, swapped(): lax.ppermute(array, 'grid', [(i, i ^ mask) for i in range(lax.axis_size('...  322 us
    ppermute x30, starting transfers between devices, swapped(): lax.ppermute(array, 'grid', [(i, i ^ mask) for i in range(lax.axis_size('...  37.9 us
    pallas_call x2, Pallas kernels, expand(): pl.pallas_call(functools.partial(expand_kernel, chunks), out_shape=(half,...  37 us
    unnamed x98, local copies, waits for them, and re-layouts  29.8 us
  transfers between devices with their start and end apart: 30, of which 18 were waited for; matrix products, arithmetic and copies ran while one was open for 0% of the time, Pallas kernels for 6%

profile of v2, /device:TPU:0, one launch (start us, length us, event | category | flops | bytes accessed | tf_op | source)
XLA Modules:
  0.0 458.5 jit_solution(8113679268873082880)
XLA Ops:
  0.0 6.5 %fusion.6 = (bf16[6,4,128,128]{3,2,1,0:T(8,128)(2,1)S(1)}, bf16[6,4,128,128]{3,2,1,0:T(8,128)(2,1)S(1)}, bf16[6,4,128,128]{3,2,1,0:T(8,128)(2,1)}, bf16[6,4,128,...) fusion(bf16[48,4,128,128]{3,2,1,0:T(8,128)(2,1)} %tiles_ref.1), kind=kLoop, calls=%fused_computation.23 | loop fusion | bytes 12582912 | tf_op jit(solution)/shard_map/slice | solution.py:324
  6.5 3.0 collective-permute-start.9
  11.0 16.3 %collective-permute-done.9.refs_2_ = bf16[6,4,128,128]{3,2,1,0:T(8,128)(2,1)S(1)} collective-permute-done((bf16[6,4,128,128]{3,2,1,0:T(8,128)(2,1)}, bf16[6,4,128,128]{3,2,1,0:T(8,128)(2,1)S(1)}, u32[]{:S(2)}, u32[]{:S(2)}) %collective-permute-start.9) | collective-permute-done | bytes 786464 | tf_op jit(solution)/shard_map/ppermute | solution.py:19
  32.0 15.1 %collective-permute-done.10.refs_6_ = bf16[6,4,128,128]{3,2,1,0:T(8,128)(2,1)} collective-permute-done((bf16[6,4,128,128]{3,2,1,0:T(8,128)(2,1)S(1)}, bf16[6,4,128,128]{3,2,1,0:T(8,128)(2,1)}, u32[]{:S(2)}, u32[]{:S(2)}) %collective-permute-start.10) | collective-permute-done | bytes 786464 | tf_op jit(solution)/shard_map/ppermute | solution.py:19
  48.8 2.8 copy-done
  51.6 3.8 panel.1.refs_0_
  55.4 2.6 collective-permute-start.1
  59.5 7.9 %collective-permute-done.3.refs_9_ = bf16[6,4,128,128]{3,2,1,0:T(8,128)(2,1)} collective-permute-done((bf16[6,4,128,128]{3,2,1,0:T(8,128)(2,1)S(1)}, bf16[6,4,128,128]{3,2,1,0:T(8,128)(2,1)}, u32[]{:S(2)}, u32[]{:S(2)}) %collective-permute-start.3) | collective-permute-done | bytes 786464 | tf_op jit(solution)/shard_map/ppermute | solution.py:19
  68.8 6.0 %collective-permute-done.11.refs_10_ = bf16[6,4,128,128]{3,2,1,0:T(8,128)(2,1)} collective-permute-done((bf16[6,4,128,128]{3,2,1,0:T(8,128)(2,1)S(1)}, bf16[6,4,128,128]{3,2,1,0:T(8,128)(2,1)}, u32[]{:S(2)}, u32[]{:S(2)}) %collective-permute-start.11) | collective-permute-done | bytes 786464 | tf_op jit(solution)/shard_map/ppermute | solution.py:19
  74.8 9.3 %collective-permute-done.18.refs_3_ = bf16[6,4,128,128]{3,2,1,0:T(8,128)(2,1)S(1)} collective-permute-done((bf16[6,4,128,128]{3,2,1,0:T(8,128)(2,1)S(1)}, bf16[6,4,128,128]{3,2,1,0:T(8,128)(2,1)S(1)}, u32[]{:S(2)}, u32[]{:S(2)}) %collective-permute-start.18) | collective-permute-done | bytes 786464 | tf_op jit(solution)/shard_map/ppermute | solution.py:19
  86.5 14.5 %collective-permute-done.4.refs_13_ = bf16[6,4,128,128]{3,2,1,0:T(8,128)(2,1)S(1)} collective-permute-done((bf16[6,4,128,128]{3,2,1,0:T(8,128)(2,1)S(1)}, bf16[6,4,128,128]{3,2,1,0:T(8,128)(2,1)S(1)}, u32[]{:S(2)}, u32[]{:S(2)}) %collective-permute-start.4) | collective-permute-done | bytes 786464 | tf_op jit(solution)/shard_map/ppermute | solution.py:19
  103.3 78.5 %collective-permute-done.12.refs_14_ = bf16[6,4,128,128]{3,2,1,0:T(8,128)(2,1)S(1)} collective-permute-done((bf16[6,4,128,128]{3,2,1,0:T(8,128)(2,1)S(1)}, bf16[6,4,128,128]{3,2,1,0:T(8,128)(2,1)S(1)}, u32[]{:S(2)}, u32[]{:S(2)}) %collective-permute-start.12) | collective-permute-done | bytes 786464 | tf_op jit(solution)/shard_map/ppermute | solution.py:19
  181.8 2.5 collective-permute-start.13
  188.1 88.0 %collective-permute-done.13.refs_18_ = bf16[6,4,128,128]{3,2,1,0:T(8,128)(2,1)S(1)} collective-permute-done((bf16[6,4,128,128]{3,2,1,0:T(8,128)(2,1)S(1)}, bf16[6,4,128,128]{3,2,1,0:T(8,128)(2,1)S(1)}, u32[]{:S(2)}, u32[]{:S(2)}) %collective-permute-start.13) | collective-permute-done | bytes 786464 | tf_op jit(solution)/shard_map/ppermute | solution.py:19
  281.0 14.6 %collective-permute-done.14.refs_22_ = bf16[6,4,128,128]{3,2,1,0:T(8,128)(2,1)S(1)} collective-permute-done((bf16[6,4,128,128]{3,2,1,0:T(8,128)(2,1)S(1)}, bf16[6,4,128,128]{3,2,1,0:T(8,128)(2,1)S(1)}, u32[]{:S(2)}, u32[]{:S(2)}) %collective-permute-start.14) | collective-permute-done | bytes 786464 | tf_op jit(solution)/shard_map/ppermute | solution.py:19
  300.7 13.6 %collective-permute-done.7.refs_1_ = bf16[6,4,128,128]{3,2,1,0:T(8,128)(2,1)S(1)} collective-permute-done((bf16[6,4,128,128]{3,2,1,0:T(8,128)(2,1)S(1)}, bf16[6,4,128,128]{3,2,1,0:T(8,128)(2,1)S(1)}, u32[]{:S(2)}, u32[]{:S(2)}) %collective-permute-start.7) | collective-permute-done | bytes 786464 | tf_op jit(solution)/shard_map/ppermute | solution.py:19
  318.8 12.3 %collective-permute-done.22.refs_19_ = bf16[6,4,128,128]{3,2,1,0:T(8,128)(2,1)S(1)} collective-permute-done((bf16[6,4,128,128]{3,2,1,0:T(8,128)(2,1)S(1)}, bf16[6,4,128,128]{3,2,1,0:T(8,128)(2,1)S(1)}, u32[]{:S(2)}, u32[]{:S(2)}) %collective-permute-start.22) | collective-permute-done | bytes 786464 | tf_op jit(solution)/shard_map/ppermute | solution.py:19
  332.0 15.1 %collective-permute-done.8.refs_5_ = bf16[6,4,128,128]{3,2,1,0:T(8,128)(2,1)} collective-permute-done((bf16[6,4,128,128]{3,2,1,0:T(8,128)(2,1)S(1)}, bf16[6,4,128,128]{3,2,1,0:T(8,128)(2,1)}, u32[]{:S(2)}, u32[]{:S(2)}) %collective-permute-start.8) | collective-permute-done | bytes 786464 | tf_op jit(solution)/shard_map/ppermute | solution.py:19
  350.8 2.9 pack.2.near_ref
  353.8 2.5 collective-permute-done.23.refs_1_
  356.3 3.7 pack.3.far_ref
  360.0 8.4 %collective-permute-done.24.refs_23_ = bf16[6,4,128,128]{3,2,1,0:T(8,128)(2,1)} collective-permute-done((bf16[6,4,128,128]{3,2,1,0:T(8,128)(2,1)}, bf16[6,4,128,128]{3,2,1,0:T(8,128)(2,1)}, u32[]{:S(2)}, u32[]{:S(2)}) %collective-permute-start.24) | collective-permute-done | bytes 786464 | tf_op jit(solution)/shard_map/ppermute | solution.py:19
  368.6 26.8 %expand.2 = (f32[36,128,384]{2,1,0:T(8,128)}, f32[36,128,384]{2,1,0:T(8,128)}) custom-call(s32[4]{0:T(128)S(1)} %iota_xor_fusion.order_ref, s32[576]{0:T(1024)S(1)} %reshape.141.index_ref, bf16[24,128,768]{2,1,0:T(8,128)(2,1)S(1)} %pack.2.near_ref, bf16[24,128,768]{2,1,0:T(8,128)(2,1)S(1)} %pack.3.far_ref, ...), custom_call_target="tpu_custom_call" | custom-call | flops 28991029248 | bytes 30000000 | tf_op jit(solution)/shard_map/expand/pallas_call | solution.py:168
  399.0 16.6 %collective-permute-done.26.refs_3_ = bf16[6,4,128,128]{3,2,1,0:T(8,128)(2,1)S(1)} collective-permute-done((bf16[6,4,128,128]{3,2,1,0:T(8,128)(2,1)}, bf16[6,4,128,128]{3,2,1,0:T(8,128)(2,1)S(1)}, u32[]{:S(2)}, u32[]{:S(2)}) %collective-permute-start.26) | collective-permute-done | bytes 786464 | tf_op jit(solution)/shard_map/ppermute | solution.py:19
  417.7 2.3 copy-done.3
  420.0 2.3 copy-done.5
  428.0 10.2 %expand.3 = (f32[12,128,384]{2,1,0:T(8,128)S(1)}, f32[12,128,384]{2,1,0:T(8,128)}) custom-call(s32[4]{0:T(128)S(1)} %iota_xor_fusion.order_ref, s32[192]{0:T(256)S(1)} %reshape.144.index_ref, bf16[24,128,768]{2,1,0:T(8,128)(2,1)S(1)} %copy-done.3, bf16[24,128,768]{2,1,0:T(8,128)(2,1)S(1)} %copy-done.5, ...), custom_call_target="tpu_custom_call" | custom-call | flops 9663676416 | bytes 30000000 | tf_op jit(solution)/shard_map/expand/pallas_call | solution.py:168
  438.9 3.0 copy-done.1
  441.9 5.6 %square.2 = (f32[36,128,384]{2,1,0:T(8,128)S(1)}, f32[8,384]{1,0:T(8,128)S(1)}) custom-call(s32[108]{0:T(128)S(1)} %reshape.140.keep_ref, f32[8,384]{1,0:T(8,128)S(1)} %broadcast_in_dim.42.before_ref, f32[36,128,384]{2,1,0:T(8,128)S(1)} %copy-done.1, f32[36,128,384]{2,1,0:T(8,128)} %collective-permute-done.25.got_ref), custom_call_target="tpu_custom_call" | custom-call | bytes 21233664 | tf_op jit(solution)/shard_map/square/pallas_call | solution.py:213
  447.5 2.4 square.3
  449.9 2.8 collective-permute-start.29
  454.6 4.0 scale.1
  (161 shorter events, 52.4 us)
Async XLA Ops:
  6.5 310.2 %copy-start.6 = (bf16[6,4,128,128]{3,2,1,0:T(8,128)(2,1)}, bf16[6,4,128,128]{3,2,1,0:T(8,128)(2,1)S(1)}, u32[]{:S(2)}) copy-start(bf16[6,4,128,128]{3,2,1,0:T(8,128)(2,1)S(1)} %get-tuple-element.47.refs_4_) | copy-start | bytes 2359300
  6.5 20.8 %collective-permute-start.9 = (bf16[6,4,128,128]{3,2,1,0:T(8,128)(2,1)}, bf16[6,4,128,128]{3,2,1,0:T(8,128)(2,1)S(1)}, u32[]{:S(2)}, u32[]{:S(2)}) collective-permute-start(bf16[6,4,128,128]{3,2,1,0:T(8,128)(2,1)} %get-tuple-element.83.refs_0_), channel_id=1, source_target_pairs={{0,4},{1,5},{2,6},{3,7},{4,0},{5,1},{6,2},{7,3},{8,12},{9,13},{10,... | collective-permute-start | bytes 2359304 | tf_op jit(solution)/shard_map/ppermute | solution.py:19
  9.5 22.0 %collective-permute-start.2 = (bf16[6,4,128,128]{3,2,1,0:T(8,128)(2,1)}, bf16[6,4,128,128]{3,2,1,0:T(8,128)(2,1)}, u32[]{:S(2)}, u32[]{:S(2)}) collective-permute-start(bf16[6,4,128,128]{3,2,1,0:T(8,128)(2,1)} %get-tuple-element.83.refs_0_), channel_id=1, source_target_pairs={{0,2},{1,3},{2,0},{3,1},{4,6},{5,7},{6,4},{7,5},{8,10},{9,11},{10,... | collective-permute-start | bytes 2359304 | tf_op jit(solution)/shard_map/ppermute | solution.py:19
  28.2 18.9 %collective-permute-start.10 = (bf16[6,4,128,128]{3,2,1,0:T(8,128)(2,1)S(1)}, bf16[6,4,128,128]{3,2,1,0:T(8,128)(2,1)}, u32[]{:S(2)}, u32[]{:S(2)}) collective-permute-start(bf16[6,4,128,128]{3,2,1,0:T(8,128)(2,1)S(1)} %get-tuple-element.41.refs_4_), channel_id=1, source_target_pairs={{0,4},{1,5},{2,6},{3,7},{4,0},{5,1},{6,2},{7,3},{8,12},{9,13},{10,... | collective-permute-start | bytes 2359304 | tf_op jit(solution)/shard_map/ppermute | solution.py:19
  29.9 28.1 %collective-permute-start.17 = (bf16[6,4,128,128]{3,2,1,0:T(8,128)(2,1)S(1)}, bf16[6,4,128,128]{3,2,1,0:T(8,128)(2,1)}, u32[]{:S(2)}, u32[]{:S(2)}) collective-permute-start(bf16[6,4,128,128]{3,2,1,0:T(8,128)(2,1)S(1)} %get-tuple-element.41.refs_4_), channel_id=1, source_target_pairs={{0,2},{1,3},{2,0},{3,1},{4,6},{5,7},{6,4},{7,5},{8,10},{9,11},{10,... | collective-permute-start | bytes 2359304 | tf_op jit(solution)/shard_map/ppermute | solution.py:19
  31.5 35.9 %collective-permute-start.3 = (bf16[6,4,128,128]{3,2,1,0:T(8,128)(2,1)S(1)}, bf16[6,4,128,128]{3,2,1,0:T(8,128)(2,1)}, u32[]{:S(2)}, u32[]{:S(2)}) collective-permute-start(bf16[6,4,128,128]{3,2,1,0:T(8,128)(2,1)S(1)} %get-tuple-element.42.refs_8_), channel_id=1, source_target_pairs={{0,2},{1,3},{2,0},{3,1},{4,6},{5,7},{6,4},{7,5},{8,10},{9,11},{10,... | collective-permute-start | bytes 2359304 | tf_op jit(solution)/shard_map/ppermute | solution.py:19
  47.1 27.7 %collective-permute-start.11 = (bf16[6,4,128,128]{3,2,1,0:T(8,128)(2,1)S(1)}, bf16[6,4,128,128]{3,2,1,0:T(8,128)(2,1)}, u32[]{:S(2)}, u32[]{:S(2)}) collective-permute-start(bf16[6,4,128,128]{3,2,1,0:T(8,128)(2,1)S(1)} %get-tuple-element.42.refs_8_), channel_id=1, source_target_pairs={{0,4},{1,5},{2,6},{3,7},{4,0},{5,1},{6,2},{7,3},{8,12},{9,13},{10,... | collective-permute-start | bytes 2359304 | tf_op jit(solution)/shard_map/ppermute | solution.py:19
  51.6 136.0 %copy-start.12 = (bf16[6,4,128,128]{3,2,1,0:T(8,128)(2,1)S(1)}, bf16[6,4,128,128]{3,2,1,0:T(8,128)(2,1)}, u32[]{:S(2)}) copy-start(bf16[6,4,128,128]{3,2,1,0:T(8,128)(2,1)} %get-tuple-element.45.refs_20_) | copy-start | bytes 2359300
  55.4 263.4 %collective-permute-start.1 = (bf16[48,128,384]{2,1,0:T(8,128)(2,1)}, bf16[48,128,384]{2,1,0:T(8,128)(2,1)}, u32[]{:S(2)}, u32[]{:S(2)}) collective-permute-start(bf16[48,128,384]{2,1,0:T(8,128)(2,1)} %panel.1.refs_0_), channel_id=1, source_target_pairs={{0,8},{1,9},{2,10},{3,11},{4,12},{5,13},{6,14},{7,15},{8,0},{9,1},... | collective-permute-start | bytes 14155784 | tf_op jit(solution)/shard_map/ppermute | solution.py:19
  58.0 26.1 %collective-permute-start.18 = (bf16[6,4,128,128]{3,2,1,0:T(8,128)(2,1)S(1)}, bf16[6,4,128,128]{3,2,1,0:T(8,128)(2,1)S(1)}, u32[]{:S(2)}, u32[]{:S(2)}) collective-permute-start(bf16[6,4,128,128]{3,2,1,0:T(8,128)(2,1)S(1)} %copy-done.15), channel_id=1, source_target_pairs={{0,2},{1,3},{2,0},{3,1},{4,6},{5,7},{6,4},{7,5},{8,10},{9,11},{10,... | collective-permute-start | bytes 2359304 | tf_op jit(solution)/shard_map/ppermute | solution.py:19
  67.4 33.6 %collective-permute-start.4 = (bf16[6,4,128,128]{3,2,1,0:T(8,128)(2,1)S(1)}, bf16[6,4,128,128]{3,2,1,0:T(8,128)(2,1)S(1)}, u32[]{:S(2)}, u32[]{:S(2)}) collective-permute-start(bf16[6,4,128,128]{3,2,1,0:T(8,128)(2,1)S(1)} %copy-done.8), channel_id=1, source_target_pairs={{0,2},{1,3},{2,0},{3,1},{4,6},{5,7},{6,4},{7,5},{8,10},{9,11},{10,... | collective-permute-start | bytes 2359304 | tf_op jit(solution)/shard_map/ppermute | solution.py:19
  74.8 107.0 %collective-permute-start.12 = (bf16[6,4,128,128]{3,2,1,0:T(8,128)(2,1)S(1)}, bf16[6,4,128,128]{3,2,1,0:T(8,128)(2,1)S(1)}, u32[]{:S(2)}, u32[]{:S(2)}) collective-permute-start(bf16[6,4,128,128]{3,2,1,0:T(8,128)(2,1)S(1)} %copy-done.8), channel_id=1, source_target_pairs={{0,4},{1,5},{2,6},{3,7},{4,0},{5,1},{6,2},{7,3},{8,12},{9,13},{10,... | collective-permute-start | bytes 2359304 | tf_op jit(solution)/shard_map/ppermute | solution.py:19
  85.0 99.3 %collective-permute-start.19 = (bf16[6,4,128,128]{3,2,1,0:T(8,128)(2,1)}, bf16[6,4,128,128]{3,2,1,0:T(8,128)(2,1)S(1)}, u32[]{:S(2)}, u32[]{:S(2)}) collective-permute-start(bf16[6,4,128,128]{3,2,1,0:T(8,128)(2,1)} %collective-permute-done.10.refs_6_), channel_id=1, source_target_pairs={{0,2},{1,3},{2,0},{3,1},{4,6},{5,7},{6,4},{7,5},{8,10},{9,11},{10,... | collective-permute-start | bytes 2359304 | tf_op jit(solution)/shard_map/ppermute | solution.py:19
  101.8 84.8 %collective-permute-start.5 = (bf16[6,4,128,128]{3,2,1,0:T(8,128)(2,1)S(1)}, bf16[6,4,128,128]{3,2,1,0:T(8,128)(2,1)S(1)}, u32[]{:S(2)}, u32[]{:S(2)}) collective-permute-start(bf16[6,4,128,128]{3,2,1,0:T(8,128)(2,1)S(1)} %copy-done.10), channel_id=1, source_target_pairs={{0,2},{1,3},{2,0},{3,1},{4,6},{5,7},{6,4},{7,5},{8,10},{9,11},{10,... | collective-permute-start | bytes 2359304 | tf_op jit(solution)/shard_map/ppermute | solution.py:19
  181.8 94.3 %collective-permute-start.13 = (bf16[6,4,128,128]{3,2,1,0:T(8,128)(2,1)S(1)}, bf16[6,4,128,128]{3,2,1,0:T(8,128)(2,1)S(1)}, u32[]{:S(2)}, u32[]{:S(2)}) collective-permute-start(bf16[6,4,128,128]{3,2,1,0:T(8,128)(2,1)S(1)} %copy-done.10), channel_id=1, source_target_pairs={{0,4},{1,5},{2,6},{3,7},{4,0},{5,1},{6,2},{7,3},{8,12},{9,13},{10,... | collective-permute-start | bytes 2359304 | tf_op jit(solution)/shard_map/ppermute | solution.py:19
  185.2 90.9 %collective-permute-start.20 = (bf16[6,4,128,128]{3,2,1,0:T(8,128)(2,1)}, bf16[6,4,128,128]{3,2,1,0:T(8,128)(2,1)S(1)}, u32[]{:S(2)}, u32[]{:S(2)}) collective-permute-start(bf16[6,4,128,128]{3,2,1,0:T(8,128)(2,1)} %collective-permute-done.11.refs_10_), channel_id=1, source_target_pairs={{0,2},{1,3},{2,0},{3,1},{4,6},{5,7},{6,4},{7,5},{8,10},{9,11},{10,... | collective-permute-start | bytes 2359304 | tf_op jit(solution)/shard_map/ppermute | solution.py:19
  187.6 91.9 %collective-permute-start.6 = (bf16[6,4,128,128]{3,2,1,0:T(8,128)(2,1)S(1)}, bf16[6,4,128,128]{3,2,1,0:T(8,128)(2,1)S(1)}, u32[]{:S(2)}, u32[]{:S(2)}) collective-permute-start(bf16[6,4,128,128]{3,2,1,0:T(8,128)(2,1)S(1)} %copy-done.12), channel_id=1, source_target_pairs={{0,2},{1,3},{2,0},{3,1},{4,6},{5,7},{6,4},{7,5},{8,10},{9,11},{10,... | collective-permute-start | bytes 2359304 | tf_op jit(solution)/shard_map/ppermute | solution.py:19
  276.1 19.5 %collective-permute-start.14 = (bf16[6,4,128,128]{3,2,1,0:T(8,128)(2,1)S(1)}, bf16[6,4,128,128]{3,2,1,0:T(8,128)(2,1)S(1)}, u32[]{:S(2)}, u32[]{:S(2)}) collective-permute-start(bf16[6,4,128,128]{3,2,1,0:T(8,128)(2,1)S(1)} %copy-done.12), channel_id=1, source_target_pairs={{0,4},{1,5},{2,6},{3,7},{4,0},{5,1},{6,2},{7,3},{8,12},{9,13},{10,... | collective-permute-start | bytes 2359304 | tf_op jit(solution)/shard_map/ppermute | solution.py:19
  277.0 20.4 %collective-permute-start.21 = (bf16[6,4,128,128]{3,2,1,0:T(8,128)(2,1)S(1)}, bf16[6,4,128,128]{3,2,1,0:T(8,128)(2,1)S(1)}, u32[]{:S(2)}, u32[]{:S(2)}) collective-permute-start(bf16[6,4,128,128]{3,2,1,0:T(8,128)(2,1)S(1)} %collective-permute-done.12.refs_14_), channel_id=1, source_target_pairs={{0,2},{1,3},{2,0},{3,1},{4,6},{5,7},{6,4},{7,5},{8,10},{9,11},{10,... | collective-permute-start | bytes 2359304 | tf_op jit(solution)/shard_map/ppermute | solution.py:19
  280.4 33.8 %collective-permute-start.7 = (bf16[6,4,128,128]{3,2,1,0:T(8,128)(2,1)S(1)}, bf16[6,4,128,128]{3,2,1,0:T(8,128)(2,1)S(1)}, u32[]{:S(2)}, u32[]{:S(2)}) collective-permute-start(bf16[6,4,128,128]{3,2,1,0:T(8,128)(2,1)S(1)} %get-tuple-element.46.refs_0_), channel_id=1, source_target_pairs={{0,2},{1,3},{2,0},{3,1},{4,6},{5,7},{6,4},{7,5},{8,10},{9,11},{10,... | collective-permute-start | bytes 2359304 | tf_op jit(solution)/shard_map/ppermute | solution.py:19
  295.6 21.1 %collective-permute-start.15 = (bf16[6,4,128,128]{3,2,1,0:T(8,128)(2,1)S(1)}, bf16[6,4,128,128]{3,2,1,0:T(8,128)(2,1)}, u32[]{:S(2)}, u32[]{:S(2)}) collective-permute-start(bf16[6,4,128,128]{3,2,1,0:T(8,128)(2,1)S(1)} %get-tuple-element.46.refs_0_), channel_id=1, source_target_pairs={{0,4},{1,5},{2,6},{3,7},{4,0},{5,1},{6,2},{7,3},{8,12},{9,13},{10,... | collective-permute-start | bytes 2359304 | tf_op jit(solution)/shard_map/ppermute | solution.py:19
  298.3 32.8 %collective-permute-start.22 = (bf16[6,4,128,128]{3,2,1,0:T(8,128)(2,1)S(1)}, bf16[6,4,128,128]{3,2,1,0:T(8,128)(2,1)S(1)}, u32[]{:S(2)}, u32[]{:S(2)}) collective-permute-start(bf16[6,4,128,128]{3,2,1,0:T(8,128)(2,1)S(1)} %collective-permute-done.13.refs_18_), channel_id=1, source_target_pairs={{0,2},{1,3},{2,0},{3,1},{4,6},{5,7},{6,4},{7,5},{8,10},{9,11},{10,... | collective-permute-start | bytes 2359304 | tf_op jit(solution)/shard_map/ppermute | solution.py:19
  315.2 31.9 %collective-permute-start.8 = (bf16[6,4,128,128]{3,2,1,0:T(8,128)(2,1)S(1)}, bf16[6,4,128,128]{3,2,1,0:T(8,128)(2,1)}, u32[]{:S(2)}, u32[]{:S(2)}) collective-permute-start(bf16[6,4,128,128]{3,2,1,0:T(8,128)(2,1)S(1)} %get-tuple-element.47.refs_4_), channel_id=1, source_target_pairs={{0,2},{1,3},{2,0},{3,1},{4,6},{5,7},{6,4},{7,5},{8,10},{9,11},{10,... | collective-permute-start | bytes 2359304 | tf_op jit(solution)/shard_map/ppermute | solution.py:19
  316.7 30.4 %collective-permute-start.16 = (bf16[6,4,128,128]{3,2,1,0:T(8,128)(2,1)S(1)}, bf16[6,4,128,128]{3,2,1,0:T(8,128)(2,1)S(1)}, u32[]{:S(2)}, u32[]{:S(2)}) collective-permute-start(bf16[6,4,128,128]{3,2,1,0:T(8,128)(2,1)S(1)} %get-tuple-element.47.refs_4_), channel_id=1, source_target_pairs={{0,4},{1,5},{2,6},{3,7},{4,0},{5,1},{6,2},{7,3},{8,12},{9,13},{10,... | collective-permute-start | bytes 2359304 | tf_op jit(solution)/shard_map/ppermute | solution.py:19
  318.8 32.0 %collective-permute-start = (bf16[48,128,384]{2,1,0:T(8,128)(2,1)}, bf16[48,128,384]{2,1,0:T(8,128)(2,1)}, u32[]{:S(2)}, u32[]{:S(2)}) collective-permute-start(bf16[48,128,384]{2,1,0:T(8,128)(2,1)} %panel.1.refs_0_), channel_id=1, source_target_pairs={{0,1},{1,0},{2,3},{3,2},{4,5},{5,4},{6,7},{7,6},{8,9},{9,8},{10,11... | collective-permute-start | bytes 14155784 | tf_op jit(solution)/shard_map/ppermute | solution.py:19
  348.1 8.3 %collective-permute-start.23 = (bf16[48,128,384]{2,1,0:T(8,128)(2,1)}, bf16[48,128,384]{2,1,0:T(8,128)(2,1)}, u32[]{:S(2)}, u32[]{:S(2)}) collective-permute-start(bf16[48,128,384]{2,1,0:T(8,128)(2,1)} %collective-permute-done.1.refs_0_), channel_id=1, source_target_pairs={{0,1},{1,0},{2,3},{3,2},{4,5},{5,4},{6,7},{7,6},{8,9},{9,8},{10,11... | collective-permute-start | bytes 14155784 | tf_op jit(solution)/shard_map/ppermute | solution.py:19
  348.2 20.3 %collective-permute-start.24 = (bf16[6,4,128,128]{3,2,1,0:T(8,128)(2,1)}, bf16[6,4,128,128]{3,2,1,0:T(8,128)(2,1)}, u32[]{:S(2)}, u32[]{:S(2)}) collective-permute-start(bf16[6,4,128,128]{3,2,1,0:T(8,128)(2,1)} %copy-done.35), channel_id=1, source_target_pairs={{0,2},{1,3},{2,0},{3,1},{4,6},{5,7},{6,4},{7,5},{8,10},{9,11},{10,... | collective-permute-start | bytes 2359304 | tf_op jit(solution)/shard_map/ppermute | solution.py:19
  395.3 43.5 %collective-permute-start.25 = (f32[36,128,384]{2,1,0:T(8,128)}, f32[36,128,384]{2,1,0:T(8,128)}, u32[]{:S(2)}, u32[]{:S(2)}) collective-permute-start(f32[36,128,384]{2,1,0:T(8,128)} %get-tuple-element.56), channel_id=1, source_target_pairs={{0,1},{1,0},{2,3},{3,2},{4,5},{5,4},{6,7},{7,6},{8,9},{9,8},{10,11... | collective-permute-start | bytes 21233672 | tf_op jit(solution)/shard_map/ppermute | solution.py:19
  395.4 20.2 %collective-permute-start.26 = (bf16[6,4,128,128]{3,2,1,0:T(8,128)(2,1)}, bf16[6,4,128,128]{3,2,1,0:T(8,128)(2,1)S(1)}, u32[]{:S(2)}, u32[]{:S(2)}) collective-permute-start(bf16[6,4,128,128]{3,2,1,0:T(8,128)(2,1)} %collective-permute-done.15.refs_2_), channel_id=1, source_target_pairs={{0,2},{1,3},{2,0},{3,1},{4,6},{5,7},{6,4},{7,5},{8,10},{9,11},{10,... | collective-permute-start | bytes 2359304 | tf_op jit(solution)/shard_map/ppermute | solution.py:19
  397.0 19.8 %collective-permute-start.27 = (bf16[6,4,128,128]{3,2,1,0:T(8,128)(2,1)}, bf16[6,4,128,128]{3,2,1,0:T(8,128)(2,1)S(1)}, u32[]{:S(2)}, u32[]{:S(2)}) collective-permute-start(bf16[6,4,128,128]{3,2,1,0:T(8,128)(2,1)} %collective-permute-done.8.refs_5_), channel_id=1, source_target_pairs={{0,4},{1,5},{2,6},{3,7},{4,0},{5,1},{6,2},{7,3},{8,12},{9,13},{10,... | collective-permute-start | bytes 2359304 | tf_op jit(solution)/shard_map/ppermute | solution.py:19
  438.3 9.2 %collective-permute-start.28 = (f32[12,128,384]{2,1,0:T(8,128)}, f32[12,128,384]{2,1,0:T(8,128)}, u32[]{:S(2)}, u32[]{:S(2)}) collective-permute-start(f32[12,128,384]{2,1,0:T(8,128)} %get-tuple-element.61), channel_id=1, source_target_pairs={{0,1},{1,0},{2,3},{3,2},{4,5},{5,4},{6,7},{7,6},{8,9},{9,8},{10,11... | collective-permute-start | bytes 7077896 | tf_op jit(solution)/shard_map/ppermute | solution.py:19
  449.9 4.7 %collective-permute-start.29 = (f32[8,384]{1,0:T(8,128)S(1)}, f32[8,384]{1,0:T(8,128)S(1)}, u32[]{:S(2)}, u32[]{:S(2)}) collective-permute-start(f32[8,384]{1,0:T(8,128)S(1)} %get-tuple-element.62.sums_ref), channel_id=1, source_target_pairs={{0,8},{1,9},{2,10},{3,11},{4,12},{5,13},{6,14},{7,15},{8,0},{9,1},... | collective-permute-start | bytes 36872 | tf_op jit(solution)/shard_map/ppermute | solution.py:19
  (47 other events, 495.8 us)

commit v3 on v2

v3 whole, which is shorter than its diff:
```python
import functools
import math

import jax
import jax.numpy as jnp
from jax import lax
from jax.experimental import pallas as pl
from jax.experimental.pallas import tpu as pltpu
from jax.sharding import PartitionSpec as P

GC = 8
CB = 12
PC = CB // 4
STRIPS = GC // 2
MIB = 1 << 20
SHORT = pl.CostEstimate(flops=0, bytes_accessed=1024, transcendentals=0)


def swapped(array, mask, among=lambda i: True):
    pairs = [(i, i ^ mask) for i in range(lax.axis_size("grid")) if among(i)]
    return lax.ppermute(array, "grid", pairs)


def inner(i):
    return (i ^ i >> 1) & (GC // 2) != 0


def panel_kernel(slot_ref, tiles_ref, panel_ref):
    rows, _, width, _ = tiles_ref.shape
    first = pl.program_id(0) * rows

    @pl.loop(0, rows)
    def _(r):
        for p in range(PC):
            slot = slot_ref[(first + r) * PC + p]
            tile = tiles_ref[r, jnp.maximum(slot, 0)]
            panel_ref[r, :, p * width : (p + 1) * width] = jnp.where(
                slot >= 0, tile, jnp.zeros_like(tile)
            )


def make_panel(tile_values, slots):
    block_rows, slots_per_row, width, _ = tile_values.shape
    step = math.gcd(block_rows, 12)
    return pl.pallas_call(
        panel_kernel,
        grid_spec=pltpu.PrefetchScalarGridSpec(
            num_scalar_prefetch=1,
            grid=(block_rows // step,),
            in_specs=[pl.BlockSpec((step, slots_per_row, width, width), lambda i, s: (i, 0, 0, 0))],
            out_specs=pl.BlockSpec((step, width, PC * width), lambda i, s: (i, 0, 0)),
        ),
        out_shape=jax.ShapeDtypeStruct((block_rows, width, PC * width), jnp.bfloat16),
        compiler_params=pltpu.CompilerParams(vmem_limit_bytes=12 * MIB),
        cost_estimate=SHORT,
        name="panel",
    )(slots.reshape(-1), tile_values)


def pack_kernel(first, parts, where_ref, *refs):
    sources, packed_ref, sem = refs[: 2 * parts], refs[-2], refs[-1]
    part_rows, _, half = sources[0].shape
    unit = math.gcd(CB, part_rows)
    for n in range(packed_ref.shape[0] // unit):
        part = where_ref[2 * (first + n)]
        offset = where_ref[2 * (first + n) + 1]
        for m in range(parts):

            @pl.when((part == m) | (parts == 1))
            def _():
                for side in range(2):
                    pltpu.make_async_copy(
                        sources[side * parts + m].at[pl.ds(offset, unit)],
                        packed_ref.at[pl.ds(n * unit, unit), :, pl.ds(side * half, half)],
                        sem.at[side],
                    ).start()
    for side in range(2):
        cols = pl.ds(side * half, half)
        pltpu.make_async_copy(
            packed_ref.at[:, :, cols], packed_ref.at[:, :, cols], sem.at[side]
        ).wait()


def pack(where, first, mine, others):
    parts = len(mine)
    _, width, half = mine[0].shape
    return pl.pallas_call(
        functools.partial(pack_kernel, first, parts),
        out_shape=jax.ShapeDtypeStruct((STRIPS // 2 * CB, width, 2 * half), jnp.bfloat16),
        in_specs=[pl.BlockSpec(memory_space=pltpu.SMEM)]
        + [pl.BlockSpec(memory_space=pl.ANY)] * (2 * parts),
        out_specs=pl.BlockSpec(memory_space=pltpu.VMEM),
        scratch_shapes=[pltpu.SemaphoreType.DMA((2,))],
        compiler_params=pltpu.CompilerParams(vmem_limit_bytes=8 * MIB),
        cost_estimate=SHORT,
        name="pack",
    )(where, *mine, *others)


def expand_kernel(offsets, order_ref, index_ref, near_ref, far_ref, *refs):
    tile_refs = refs[:STRIPS]
    mine_ref, other_ref, tiles, sums, tile_sem, sum_sem = refs[STRIPS:]
    _, _, rows, slots, width, _ = tiles.shape
    half = PC * width
    total_rows = mine_ref.shape[0]
    steps = total_rows // rows

    def fetch(k):
        return [
            pltpu.make_async_copy(
                source.at[pl.ds(offset + k * rows, rows)], tiles.at[k % 2, q], tile_sem.at[k % 2, q]
            )
            for q, (source, offset) in enumerate(zip(tile_refs, offsets))
        ]

    def stores(row, slot):
        return [
            pltpu.make_async_copy(
                sums.at[slot, :, pl.ds(side * half, half)], out.at[row], sum_sem.at[slot, side]
            )
            for side, out in enumerate((mine_ref, other_ref))
        ]

    for copy in fetch(0):
        copy.start()
    for k in range(steps):
        if k + 1 < steps:
            for copy in fetch(k + 1):
                copy.start()
        for copy in fetch(k):
            copy.wait()

        @pl.loop(0, rows)
        def _(r):
            row = k * rows + r
            slot = lax.rem(row, 2)

            @pl.when(row >= 2)
            def _():
                for copy in stores(row - 2, slot):
                    copy.wait()

            total = None
            for n in range(STRIPS):
                panel = near_ref if n < STRIPS // 2 else far_ref
                q = order_ref[n]
                for t in range(0, slots, 2):
                    base = row * (STRIPS * slots) + n * slots + t
                    left = jnp.concatenate(
                        [tiles[k % 2, q, r, t], tiles[k % 2, q, r, t + 1]], axis=1
                    )
                    right = jnp.concatenate(
                        [panel[index_ref[base]], panel[index_ref[base + 1]]], axis=0
                    )
                    term = jnp.dot(left, right, preferred_element_type=jnp.float32)
                    total = term if total is None else total + term
            sums[slot] = total
            for copy in stores(row, slot):
                copy.start()

    for row in range(max(total_rows - 2, 0), total_rows):
        for copy in stores(row, row % 2):
            copy.wait()


def expand(sources, order, index, near, far):
    arrays, offsets = zip(*sources)
    _, slots, width, _ = arrays[0].shape
    total_rows = index.shape[0]
    rows = math.gcd(total_rows, 6)
    half = jax.ShapeDtypeStruct((total_rows, width, PC * width), jnp.float32)
    anywhere = pl.BlockSpec(memory_space=pl.ANY)
    smem = pl.BlockSpec(memory_space=pltpu.SMEM)
    vmem = pl.BlockSpec(memory_space=pltpu.VMEM)
    return pl.pallas_call(
        functools.partial(expand_kernel, offsets),
        out_shape=(half, half),
        in_specs=[smem, smem, vmem, vmem] + [anywhere] * STRIPS,
        out_specs=(anywhere, anywhere),
        scratch_shapes=[
            pltpu.VMEM((2, STRIPS, rows, slots, width, width), jnp.bfloat16),
            pltpu.VMEM((2, width, 2 * PC * width), jnp.float32),
            pltpu.SemaphoreType.DMA((2, STRIPS)),
            pltpu.SemaphoreType.DMA((2, 2)),
        ],
        compiler_params=pltpu.CompilerParams(vmem_limit_bytes=12 * MIB),
        cost_estimate=SHORT,
        name="expand",
    )(order, index.reshape(-1), near, far, *arrays)


def square_kernel(keep_ref, before_ref, mine_ref, got_ref, *refs):
    squared_ref, sums_ref = refs[-2:]
    rows, width, _ = mine_ref.shape
    first = pl.program_id(0) * rows

    @pl.when(pl.program_id(0) == 0)
    def _():
        sums_ref[...] = before_ref[...]

    @pl.loop(0, rows)
    def _(r):
        for p in range(PC):
            keep = keep_ref[(first + r) * PC + p].astype(jnp.float32)
            cols = slice(p * width, (p + 1) * width)
            value = mine_ref[r, :, cols] + got_ref[r, :, cols]
            value = value * value * keep
            squared_ref[r, :, cols] = value
            sums_ref[:, cols] += jnp.sum(value.reshape(width // 8, 8, width), axis=0)


def square(keep, before, mine, got, lo, total_rows, buffer):
    rows, width, half = mine.shape
    step = math.gcd(math.gcd(rows, 6), lo) if lo else math.gcd(rows, 6)
    block = pl.BlockSpec((step, width, half), lambda i, s: (i, 0, 0))
    target = pl.BlockSpec((step, width, half), lambda i, s: (lo // step + i, 0, 0))
    sums = pl.BlockSpec((8, half), lambda i, s: (0, 0))
    operands = [keep.reshape(-1), before, mine, got]
    in_specs = [sums, block, block]
    aliases = {}
    if buffer is not None:
        operands.append(buffer)
        in_specs.append(pl.BlockSpec(memory_space=pl.ANY))
        aliases = {len(operands) - 1: 0}
    return pl.pallas_call(
        square_kernel,
        grid_spec=pltpu.PrefetchScalarGridSpec(
            num_scalar_prefetch=1,
            grid=(rows // step,),
            in_specs=in_specs,
            out_specs=(target, sums),
        ),
        out_shape=(
            jax.ShapeDtypeStruct((total_rows, width, half), jnp.float32),
            jax.ShapeDtypeStruct((8, half), jnp.float32),
        ),
        input_output_aliases=aliases,
        compiler_params=pltpu.CompilerParams(vmem_limit_bytes=12 * MIB),
        cost_estimate=SHORT,
        name="square",
    )(*operands)


def scale_kernel(count, sums_ref, got_ref, squared_ref, out_ref):
    step, width, _ = squared_ref.shape
    for p in range(PC):
        cols = slice(p * width, (p + 1) * width)
        sums = jnp.sum(sums_ref[:, cols] + got_ref[:, cols], axis=0, keepdims=True)
        inverse = 1.0 / (sums / count + 1e-6)
        for r in range(step):
            out_ref[r, p] = squared_ref[r, :, cols] * inverse


def scale(count, sums, got, squared):
    rows, width, half = squared.shape
    step = math.gcd(rows, 6)
    return pl.pallas_call(
        functools.partial(scale_kernel, count),
        grid=(rows // step,),
        in_specs=[pl.BlockSpec((8, half), lambda i: (0, 0))] * 2
        + [pl.BlockSpec((step, width, half), lambda i: (i, 0, 0))],
        out_specs=pl.BlockSpec((step, PC, width, width), lambda i: (i, 0, 0, 0)),
        out_shape=jax.ShapeDtypeStruct((rows, PC, width, width), jnp.float32),
        compiler_params=pltpu.CompilerParams(vmem_limit_bytes=12 * MIB),
        cost_estimate=SHORT,
        name="scale",
    )(sums, got, squared)


def after(array, *earlier):
    return lax.optimization_barrier((array, *earlier))[0]


def shards(tile_values, tile_columns, keep_tiles):
    devices = lax.axis_size("grid")
    device = lax.axis_index("grid")
    all_bits = devices.bit_length() - 1
    low_bits = GC.bit_length() - 1
    grid_rows = devices // GC
    row_strip = device // GC
    col_strip = device % GC
    block_rows, slots, width, _ = tile_values.shape
    pair = STRIPS // 2

    strip_rows = lax.dynamic_slice_in_dim(tile_columns, row_strip * block_rows, block_rows, 0)
    far_first = 0
    if block_rows == pair * 2 * CB:
        far_first = pair * (col_strip // (pair * 2) != row_strip).astype(jnp.int32)
    order = jnp.bitwise_xor(jnp.arange(STRIPS, dtype=jnp.int32), far_first)
    strips = jnp.bitwise_xor(col_strip, 2 * order)
    own = jnp.take(strip_rows, col_strip, axis=1)
    match = own[:, :, None] == jnp.arange(PC, dtype=jnp.int32)
    slot = jnp.max(
        jnp.where(match, jnp.arange(slots, dtype=jnp.int32)[None, :, None], -1), axis=1
    )
    index = jnp.take(strip_rows, strips, axis=1)
    index = index + CB * (jnp.arange(STRIPS, dtype=jnp.int32) % pair)[None, :, None]
    index = index.reshape(block_rows, STRIPS * slots)
    relayed = grid_rows == 2 and block_rows == 2 * pair * CB
    unit = math.gcd(CB, block_rows)
    unit_rows = strips[:, None] * CB + unit * jnp.arange(CB // unit, dtype=jnp.int32)
    part = jnp.bitwise_xor(unit_rows // block_rows, row_strip)
    offset = unit_rows % block_rows
    if relayed:
        part, offset = offset // (2 * CB), offset % CB
    where = jnp.stack([part, offset], axis=-1).reshape(-1)
    half = len(where) // 2

    def shared(pieces):
        odd = col_strip % 2 == 1
        pieces = [p[r : r + CB] for p in pieces for r in range(0, p.shape[0], CB)]
        kept = [jnp.where(odd, b, a) for a, b in zip(pieces[::2], pieces[1::2])]
        given = [jnp.where(odd, a, b) for a, b in zip(pieces[::2], pieces[1::2])]
        return kept, [swapped(p, 1) for p in given]

    cuts = [0, 3 * block_rows // 8, 2 * (3 * block_rows // 8), block_rows]
    parts = list(zip(cuts[:-1], cuts[1:]))
    own = [tile_values[lo:hi] for lo, hi in parts]
    panel = make_panel(tile_values, slot)
    from_x = swapped(tile_values, 2)
    from_z = [swapped(own[0], 4)]
    if relayed:
        step = block_rows // 2
        is_inner = inner(device)
        pieces = [panel[:step], panel[step:]]
        near = pack(where, 0, *shared(pieces))
        across = GC + GC // 2
        crossed = [swapped(pieces[0], across, inner)]
        crossed.append(swapped(after(pieces[1], crossed[0]), across, inner))
        passed = []
        for got, piece in zip(crossed, pieces):
            got = after(got, *(passed or from_z))
            passed.append(swapped(jnp.where(is_inner, got, piece), 4))
        returned = [swapped(after(passed[0], crossed[1]), across, inner)]
        returned.append(swapped(after(passed[1], returned[0]), across, inner))
        far = [jnp.where(is_inner, a, b) for a, b in zip(returned, passed)]
        far = pack(where, half // 2, *shared(far))
        own[1] = after(own[1], passed[1], near)
    else:
        panels = [panel]
        for bit in range(low_bits, all_bits):
            panels = panels + [swapped(p, 1 << bit) for p in panels]
        others = [swapped(p, 1) for p in panels]
        near = pack(where, 0, panels, others)
        far = pack(where, half // 2, panels, others)
    from_xz = [swapped(after(from_z[0], from_x), 2)]
    from_z.append(swapped(own[1], 4))
    last = jnp.concatenate([from_x[cuts[2] :], own[2]])
    last = swapped(after(last, from_z[1], from_xz[0]), 4)
    from_xz.append(swapped(after(from_z[1], from_xz[0]), 2))

    squared = None
    sums = jnp.zeros((8, PC * width), jnp.float32)
    for n, (lo, hi) in enumerate(parts):
        if n < 2:
            received = [(from_z[n], 0), (from_xz[n], 0)]
        else:
            received = [(last, hi - lo), (last, 0)]
        mine, other = expand(
            [(tile_values, lo), (from_x, lo)] + received, order, index[lo:hi], near, far
        )
        got = swapped(other, 1)
        squared, sums = square(keep_tiles[lo:hi], sums, mine, got, lo, block_rows, squared)
    for bit in range(low_bits, all_bits - 1):
        sums = sums + swapped(sums, 1 << bit)
    got = swapped(sums, 1 << (all_bits - 1))
    return scale(float(CB * GC * width), sums, got, squared)


def solution(mesh):
    return jax.shard_map(
        shards,
        mesh=mesh,
        in_specs=(
            P(("groups", "grid"), None, None, None),
            P("groups", None, None),
            P(("groups", "grid"), None),
        ),
        out_specs=P(("groups", "grid"), None, None, None),
        check_vma=False,
    )
```

time: 459 us -> 352 us (0.77)
  waiting for transfers between devices: 322 us -> 197 us
  other arithmetic: 0.3 us -> 19 us
  starting transfers between devices: 37.9 us -> 28 us
  Pallas kernels: 59.4 us -> 65.6 us
    ppermute x30 -> x20, waiting for transfers between devices: 322 us -> 197 us  [swapped(): return lax.ppermute(array, 'grid', pairs)]
    select_n x1 -> x7, other arithmetic: 0.02 us -> 12.4 us  [the longest x3 6.65 us: shared(): given = [jnp.where(odd, a, b) for a, b in zip(pieces[::2], pieces[1::2])]]
    ppermute x30 -> x20, starting transfers between devices: 37.9 us -> 28 us  [swapped(): return lax.ppermute(array, 'grid', pairs)]
    unnamed x98 -> x46, local copies, waits for them, and re-layouts: 29.8 us -> 20.6 us
    slice x4 -> x9, local copies, waits for them, and re-layouts: 6.75 us -> 13.4 us  [the longest x2 7.91 us: shards(): own = [tile_values[lo:hi] for lo, hi in parts]]
    pallas_call x3 -> x4, Pallas kernels: 40.9 us -> 45.7 us  [the longest x3 40.9 us: expand(): pl.pallas_call(functools.partial(expand_kernel, offsets), out_shape=(half...]
    pallas_call x2 -> x3, Pallas kernels: 8.03 us -> 9.78 us  [square(): pl.pallas_call(square_kernel, grid_spec=pltpu.PrefetchScalarGridSpec(num_...]
  transfers between devices with their start and end apart: 30 -> 20, of which waited for: 18 -> 11; matrix products, arithmetic and copies ran while one was open for 0% -> 10% of each run, Pallas kernels for 6% -> 15%
where the time goes in v3:
time: 352 us; the launch traced here: 351 us
  waiting for transfers between devices  197 us (56%)
  Pallas kernels  65.6 us (19%)
  local copies, waits for them, and re-layouts  40.8 us (12%)
  starting transfers between devices  28 us (8%)
  other arithmetic  19 us (5%)
    ppermute x20, waiting for transfers between devices, swapped(): return lax.ppermute(array, 'grid', pairs)  197 us
    pallas_call x3, Pallas kernels, expand(): pl.pallas_call(functools.partial(expand_kernel, offsets), out_shape=(half...  40.9 us
    ppermute x20, starting transfers between devices, swapped(): return lax.ppermute(array, 'grid', pairs)  28 us
    unnamed x46, local copies, waits for them, and re-layouts  20.6 us
    pallas_call x3, Pallas kernels, square(): pl.pallas_call(square_kernel, grid_spec=pltpu.PrefetchScalarGridSpec(num_...  9.78 us
    slice x2, local copies, waits for them, and re-layouts, shards(): own = [tile_values[lo:hi] for lo, hi in parts]  7.91 us
  transfers between devices with their start and end apart: 20, of which 11 were waited for; matrix products, arithmetic and copies ran while one was open for 10% of the time, Pallas kernels for 15%

profile of v3, /device:TPU:0, one launch (start us, length us, event | category | flops | bytes accessed | tf_op | source)
XLA Modules:
  0.0 351.1 jit_solution(414514258025251568)
XLA Ops:
  1.0 4.8 %panel.1 = bf16[48,128,384]{2,1,0:T(8,128)(2,1)S(1)} custom-call(s32[144]{0:T(256)S(1)} %reshape.178.slot_ref, bf16[48,4,128,128]{3,2,1,0:T(8,128)(2,1)} %refs_0_.5), custom_call_target="tpu_custom_call" | custom-call | bytes 1024 | tf_op jit(solution)/shard_map/panel/pallas_call | solution.py:45
  5.8 2.2 copy-done
  11.8 6.3 %fusion.3 = (bf16[18,4,128,128]{3,2,1,0:T(8,128)(2,1)}, bf16[18,4,128,128]{3,2,1,0:T(8,128)(2,1)}) fusion(bf16[48,4,128,128]{3,2,1,0:T(8,128)(2,1)} %refs_0_.5), kind=kLoop, calls=%fused_computation.35 | loop fusion | bytes 9437184 | tf_op jit(solution)/shard_map/slice | solution.py:318
  18.1 4.5 %collective-permute-start.3 = (bf16[18,4,128,128]{3,2,1,0:T(8,128)(2,1)}, bf16[18,4,128,128]{3,2,1,0:T(8,128)(2,1)S(1)}, u32[]{:S(2)}, u32[]{:S(2)}) collective-permute-start(bf16[18,4,128,128]{3,2,1,0:T(8,128)(2,1)} %get-tuple-element.59), channel_id=1, source_target_pairs={{0,4},{1,5},{2,6},{3,7},{4,0},{5,1},{6,2},{7,3},{8,12},{9,13},{10,... | collective-permute-start | bytes 7077896 | tf_op jit(solution)/shard_map/ppermute | solution.py:21
  24.1 49.7 %collective-permute-done.3.refs_2_ = bf16[18,4,128,128]{3,2,1,0:T(8,128)(2,1)S(1)} collective-permute-done((bf16[18,4,128,128]{3,2,1,0:T(8,128)(2,1)}, bf16[18,4,128,128]{3,2,1,0:T(8,128)(2,1)S(1)}, u32[]{:S(2)}, u32[]{:S(2)}) %collective-permute-start.3) | collective-permute-done | bytes 2359328 | tf_op jit(solution)/shard_map/ppermute | solution.py:21
  73.7 3.7 %fusion.4 = (bf16[24,128,384]{2,1,0:T(8,128)(2,1)S(1)}, bf16[24,128,384]{2,1,0:T(8,128)(2,1)S(1)}) fusion(bf16[48,128,384]{2,1,0:T(8,128)(2,1)} %copy-done, bf16[24,128,384]{2,1,0:T(8,128)(2,1)} %collective-permute-done.2, pred[]{:T(512)S(6)} %ne.147), kind=kLoop, calls=%fused_computation.36 | loop fusion | flops 1179648 | bytes 11796481 | tf_op jit(solution)/shard_map/slice | solution.py:325
  78.3 4.1 %collective-permute-start.4 = (bf16[24,128,384]{2,1,0:T(8,128)(2,1)S(1)}, bf16[24,128,384]{2,1,0:T(8,128)(2,1)}, u32[]{:S(2)}, u32[]{:S(2)}) collective-permute-start(bf16[24,128,384]{2,1,0:T(8,128)(2,1)S(1)} %get-tuple-element.61), channel_id=1, source_target_pairs={{0,4},{1,5},{2,6},{3,7},{4,0},{5,1},{6,2},{7,3},{8,12},{9,13},{10,... | collective-permute-start | bytes 7077896 | tf_op jit(solution)/shard_map/ppermute | solution.py:21
  82.3 50.0 %collective-permute-done.4 = bf16[24,128,384]{2,1,0:T(8,128)(2,1)} collective-permute-done((bf16[24,128,384]{2,1,0:T(8,128)(2,1)S(1)}, bf16[24,128,384]{2,1,0:T(8,128)(2,1)}, u32[]{:S(2)}, u32[]{:S(2)}) %collective-permute-start.4) | collective-permute-done | bytes 2359328 | tf_op jit(solution)/shard_map/ppermute | solution.py:21
  137.8 4.2 %broadcast_select_fusion.8 = (bf16[12,128,384]{2,1,0:T(8,128)(2,1)}, bf16[12,128,384]{2,1,0:T(8,128)(2,1)S(1)}, bf16[12,128,384]{2,1,0:T(8,128)(2,1)}, bf16[12,128,384]{2,1,0:T(8,128)(2,1)S(1)}) fusion(pred[]{:T(512)S(6)} %eq.26, bf16[48,128,384]{2,1,0:T(8,128)(2,1)} %copy-done), kind=kLoop, calls=%fused_computation.10 | loop fusion | flops 2359296 | bytes 9437185 | tf_op jit(solution)/shard_map/jit(_where)/select_n | solution.py:313
  142.7 4.0 %collective-permute-done.refs_2_ = bf16[12,128,384]{2,1,0:T(8,128)(2,1)S(1)} collective-permute-done((bf16[12,128,384]{2,1,0:T(8,128)(2,1)}, bf16[12,128,384]{2,1,0:T(8,128)(2,1)S(1)}, u32[]{:S(2)}, u32[]{:S(2)}) %collective-permute-start) | collective-permute-done | bytes 1179680 | tf_op jit(solution)/shard_map/ppermute | solution.py:21
  146.9 2.7 pack.2.near_ref
  149.6 2.2 copy-done.1
  151.7 7.8 %collective-permute-done.11.refs_1_ = bf16[48,4,128,128]{3,2,1,0:T(8,128)(2,1)} collective-permute-done((bf16[48,4,128,128]{3,2,1,0:T(8,128)(2,1)}, bf16[48,4,128,128]{3,2,1,0:T(8,128)(2,1)}, u32[]{:S(2)}, u32[]{:S(2)}) %collective-permute-start.11) | collective-permute-done | bytes 6291488 | tf_op jit(solution)/shard_map/ppermute | solution.py:21
  161.1 24.6 %collective-permute-done.7 = bf16[24,128,384]{2,1,0:T(8,128)(2,1)} collective-permute-done((bf16[24,128,384]{2,1,0:T(8,128)(2,1)}, bf16[24,128,384]{2,1,0:T(8,128)(2,1)}, u32[]{:S(2)}, u32[]{:S(2)}) %collective-permute-start.7) | collective-permute-done | bytes 2359328 | tf_op jit(solution)/shard_map/ppermute | solution.py:21
  193.3 17.8 %collective-permute-done.12.refs_3_ = bf16[18,4,128,128]{3,2,1,0:T(8,128)(2,1)S(1)} collective-permute-done((bf16[18,4,128,128]{3,2,1,0:T(8,128)(2,1)S(1)}, bf16[18,4,128,128]{3,2,1,0:T(8,128)(2,1)S(1)}, u32[]{:S(2)}, u32[]{:S(2)}) %collective-permute-start.12) | collective-permute-done | bytes 2359328 | tf_op jit(solution)/shard_map/ppermute | solution.py:21
  211.1 24.8 %collective-permute-done.14.refs_2_ = bf16[18,4,128,128]{3,2,1,0:T(8,128)(2,1)} collective-permute-done((bf16[18,4,128,128]{3,2,1,0:T(8,128)(2,1)S(1)}, bf16[18,4,128,128]{3,2,1,0:T(8,128)(2,1)}, u32[]{:S(2)}, u32[]{:S(2)}) %collective-permute-start.14) | collective-permute-done | bytes 2359328 | tf_op jit(solution)/shard_map/ppermute | solution.py:21
  242.1 2.1 broadcast_select_fusion
  248.8 2.6 pack.3.far_ref
  253.1 15.4 %expand.3 = (f32[18,128,384]{2,1,0:T(8,128)S(1)}, f32[18,128,384]{2,1,0:T(8,128)}) custom-call(s32[4]{0:T(128)S(1)} %iota_xor_fusion.order_ref, s32[288]{0:T(512)S(1)} %reshape.176.index_ref, bf16[24,128,768]{2,1,0:T(8,128)(2,1)S(1)} %bitcast.11, bf16[24,128,768]{2,1,0:T(8,128)(2,1)S(1)} %pack.3.far_ref, bf16[48,4,128,128]{3,2,1,0:T(8,128)(2,1)} %refs_0_.5, ...), custom_call_target="tpu_custom_call" | custom-call | bytes 1024 | tf_op jit(solution)/shard_map/expand/pallas_call | solution.py:175
  270.8 14.6 %collective-permute-done.15.refs_3_ = bf16[18,4,128,128]{3,2,1,0:T(8,128)(2,1)} collective-permute-done((bf16[18,4,128,128]{3,2,1,0:T(8,128)(2,1)}, bf16[18,4,128,128]{3,2,1,0:T(8,128)(2,1)}, u32[]{:S(2)}, u32[]{:S(2)}) %collective-permute-start.15) | collective-permute-done | bytes 2359328 | tf_op jit(solution)/shard_map/ppermute | solution.py:21
  285.4 2.3 copy-done.2
  287.7 2.3 copy-done.5
  290.1 14.7 %expand.4 = (f32[18,128,384]{2,1,0:T(8,128)S(1)}, f32[18,128,384]{2,1,0:T(8,128)}) custom-call(s32[4]{0:T(128)S(1)} %iota_xor_fusion.order_ref, s32[288]{0:T(512)S(1)} %reshape.179.index_ref, bf16[24,128,768]{2,1,0:T(8,128)(2,1)S(1)} %copy-done.2, bf16[24,128,768]{2,1,0:T(8,128)(2,1)S(1)} %copy-done.5, bf16[48,4,128,128]{3,2,1,0:T(8,128)(2,1)} %refs_0_.5, ...), custom_call_target="tpu_custom_call" | custom-call | bytes 1024 | tf_op jit(solution)/shard_map/expand/pallas_call | solution.py:175
  307.8 2.3 copy-done.3
  310.2 2.3 copy-done.6
  312.5 10.8 %expand.5 = (f32[12,128,384]{2,1,0:T(8,128)S(1)}, f32[12,128,384]{2,1,0:T(8,128)}) custom-call(s32[4]{0:T(128)S(1)} %iota_xor_fusion.order_ref, s32[192]{0:T(256)S(1)} %reshape.180.index_ref, bf16[24,128,768]{2,1,0:T(8,128)(2,1)S(1)} %copy-done.3, bf16[24,128,768]{2,1,0:T(8,128)(2,1)S(1)} %copy-done.6, bf16[48,4,128,128]{3,2,1,0:T(8,128)(2,1)} %refs_0_.5, ...), custom_call_target="tpu_custom_call" | custom-call | bytes 1024 | tf_op jit(solution)/shard_map/expand/pallas_call | solution.py:175
  331.8 3.6 %square.3 = (f32[48,128,384]{2,1,0:T(8,128)S(1)}, f32[8,384]{1,0:T(8,128)S(1)}) custom-call(s32[54]{0:T(128)S(1)} %reshape.175.keep_ref, f32[8,384]{1,0:T(8,128)S(1)} %broadcast_in_dim.42.before_ref, f32[18,128,384]{2,1,0:T(8,128)S(1)} %copy-done.8, f32[18,128,384]{2,1,0:T(8,128)} %collective-permute-done.13.got_ref), custom_call_target="tpu_custom_call" | custom-call | bytes 1024 | tf_op jit(solution)/shard_map/square/pallas_call | solution.py:225
  335.4 3.8 %square.4 = (f32[48,128,384]{2,1,0:T(8,128)S(1)}, f32[8,384]{1,0:T(8,128)S(1)}) custom-call(s32[54]{0:T(128)S(1)} %reshape.174.keep_ref, f32[8,384]{1,0:T(8,128)S(1)} %get-tuple-element.34.before_ref, f32[18,128,384]{2,1,0:T(8,128)S(1)} %get-tuple-element.37.mine_ref, ...), custom_call_target="tpu_custom_call", output_to_operand_aliasing={{0}: (4, {})} | custom-call | bytes 1024 | tf_op jit(solution)/shard_map/square/pallas_call | solution.py:225
  339.2 2.4 square.5
  341.6 2.2 collective-permute-start.19
  343.9 2.4 collective-permute-done.19.got_ref
  346.3 4.8 %scale.1 = f32[48,3,128,128]{3,2,1,0:T(8,128)} custom-call(f32[8,384]{1,0:T(8,128)S(1)} %get-tuple-element.45.sums_ref, f32[8,384]{1,0:T(8,128)S(1)} %collective-permute-done.19.got_ref, f32[48,128,384]{2,1,0:T(8,128)S(1)} %get-tuple-element.46.squared_ref), custom_call_target="tpu_custom_call" | custom-call | bytes 1024 | tf_op jit(solution)/shard_map/scale/pallas_call | solution.py:257
  (110 shorter events, 48.8 us)
Async XLA Ops:
  9.7 14.3 %collective-permute-start.2 = (bf16[24,128,384]{2,1,0:T(8,128)(2,1)}, bf16[24,128,384]{2,1,0:T(8,128)(2,1)}, u32[]{:S(2)}, u32[]{:S(2)}) collective-permute-start(bf16[24,128,384]{2,1,0:T(8,128)(2,1)} %slice.103), channel_id=1, source_target_pairs={{4,8},{5,9},{6,10},{7,11},{8,4},{9,5},{10,6},{11,7},{20,24},{21,25... | collective-permute-start | bytes 7077896 | tf_op jit(solution)/shard_map/ppermute | solution.py:21
  18.1 55.6 %collective-permute-start.3 = (bf16[18,4,128,128]{3,2,1,0:T(8,128)(2,1)}, bf16[18,4,128,128]{3,2,1,0:T(8,128)(2,1)S(1)}, u32[]{:S(2)}, u32[]{:S(2)}) collective-permute-start(bf16[18,4,128,128]{3,2,1,0:T(8,128)(2,1)} %get-tuple-element.59), channel_id=1, source_target_pairs={{0,4},{1,5},{2,6},{3,7},{4,0},{5,1},{6,2},{7,3},{8,12},{9,13},{10,... | collective-permute-start | bytes 7077896 | tf_op jit(solution)/shard_map/ppermute | solution.py:21
  22.6 137.0 %collective-permute-start.11 = (bf16[48,4,128,128]{3,2,1,0:T(8,128)(2,1)}, bf16[48,4,128,128]{3,2,1,0:T(8,128)(2,1)}, u32[]{:S(2)}, u32[]{:S(2)}) collective-permute-start(bf16[48,4,128,128]{3,2,1,0:T(8,128)(2,1)} %refs_0_.5), channel_id=1, source_target_pairs={{0,2},{1,3},{2,0},{3,1},{4,6},{5,7},{6,4},{7,5},{8,10},{9,11},{10,... | collective-permute-start | bytes 18874376 | tf_op jit(solution)/shard_map/ppermute | solution.py:21
  24.1 108.3 %slice-start = ((s8[4718592]{0:T(1024)(128)(4,1)}), s8[524288]{0:T(1024)(128)(4,1)S(1)}, s32[]{:S(2)}) async-start(s8[4718592]{0:T(1024)(128)(4,1)} %bitcast.8), calls=%async_computation | async-start | bytes 1048576
  24.1 108.3 %slice-start.1 = ((s8[4718592]{0:T(1024)(128)(4,1)}), s8[4194304]{0:T(1024)(128)(4,1)S(1)}, s32[]{:S(2)}) async-start(s8[4718592]{0:T(1024)(128)(4,1)} %bitcast.8), calls=%async_computation.1 | async-start | bytes 8388608
  73.7 3.7 %copy-start.9 = (bf16[18,4,128,128]{3,2,1,0:T(8,128)(2,1)}, bf16[18,4,128,128]{3,2,1,0:T(8,128)(2,1)S(1)}, u32[]{:S(2)}) copy-start(bf16[18,4,128,128]{3,2,1,0:T(8,128)(2,1)S(1)} %collective-permute-done.3.refs_2_) | copy-start | bytes 7077892
  77.4 4.9 %collective-permute-start.5 = (bf16[24,128,384]{2,1,0:T(8,128)(2,1)S(1)}, bf16[24,128,384]{2,1,0:T(8,128)(2,1)S(1)}, u32[]{:S(2)}, u32[]{:S(2)}) collective-permute-start(bf16[24,128,384]{2,1,0:T(8,128)(2,1)S(1)} %get-tuple-element.27), channel_id=1, source_target_pairs={{4,8},{5,9},{6,10},{7,11},{8,4},{9,5},{10,6},{11,7},{20,24},{21,25... | collective-permute-start | bytes 7077896 | tf_op jit(solution)/shard_map/ppermute | solution.py:21
  78.3 54.1 %collective-permute-start.4 = (bf16[24,128,384]{2,1,0:T(8,128)(2,1)S(1)}, bf16[24,128,384]{2,1,0:T(8,128)(2,1)}, u32[]{:S(2)}, u32[]{:S(2)}) collective-permute-start(bf16[24,128,384]{2,1,0:T(8,128)(2,1)S(1)} %get-tuple-element.61), channel_id=1, source_target_pairs={{0,4},{1,5},{2,6},{3,7},{4,0},{5,1},{6,2},{7,3},{8,12},{9,13},{10,... | collective-permute-start | bytes 7077896 | tf_op jit(solution)/shard_map/ppermute | solution.py:21
  134.0 51.6 %collective-permute-start.7 = (bf16[24,128,384]{2,1,0:T(8,128)(2,1)}, bf16[24,128,384]{2,1,0:T(8,128)(2,1)}, u32[]{:S(2)}, u32[]{:S(2)}) collective-permute-start(bf16[24,128,384]{2,1,0:T(8,128)(2,1)} %broadcast_select_fusion.1), channel_id=1, source_target_pairs={{0,4},{1,5},{2,6},{3,7},{4,0},{5,1},{6,2},{7,3},{8,12},{9,13},{10,... | collective-permute-start | bytes 7077896 | tf_op jit(solution)/shard_map/ppermute | solution.py:21
  135.8 51.6 %collective-permute-start.6 = (bf16[24,128,384]{2,1,0:T(8,128)(2,1)}, bf16[24,128,384]{2,1,0:T(8,128)(2,1)}, u32[]{:S(2)}, u32[]{:S(2)}) collective-permute-start(bf16[24,128,384]{2,1,0:T(8,128)(2,1)} %collective-permute-done.4), channel_id=1, source_target_pairs={{4,8},{5,9},{6,10},{7,11},{8,4},{9,5},{10,6},{11,7},{20,24},{21,25... | collective-permute-start | bytes 7077896 | tf_op jit(solution)/shard_map/ppermute | solution.py:21
  142.0 4.7 %collective-permute-start = (bf16[12,128,384]{2,1,0:T(8,128)(2,1)}, bf16[12,128,384]{2,1,0:T(8,128)(2,1)S(1)}, u32[]{:S(2)}, u32[]{:S(2)}) collective-permute-start(bf16[12,128,384]{2,1,0:T(8,128)(2,1)} %get-tuple-element.64), channel_id=1, source_target_pairs={{0,1},{1,0},{2,3},{3,2},{4,5},{5,4},{6,7},{7,6},{8,9},{9,8},{10,11... | collective-permute-start | bytes 3538952 | tf_op jit(solution)/shard_map/ppermute | solution.py:21
  142.0 4.9 %collective-permute-start.1 = (bf16[12,128,384]{2,1,0:T(8,128)(2,1)}, bf16[12,128,384]{2,1,0:T(8,128)(2,1)}, u32[]{:S(2)}, u32[]{:S(2)}) collective-permute-start(bf16[12,128,384]{2,1,0:T(8,128)(2,1)} %get-tuple-element.62), channel_id=1, source_target_pairs={{0,1},{1,0},{2,3},{3,2},{4,5},{5,4},{6,7},{7,6},{8,9},{9,8},{10,11... | collective-permute-start | bytes 3538952 | tf_op jit(solution)/shard_map/ppermute | solution.py:21
  146.9 12.7 %copy-start.10 = (bf16[18,4,128,128]{3,2,1,0:T(8,128)(2,1)S(1)}, bf16[18,4,128,128]{3,2,1,0:T(8,128)(2,1)}, u32[]{:S(2)}) copy-start(bf16[18,4,128,128]{3,2,1,0:T(8,128)(2,1)} %copy-done.9) | copy-start | bytes 7077892
  146.9 38.8 %copy-start.16 = (bf16[18,4,128,128]{3,2,1,0:T(8,128)(2,1)S(1)}, bf16[18,4,128,128]{3,2,1,0:T(8,128)(2,1)}, u32[]{:S(2)}) copy-start(bf16[18,4,128,128]{3,2,1,0:T(8,128)(2,1)} %get-tuple-element.35) | copy-start | bytes 7077892
  159.6 51.5 %collective-permute-start.12 = (bf16[18,4,128,128]{3,2,1,0:T(8,128)(2,1)S(1)}, bf16[18,4,128,128]{3,2,1,0:T(8,128)(2,1)S(1)}, u32[]{:S(2)}, u32[]{:S(2)}) collective-permute-start(bf16[18,4,128,128]{3,2,1,0:T(8,128)(2,1)S(1)} %copy-done.10), channel_id=1, source_target_pairs={{0,2},{1,3},{2,0},{3,1},{4,6},{5,7},{6,4},{7,5},{8,10},{9,11},{10,... | collective-permute-start | bytes 7077896 | tf_op jit(solution)/shard_map/ppermute | solution.py:21
  185.6 50.2 %collective-permute-start.14 = (bf16[18,4,128,128]{3,2,1,0:T(8,128)(2,1)S(1)}, bf16[18,4,128,128]{3,2,1,0:T(8,128)(2,1)}, u32[]{:S(2)}, u32[]{:S(2)}) collective-permute-start(bf16[18,4,128,128]{3,2,1,0:T(8,128)(2,1)S(1)} %copy-done.16), channel_id=1, source_target_pairs={{0,4},{1,5},{2,6},{3,7},{4,0},{5,1},{6,2},{7,3},{8,12},{9,13},{10,... | collective-permute-start | bytes 7077896 | tf_op jit(solution)/shard_map/ppermute | solution.py:21
  187.4 54.7 %collective-permute-start.8 = (bf16[24,128,384]{2,1,0:T(8,128)(2,1)}, bf16[24,128,384]{2,1,0:T(8,128)(2,1)S(1)}, u32[]{:S(2)}, u32[]{:S(2)}) collective-permute-start(bf16[24,128,384]{2,1,0:T(8,128)(2,1)} %collective-permute-done.7), channel_id=1, source_target_pairs={{4,8},{5,9},{6,10},{7,11},{8,4},{9,5},{10,6},{11,7},{20,24},{21,25... | collective-permute-start | bytes 7077896 | tf_op jit(solution)/shard_map/ppermute | solution.py:21
  211.1 28.2 %copy-start.12 = (bf16[18,4,128,128]{3,2,1,0:T(8,128)(2,1)}, bf16[18,4,128,128]{3,2,1,0:T(8,128)(2,1)S(1)}, u32[]{:S(2)}) copy-start(bf16[18,4,128,128]{3,2,1,0:T(8,128)(2,1)S(1)} %collective-permute-done.12.refs_3_) | copy-start | bytes 7077892
  235.9 49.5 %collective-permute-start.15 = (bf16[18,4,128,128]{3,2,1,0:T(8,128)(2,1)}, bf16[18,4,128,128]{3,2,1,0:T(8,128)(2,1)}, u32[]{:S(2)}, u32[]{:S(2)}) collective-permute-start(bf16[18,4,128,128]{3,2,1,0:T(8,128)(2,1)} %collective-permute-done.14.refs_2_), channel_id=1, source_target_pairs={{0,2},{1,3},{2,0},{3,1},{4,6},{5,7},{6,4},{7,5},{8,10},{9,11},{10,... | collective-permute-start | bytes 7077896 | tf_op jit(solution)/shard_map/ppermute | solution.py:21
  239.3 68.5 %collective-permute-start.17 = (bf16[24,4,128,128]{3,2,1,0:T(8,128)(2,1)}, bf16[24,4,128,128]{3,2,1,0:T(8,128)(2,1)}, u32[]{:S(2)}, u32[]{:S(2)}) collective-permute-start(bf16[24,4,128,128]{3,2,1,0:T(8,128)(2,1)} %pad_maximum_fusion), channel_id=1, source_target_pairs={{0,4},{1,5},{2,6},{3,7},{4,0},{5,1},{6,2},{7,3},{8,12},{9,13},{10,... | collective-permute-start | bytes 9437192 | tf_op jit(solution)/shard_map/ppermute | solution.py:21
  242.1 5.1 %collective-permute-start.9 = (bf16[12,128,384]{2,1,0:T(8,128)(2,1)}, bf16[12,128,384]{2,1,0:T(8,128)(2,1)}, u32[]{:S(2)}, u32[]{:S(2)}) collective-permute-start(bf16[12,128,384]{2,1,0:T(8,128)(2,1)} %get-tuple-element.68), channel_id=1, source_target_pairs={{0,1},{1,0},{2,3},{3,2},{4,5},{5,4},{6,7},{7,6},{8,9},{9,8},{10,11... | collective-permute-start | bytes 3538952 | tf_op jit(solution)/shard_map/ppermute | solution.py:21
  244.2 7.2 %slice-start.2 = ((s8[4718592]{0:T(1024)(128)(4,1)}), s8[524288]{0:T(1024)(128)(4,1)S(1)}, s32[]{:S(2)}) async-start(s8[4718592]{0:T(1024)(128)(4,1)} %bitcast.10), calls=%async_computation.2 | async-start | bytes 1048576
  245.5 3.3 collective-permute-start.10
  248.8 3.6 %copy-start.11 = (bf16[18,4,128,128]{3,2,1,0:T(8,128)(2,1)S(1)}, bf16[18,4,128,128]{3,2,1,0:T(8,128)(2,1)}, u32[]{:S(2)}) copy-start(bf16[18,4,128,128]{3,2,1,0:T(8,128)(2,1)} %copy-done.9) | copy-start | bytes 7077892
  248.8 4.3 %copy-start.13 = (bf16[18,4,128,128]{3,2,1,0:T(8,128)(2,1)S(1)}, bf16[18,4,128,128]{3,2,1,0:T(8,128)(2,1)}, u32[]{:S(2)}) copy-start(bf16[18,4,128,128]{3,2,1,0:T(8,128)(2,1)} %copy-done.12) | copy-start | bytes 7077892
  253.1 15.4 %copy-start.4 = (bf16[24,128,768]{2,1,0:T(8,128)(2,1)}, bf16[24,128,768]{2,1,0:T(8,128)(2,1)S(1)}, u32[]{:S(2)}) copy-start(bf16[24,128,768]{2,1,0:T(8,128)(2,1)S(1)} %pack.3.far_ref) | copy-start | bytes 14155780
  270.4 59.4 %collective-permute-start.13 = (f32[18,128,384]{2,1,0:T(8,128)}, f32[18,128,384]{2,1,0:T(8,128)}, u32[]{:S(2)}, u32[]{:S(2)}) collective-permute-start(f32[18,128,384]{2,1,0:T(8,128)} %get-tuple-element.33), channel_id=1, source_target_pairs={{0,1},{1,0},{2,3},{3,2},{4,5},{5,4},{6,7},{7,6},{8,9},{9,8},{10,11... | collective-permute-start | bytes 10616840 | tf_op jit(solution)/shard_map/ppermute | solution.py:21
  304.8 30.6 %collective-permute-start.16 = (f32[18,128,384]{2,1,0:T(8,128)}, f32[18,128,384]{2,1,0:T(8,128)}, u32[]{:S(2)}, u32[]{:S(2)}) collective-permute-start(f32[18,128,384]{2,1,0:T(8,128)} %get-tuple-element.38), channel_id=1, source_target_pairs={{0,1},{1,0},{2,3},{3,2},{4,5},{5,4},{6,7},{7,6},{8,9},{9,8},{10,11... | collective-permute-start | bytes 10616840 | tf_op jit(solution)/shard_map/ppermute | solution.py:21
  312.5 12.7 %copy-start.18 = (s32[48,3]{0,1:T(4,128)S(1)}, s32[48,3]{0,1:T(4,128)}, u32[]{:S(2)}) copy-start(s32[48,3]{0,1:T(4,128)} %param.5) | copy-start | bytes 1732
  324.7 14.5 %collective-permute-start.18 = (f32[12,128,384]{2,1,0:T(8,128)}, f32[12,128,384]{2,1,0:T(8,128)}, u32[]{:S(2)}, u32[]{:S(2)}) collective-permute-start(f32[12,128,384]{2,1,0:T(8,128)} %get-tuple-element.43), channel_id=1, source_target_pairs={{0,1},{1,0},{2,3},{3,2},{4,5},{5,4},{6,7},{7,6},{8,9},{9,8},{10,11... | collective-permute-start | bytes 7077896 | tf_op jit(solution)/shard_map/ppermute | solution.py:21
  335.4 3.8 %copy-start.15 = (f32[12,128,384]{2,1,0:T(8,128)S(1)}, f32[12,128,384]{2,1,0:T(8,128)}, u32[]{:S(2)}) copy-start(f32[12,128,384]{2,1,0:T(8,128)} %copy-done.14) | copy-start | bytes 7077892
  341.6 4.7 %collective-permute-start.19 = (f32[8,384]{1,0:T(8,128)S(1)}, f32[8,384]{1,0:T(8,128)S(1)}, u32[]{:S(2)}, u32[]{:S(2)}) collective-permute-start(f32[8,384]{1,0:T(8,128)S(1)} %get-tuple-element.45.sums_ref), channel_id=1, source_target_pairs={{0,8},{1,9},{2,10},{3,11},{4,12},{5,13},{6,14},{7,15},{8,0},{9,1},... | collective-permute-start | bytes 36872 | tf_op jit(solution)/shard_map/ppermute | solution.py:21
  (11 other events, 23.6 us)

commit v4 on v3

--- a/solution.py
+++ b/solution.py
@@ -25,32 +25,49 @@
     return (i ^ i >> 1) & (GC // 2) != 0
 
 
-def panel_kernel(slot_ref, tiles_ref, panel_ref):
+def outer(i):
+    return not inner(i)
+
+
+def panel_kernel(slot_ref, tiles_ref, *panel_refs):
     rows, _, width, _ = tiles_ref.shape
     first = pl.program_id(0) * rows
-
-    @pl.loop(0, rows)
-    def _(r):
-        for p in range(PC):
-            slot = slot_ref[(first + r) * PC + p]
-            tile = tiles_ref[r, jnp.maximum(slot, 0)]
-            panel_ref[r, :, p * width : (p + 1) * width] = jnp.where(
-                slot >= 0, tile, jnp.zeros_like(tile)
-            )
-
-
-def make_panel(tile_values, slots):
+    steps = pl.num_programs(0) // len(panel_refs)
+
+    for n, panel_ref in enumerate(panel_refs):
+
+        @pl.when(pl.program_id(0) // steps == n)
+        def _():
+            @pl.loop(0, rows)
+            def _(r):
+                for p in range(PC):
+                    slot = slot_ref[(first + r) * PC + p]
+                    tile = tiles_ref[r, jnp.maximum(slot, 0)]
+                    panel_ref[r, :, p * width : (p + 1) * width] = jnp.where(
+                        slot >= 0, tile, jnp.zeros_like(tile)
+                    )
+
+
+def make_panel(tile_values, slots, parts):
     block_rows, slots_per_row, width, _ = tile_values.shape
-    step = math.gcd(block_rows, 12)
+    part_rows = block_rows // parts
+    step = math.gcd(part_rows, 12)
+    steps = part_rows // step
+
+    def part_block(n):
+        return pl.BlockSpec(
+            (step, width, PC * width), lambda i, s: (jnp.clip(i - n * steps, 0, steps - 1), 0, 0)
+        )
+
     return pl.pallas_call(
         panel_kernel,
         grid_spec=pltpu.PrefetchScalarGridSpec(
             num_scalar_prefetch=1,
             grid=(block_rows // step,),
             in_specs=[pl.BlockSpec((step, slots_per_row, width, width), lambda i, s: (i, 0, 0, 0))],
-            out_specs=pl.BlockSpec((step, width, PC * width), lambda i, s: (i, 0, 0)),
+            out_specs=[part_block(n) for n in range(parts)],
         ),
-        out_shape=jax.ShapeDtypeStruct((block_rows, width, PC * width), jnp.bfloat16),
+        out_shape=[jax.ShapeDtypeStruct((part_rows, width, PC * width), jnp.bfloat16)] * parts,
         compiler_params=pltpu.CompilerParams(vmem_limit_bytes=12 * MIB),
         cost_estimate=SHORT,
         name="panel",
@@ -97,28 +114,29 @@
     )(where, *mine, *others)
 
 
-def expand_kernel(offsets, order_ref, index_ref, near_ref, far_ref, *refs):
-    tile_refs = refs[:STRIPS]
-    mine_ref, other_ref, tiles, sums, tile_sem, sum_sem = refs[STRIPS:]
+def expand_kernel(first, plan, order_ref, index_ref, near_ref, far_ref, *refs):
+    steps = len(plan)
+    outs, (tiles, sums, tile_sem, sum_sem) = refs[-5 - steps : -4], refs[-4:]
+    mine_ref, other_refs = outs[0], outs[1:]
     _, _, rows, slots, width, _ = tiles.shape
     half = PC * width
-    total_rows = mine_ref.shape[0]
-    steps = total_rows // rows
+    total_rows = steps * rows
 
     def fetch(k):
         return [
             pltpu.make_async_copy(
-                source.at[pl.ds(offset + k * rows, rows)], tiles.at[k % 2, q], tile_sem.at[k % 2, q]
+                refs[source].at[pl.ds(offset, rows)], tiles.at[k % 2, q], tile_sem.at[k % 2, q]
             )
-            for q, (source, offset) in enumerate(zip(tile_refs, offsets))
+            for q, (source, offset) in enumerate(plan[k])
         ]
 
-    def stores(row, slot):
+    def stores(k, r, slot):
+        targets = (mine_ref.at[k * rows + r], other_refs[k].at[r])
         return [
             pltpu.make_async_copy(
-                sums.at[slot, :, pl.ds(side * half, half)], out.at[row], sum_sem.at[slot, side]
+                sums.at[slot, :, pl.ds(side * half, half)], target, sum_sem.at[slot, side]
             )
-            for side, out in enumerate((mine_ref, other_ref))
+            for side, target in enumerate(targets)
         ]
 
     for copy in fetch(0):
@@ -137,7 +155,7 @@
 
             @pl.when(row >= 2)
             def _():
-                for copy in stores(row - 2, slot):
+                for copy in stores(k, r, slot):
                     copy.wait()
 
             total = None
@@ -145,7 +163,7 @@
                 panel = near_ref if n < STRIPS // 2 else far_ref
                 q = order_ref[n]
                 for t in range(0, slots, 2):
-                    base = row * (STRIPS * slots) + n * slots + t
+                    base = (first + row) * (STRIPS * slots) + n * slots + t
                     left = jnp.concatenate(
                         [tiles[k % 2, q, r, t], tiles[k % 2, q, r, t + 1]], axis=1
                     )
@@ -155,78 +173,89 @@
                     term = jnp.dot(left, right, preferred_element_type=jnp.float32)
                     total = term if total is None else total + term
             sums[slot] = total
-            for copy in stores(row, slot):
+            for copy in stores(k, r, slot):
                 copy.start()
 
     for row in range(max(total_rows - 2, 0), total_rows):
-        for copy in stores(row, row % 2):
+        for copy in stores(row // rows, row % rows, row % 2):
             copy.wait()
 
 
-def expand(sources, order, index, near, far):
-    arrays, offsets = zip(*sources)
+def expand(rows, first, pieces, order, index, near, far):
+    arrays = []
+    plan = []
+    for piece in pieces:
+        for array, _ in piece:
+            if all(array is not a for a in arrays):
+                arrays.append(array)
+        plan.append([([array is a for a in arrays].index(True), row) for array, row in piece])
     _, slots, width, _ = arrays[0].shape
-    total_rows = index.shape[0]
-    rows = math.gcd(total_rows, 6)
-    half = jax.ShapeDtypeStruct((total_rows, width, PC * width), jnp.float32)
+    half = PC * width
     anywhere = pl.BlockSpec(memory_space=pl.ANY)
     smem = pl.BlockSpec(memory_space=pltpu.SMEM)
     vmem = pl.BlockSpec(memory_space=pltpu.VMEM)
-    return pl.pallas_call(
-        functools.partial(expand_kernel, offsets),
-        out_shape=(half, half),
-        in_specs=[smem, smem, vmem, vmem] + [anywhere] * STRIPS,
-        out_specs=(anywhere, anywhere),
+    out = pl.pallas_call(
+        functools.partial(expand_kernel, first, plan),
+        out_shape=[jax.ShapeDtypeStruct((len(plan) * rows, width, half), jnp.float32)]
+        + [jax.ShapeDtypeStruct((rows, width, half), jnp.float32)] * len(plan),
+        in_specs=[smem, smem, vmem, vmem] + [anywhere] * len(arrays),
+        out_specs=[anywhere] * (1 + len(plan)),
         scratch_shapes=[
             pltpu.VMEM((2, STRIPS, rows, slots, width, width), jnp.bfloat16),
-            pltpu.VMEM((2, width, 2 * PC * width), jnp.float32),
+            pltpu.VMEM((2, width, 2 * half), jnp.float32),
             pltpu.SemaphoreType.DMA((2, STRIPS)),
             pltpu.SemaphoreType.DMA((2, 2)),
         ],
         compiler_params=pltpu.CompilerParams(vmem_limit_bytes=12 * MIB),
         cost_estimate=SHORT,
         name="expand",
-    )(order, index.reshape(-1), near, far, *arrays)
-
-
-def square_kernel(keep_ref, before_ref, mine_ref, got_ref, *refs):
-    squared_ref, sums_ref = refs[-2:]
+    )(order, index, near, far, *arrays)
+    return out[0], out[1:]
+
+
+def square_kernel(lo, pieces, keep_ref, before_ref, mine_ref, *refs):
+    got_refs, (squared_ref, sums_ref) = refs[:pieces], refs[-2:]
     rows, width, _ = mine_ref.shape
-    first = pl.program_id(0) * rows
+    first = lo + pl.program_id(0) * rows
 
     @pl.when(pl.program_id(0) == 0)
     def _():
         sums_ref[...] = before_ref[...]
 
-    @pl.loop(0, rows)
-    def _(r):
-        for p in range(PC):
-            keep = keep_ref[(first + r) * PC + p].astype(jnp.float32)
-            cols = slice(p * width, (p + 1) * width)
-            value = mine_ref[r, :, cols] + got_ref[r, :, cols]
-            value = value * value * keep
-            squared_ref[r, :, cols] = value
-            sums_ref[:, cols] += jnp.sum(value.reshape(width // 8, 8, width), axis=0)
+    for n, got_ref in enumerate(got_refs):
+
+        @pl.when(pl.program_id(0) == n)
+        def _():
+            @pl.loop(0, rows)
+            def _(r):
+                for p in range(PC):
+                    keep = keep_ref[(first + r) * PC + p].astype(jnp.float32)
+                    cols = slice(p * width, (p + 1) * width)
+                    value = mine_ref[r, :, cols] + got_ref[r, :, cols]
+                    value = value * value * keep
+                    squared_ref[r, :, cols] = value
+                    sums_ref[:, cols] += jnp.sum(value.reshape(width // 8, 8, width), axis=0)
 
 
 def square(keep, before, mine, got, lo, total_rows, buffer):
-    rows, width, half = mine.shape
-    step = math.gcd(math.gcd(rows, 6), lo) if lo else math.gcd(rows, 6)
+    _, width, half = mine.shape
+    step = got[0].shape[0]
     block = pl.BlockSpec((step, width, half), lambda i, s: (i, 0, 0))
+    whole = pl.BlockSpec((step, width, half), lambda i, s: (0, 0, 0))
     target = pl.BlockSpec((step, width, half), lambda i, s: (lo // step + i, 0, 0))
     sums = pl.BlockSpec((8, half), lambda i, s: (0, 0))
-    operands = [keep.reshape(-1), before, mine, got]
-    in_specs = [sums, block, block]
+    operands = [keep, before, mine, *got]
+    in_specs = [sums, block] + [whole] * len(got)
     aliases = {}
     if buffer is not None:
         operands.append(buffer)
         in_specs.append(pl.BlockSpec(memory_space=pl.ANY))
         aliases = {len(operands) - 1: 0}
     return pl.pallas_call(
-        square_kernel,
+        functools.partial(square_kernel, lo, len(got)),
         grid_spec=pltpu.PrefetchScalarGridSpec(
             num_scalar_prefetch=1,
-            grid=(rows // step,),
+            grid=(len(got),),
             in_specs=in_specs,
             out_specs=(target, sums),
         ),
@@ -235,7 +264,7 @@
             jax.ShapeDtypeStruct((8, half), jnp.float32),
         ),
         input_output_aliases=aliases,
-        compiler_params=pltpu.CompilerParams(vmem_limit_bytes=12 * MIB),
+        compiler_params=pltpu.CompilerParams(vmem_limit_bytes=16 * MIB),
         cost_estimate=SHORT,
         name="square",
     )(*operands)
@@ -295,7 +324,8 @@
     )
     index = jnp.take(strip_rows, strips, axis=1)
     index = index + CB * (jnp.arange(STRIPS, dtype=jnp.int32) % pair)[None, :, None]
-    index = index.reshape(block_rows, STRIPS * slots)
+    index = index.reshape(-1)
+    keep = keep_tiles.reshape(-1)
     relayed = grid_rows == 2 and block_rows == 2 * pair * CB
     unit = math.gcd(CB, block_rows)
     unit_rows = strips[:, None] * CB + unit * jnp.arange(CB // unit, dtype=jnp.int32)
@@ -313,54 +343,66 @@
         given = [jnp.where(odd, a, b) for a, b in zip(pieces[::2], pieces[1::2])]
         return kept, [swapped(p, 1) for p in given]
 
-    cuts = [0, 3 * block_rows // 8, 2 * (3 * block_rows // 8), block_rows]
-    parts = list(zip(cuts[:-1], cuts[1:]))
-    own = [tile_values[lo:hi] for lo, hi in parts]
-    panel = make_panel(tile_values, slot)
+    rows = math.gcd(block_rows // 8, 6) if block_rows >= 8 else 1
+    one, two = 3 * block_rows // 8, 2 * (3 * block_rows // 8)
+    few = one // 3 if one >= 3 else one
     from_x = swapped(tile_values, 2)
-    from_z = [swapped(own[0], 4)]
+    own = tile_values[:one]
+    from_z = [swapped(own, 4)]
+    panel = make_panel(after(tile_values, own), slot, 2 if relayed else 1)
     if relayed:
-        step = block_rows // 2
+        across = GC + GC // 2
+        near = pack(where, 0, *shared(panel))
+        crossed = [swapped(panel[0], across, inner)]
+        crossed.append(swapped(after(panel[1], crossed[0]), across, inner))
+        inward, outward = [], []
+        for got, piece in zip(crossed, panel):
+            ready = from_z + inward + outward
+            inward.append(swapped(after(piece, *ready), 4, outer))
+            outward.append(swapped(after(got, *ready), 4, inner))
+        returned = [swapped(after(inward[0], crossed[1]), across, inner)]
+        returned.append(swapped(after(inward[1], returned[0]), across, inner))
         is_inner = inner(device)
-        pieces = [panel[:step], panel[step:]]
-        near = pack(where, 0, *shared(pieces))
-        across = GC + GC // 2
-        crossed = [swapped(pieces[0], across, inner)]
-        crossed.append(swapped(after(pieces[1], crossed[0]), across, inner))
-        passed = []
-        for got, piece in zip(crossed, pieces):
-            got = after(got, *(passed or from_z))
-            passed.append(swapped(jnp.where(is_inner, got, piece), 4))
-        returned = [swapped(after(passed[0], crossed[1]), across, inner)]
-        returned.append(swapped(after(passed[1], returned[0]), across, inner))
-        far = [jnp.where(is_inner, a, b) for a, b in zip(returned, passed)]
+        far = [jnp.where(is_inner, a, b) for a, b in zip(returned, outward)]
         far = pack(where, half // 2, *shared(far))
-        own[1] = after(own[1], passed[1], near)
+        tied = inward[1], outward[1], near
     else:
-        panels = [panel]
+        panels = list(panel)
         for bit in range(low_bits, all_bits):
             panels = panels + [swapped(p, 1 << bit) for p in panels]
         others = [swapped(p, 1) for p in panels]
         near = pack(where, 0, panels, others)
         far = pack(where, half // 2, panels, others)
-    from_xz = [swapped(after(from_z[0], from_x), 2)]
-    from_z.append(swapped(own[1], 4))
-    last = jnp.concatenate([from_x[cuts[2] :], own[2]])
-    last = swapped(after(last, from_z[1], from_xz[0]), 4)
-    from_xz.append(swapped(after(from_z[1], from_xz[0]), 2))
+        tied = (near,)
+    from_xz = [swapped(after(from_z[0][:few], from_x), 2)]
+    if few < one:
+        from_xz.append(swapped(after(from_z[0][few:], from_xz[0]), 2))
+    later = after(tile_values, *tied, from_xz[0])
+    from_z.append(swapped(later[one:two], 4))
+    last = jnp.concatenate([from_x[two:], later[two:]])
+    last = swapped(after(last, from_z[1], from_xz[-1]), 4)
+    from_xz.append(swapped(after(from_z[1], from_xz[-1]), 2))
+
+    def tiles_at(row):
+        if row >= two:
+            far_tiles = [(last, row - two + block_rows - two), (last, row - two)]
+        elif row >= one:
+            far_tiles = [(from_z[1], row - one), (from_xz[-1], row - one)]
+        else:
+            first = row < few
+            far_tiles = [(from_z[0], row), (from_xz[0 if first else 1], row if first else row - few)]
+        return [(tile_values, row), (from_x, row)] + far_tiles
 
     squared = None
+    totals = []
     sums = jnp.zeros((8, PC * width), jnp.float32)
-    for n, (lo, hi) in enumerate(parts):
-        if n < 2:
-            received = [(from_z[n], 0), (from_xz[n], 0)]
-        else:
-            received = [(last, hi - lo), (last, 0)]
-        mine, other = expand(
-            [(tile_values, lo), (from_x, lo)] + received, order, index[lo:hi], near, far
-        )
-        got = swapped(other, 1)
-        squared, sums = square(keep_tiles[lo:hi], sums, mine, got, lo, block_rows, squared)
+    for lo, hi in ((0, one), (one, two), (two, block_rows)):
+        table = after(index, totals[0], got[0]) if len(totals) == 2 else index
+        pieces = [tiles_at(row) for row in range(lo, hi, rows)]
+        mine, other = expand(rows, lo, pieces, order, table, near, far)
+        got = [swapped(a, 1) for a in other]
+        squared, sums = square(keep, sums, mine, got, lo, block_rows, squared)
+        totals.append(sums)
     for bit in range(low_bits, all_bits - 1):
         sums = sums + swapped(sums, 1 << bit)
     got = swapped(sums, 1 << (all_bits - 1))

time: 352 us -> 342 us (0.972)
  starting transfers between devices: 28 us -> 41.1 us
  Pallas kernels: 65.6 us -> 58.3 us
  other arithmetic: 19 us -> 11.8 us
  waiting for transfers between devices: 197 us -> 190 us
    ppermute x20 -> x28, starting transfers between devices: 28 us -> 41.1 us  [swapped(): return lax.ppermute(array, 'grid', pairs)]
    ppermute x20 -> x28, waiting for transfers between devices: 197 us -> 190 us  [swapped(): return lax.ppermute(array, 'grid', pairs)]
    unnamed x46 -> x65, local copies, waits for them, and re-layouts: 20.6 us -> 26.8 us
    pallas_call x6, Pallas kernels: 50.7 us -> 45.6 us  [the longest x3 39.9 us: expand(): pl.pallas_call(functools.partial(expand_kernel, first, plan), out_shape=[...]
    slice x1 -> x0, other arithmetic: 3.69 us -> none  [shards(): pieces = [panel[:step], panel[step:]]]
    slice x14 -> x6, local copies, waits for them, and re-layouts: 15.8 us -> 12.2 us  [the longest x1 3.46 us: shards(): own = tile_values[:one]]
  transfers between devices with their start and end apart: 20 -> 28, of which waited for: 11 -> 13; matrix products, arithmetic and copies ran while one was open for 10% -> 7% of each run, Pallas kernels for 15% -> 15%
where the time goes in v4:
time: 342 us
  waiting for transfers between devices  190 us (56%)
  Pallas kernels  58.3 us (17%)
  starting transfers between devices  41.1 us (12%)
  local copies, waits for them, and re-layouts  40.3 us (12%)
  other arithmetic  11.8 us (3%)
    ppermute x28, waiting for transfers between devices, swapped(): return lax.ppermute(array, 'grid', pairs)  190 us
    ppermute x28, starting transfers between devices, swapped(): return lax.ppermute(array, 'grid', pairs)  41.1 us
    pallas_call x3, Pallas kernels, expand(): pl.pallas_call(functools.partial(expand_kernel, first, plan), out_shape=[...  39.9 us
    unnamed x65, local copies, waits for them, and re-layouts  26.8 us
  transfers between devices with their start and end apart: 28, of which 13 were waited for; matrix products, arithmetic and copies ran while one was open for 7% of the time, Pallas kernels for 15%

profile of v4, /device:TPU:0, one launch (start us, length us, event | category | flops | bytes accessed | tf_op | source)
XLA Modules:
  0.0 341.6 jit_solution(3608195328696614360)
XLA Ops:
  0.0 2.9 collective-permute-start.13
  2.9 3.5 %slice.42 = bf16[18,4,128,128]{3,2,1,0:T(8,128)(2,1)} slice(bf16[48,4,128,128]{3,2,1,0:T(8,128)(2,1)} %refs_0_.5), slice={[0:18], [0:4], [0:128], [0:128]} | slice | bytes 4718592 | tf_op jit(solution)/shard_map/slice | solution.py:350
  7.4 2.8 copy-done
  10.2 3.3 panel.1
  14.3 4.3 %collective-permute-start.2 = (bf16[18,4,128,128]{3,2,1,0:T(8,128)(2,1)S(1)}, bf16[18,4,128,128]{3,2,1,0:T(8,128)(2,1)S(1)}, u32[]{:S(2)}, u32[]{:S(2)}) collective-permute-start(bf16[18,4,128,128]{3,2,1,0:T(8,128)(2,1)S(1)} %copy-done.25), channel_id=1, source_target_pairs={{0,4},{1,5},{2,6},{3,7},{4,0},{5,1},{6,2},{7,3},{8,12},{9,13},{10,... | collective-permute-start | bytes 7077896 | tf_op jit(solution)/shard_map/ppermute | solution.py:21
  18.7 2.1 collective-permute-start.5
  20.8 48.6 %collective-permute-done.2.refs_2_ = bf16[18,4,128,128]{3,2,1,0:T(8,128)(2,1)S(1)} collective-permute-done((bf16[18,4,128,128]{3,2,1,0:T(8,128)(2,1)S(1)}, bf16[18,4,128,128]{3,2,1,0:T(8,128)(2,1)S(1)}, u32[]{:S(2)}, u32[]{:S(2)}) %collective-permute-start.2) | collective-permute-done | bytes 2359328 | tf_op jit(solution)/shard_map/ppermute | solution.py:21
  70.6 7.3 %collective-permute-start.3 = (bf16[24,128,384]{2,1,0:T(8,128)(2,1)S(1)}, bf16[24,128,384]{2,1,0:T(8,128)(2,1)}, u32[]{:S(2)}, u32[]{:S(2)}) collective-permute-start(bf16[24,128,384]{2,1,0:T(8,128)(2,1)S(1)} %get-tuple-element.41), channel_id=1, source_target_pairs={{0,4},{1,5},{2,6},{3,7},{12,8},{13,9},{14,10},{15,11},{16,20},{17,... | collective-permute-start | bytes 7077896 | tf_op jit(solution)/shard_map/ppermute | solution.py:21
  78.0 46.4 %collective-permute-done.7 = bf16[24,128,384]{2,1,0:T(8,128)(2,1)S(1)} collective-permute-done((bf16[24,128,384]{2,1,0:T(8,128)(2,1)S(1)}, bf16[24,128,384]{2,1,0:T(8,128)(2,1)S(1)}, u32[]{:S(2)}, u32[]{:S(2)}) %collective-permute-start.7) | collective-permute-done | bytes 2359328 | tf_op jit(solution)/shard_map/ppermute | solution.py:21
  127.0 7.4 %collective-permute-start.8 = (bf16[24,128,384]{2,1,0:T(8,128)(2,1)}, bf16[24,128,384]{2,1,0:T(8,128)(2,1)}, u32[]{:S(2)}, u32[]{:S(2)}) collective-permute-start(bf16[24,128,384]{2,1,0:T(8,128)(2,1)} %get-tuple-element.42), channel_id=1, source_target_pairs={{0,4},{1,5},{2,6},{3,7},{12,8},{13,9},{14,10},{15,11},{16,20},{17,... | collective-permute-start | bytes 7077896 | tf_op jit(solution)/shard_map/ppermute | solution.py:21
  134.5 2.1 collective-permute-start.6
  148.4 2.2 copy-done.2
  150.5 28.5 %collective-permute-done.10 = bf16[24,128,384]{2,1,0:T(8,128)(2,1)} collective-permute-done((bf16[24,128,384]{2,1,0:T(8,128)(2,1)}, bf16[24,128,384]{2,1,0:T(8,128)(2,1)}, u32[]{:S(2)}, u32[]{:S(2)}) %collective-permute-start.10) | collective-permute-done | bytes 2359328 | tf_op jit(solution)/shard_map/ppermute | solution.py:21
  179.0 2.6 collective-permute-done.8
  181.6 3.3 slice.53
  184.9 2.5 collective-permute-start.19
  187.4 2.0 collective-permute-start.9
  196.4 27.3 %collective-permute-done.15.refs_4_ = bf16[12,4,128,128]{3,2,1,0:T(8,128)(2,1)S(1)} collective-permute-done((bf16[12,4,128,128]{3,2,1,0:T(8,128)(2,1)}, bf16[12,4,128,128]{3,2,1,0:T(8,128)(2,1)S(1)}, u32[]{:S(2)}, u32[]{:S(2)}) %collective-permute-start.15) | collective-permute-done | bytes 1572896 | tf_op jit(solution)/shard_map/ppermute | solution.py:21
  223.7 13.0 %collective-permute-done.19.refs_2_ = bf16[18,4,128,128]{3,2,1,0:T(8,128)(2,1)} collective-permute-done((bf16[18,4,128,128]{3,2,1,0:T(8,128)(2,1)}, bf16[18,4,128,128]{3,2,1,0:T(8,128)(2,1)}, u32[]{:S(2)}, u32[]{:S(2)}) %collective-permute-start.19) | collective-permute-done | bytes 2359328 | tf_op jit(solution)/shard_map/ppermute | solution.py:21
  236.8 2.0 collective-permute-start.24
  239.3 2.2 broadcast_select_fusion
  249.0 2.6 pack.3.far_ref
  253.1 2.3 copy-done.3
  255.4 15.5 %expand.3 = (f32[18,128,384]{2,1,0:T(8,128)S(1)}, f32[6,128,384]{2,1,0:T(8,128)}, f32[6,128,384]{2,1,0:T(8,128)}, f32[6,128,384]{2,1,0:T(8,128)}) custom-call(s32[4]{0:T(128)S(1)} %iota_xor_fusion.order_ref, s32[768]{0:T(1024)S(1)} %add.104.index_ref, bf16[24,128,768]{2,1,0:T(8,128)(2,1)S(1)} %copy-done.3, bf16[24,128,768]{2,1,0:T(8,128)(2,1)S(1)} %pack.3.far_ref, ...), custom_call_target="tpu_custom_call" | custom-call | bytes 1024 | tf_op jit(solution)/shard_map/expand/pallas_call | solution.py:197
  273.6 13.0 %collective-permute-done.20.refs_3_ = bf16[18,4,128,128]{3,2,1,0:T(8,128)(2,1)} collective-permute-done((bf16[18,4,128,128]{3,2,1,0:T(8,128)(2,1)}, bf16[18,4,128,128]{3,2,1,0:T(8,128)(2,1)}, u32[]{:S(2)}, u32[]{:S(2)}) %collective-permute-start.20) | collective-permute-done | bytes 2359328 | tf_op jit(solution)/shard_map/ppermute | solution.py:21
  286.6 13.8 %expand.4 = (f32[18,128,384]{2,1,0:T(8,128)S(1)}, f32[6,128,384]{2,1,0:T(8,128)}, f32[6,128,384]{2,1,0:T(8,128)S(1)}, f32[6,128,384]{2,1,0:T(8,128)S(1)}) custom-call(s32[4]{0:T(128)S(1)} %iota_xor_fusion.order_ref, s32[768]{0:T(1024)S(1)} %add.104.index_ref, bf16[24,128,768]{2,1,0:T(8,128)(2,1)S(1)} %copy-done.3, bf16[24,128,768]{2,1,0:T(8,128)(2,1)S(1)} %pack.3.far_ref, ...), custom_call_target="tpu_custom_call" | custom-call | bytes 1024 | tf_op jit(solution)/shard_map/expand/pallas_call | solution.py:197
  306.6 3.3 square.3
  310.6 2.8 copy-done.1
  313.4 2.3 copy-done.4
  315.7 10.6 %expand.5 = (f32[12,128,384]{2,1,0:T(8,128)S(1)}, f32[6,128,384]{2,1,0:T(8,128)S(1)}, f32[6,128,384]{2,1,0:T(8,128)S(1)}) custom-call(s32[4]{0:T(128)S(1)} %iota_xor_fusion.order_ref, s32[768]{0:T(1024)S(1)} %add.104.index_ref, bf16[24,128,768]{2,1,0:T(8,128)(2,1)S(1)} %copy-done.4, bf16[24,128,768]{2,1,0:T(8,128)(2,1)S(1)} %copy-done.6, ...), custom_call_target="tpu_custom_call" | custom-call | bytes 1024 | tf_op jit(solution)/shard_map/expand/pallas_call | solution.py:197
  332.6 4.3 %collective-permute-done.27.got_ref = f32[8,384]{1,0:T(8,128)S(1)} collective-permute-done((f32[8,384]{1,0:T(8,128)S(1)}, f32[8,384]{1,0:T(8,128)S(1)}, u32[]{:S(2)}, u32[]{:S(2)}) %collective-permute-start.27) | collective-permute-done | bytes 12320 | tf_op jit(solution)/shard_map/ppermute | solution.py:21
  336.8 4.8 %scale.1 = f32[48,3,128,128]{3,2,1,0:T(8,128)} custom-call(f32[8,384]{1,0:T(8,128)S(1)} %get-tuple-element.69.sums_ref, f32[8,384]{1,0:T(8,128)S(1)} %collective-permute-done.27.got_ref, f32[48,128,384]{2,1,0:T(8,128)S(1)} %get-tuple-element.70.squared_ref), custom_call_target="tpu_custom_call" | custom-call | bytes 1024 | tf_op jit(solution)/shard_map/scale/pallas_call | solution.py:286
  (131 shorter events, 49.6 us)
Async XLA Ops:
  0.0 140.6 %collective-permute-start.13 = (bf16[48,4,128,128]{3,2,1,0:T(8,128)(2,1)}, bf16[48,4,128,128]{3,2,1,0:T(8,128)(2,1)}, u32[]{:S(2)}, u32[]{:S(2)}) collective-permute-start(bf16[48,4,128,128]{3,2,1,0:T(8,128)(2,1)} %refs_0_.5), channel_id=1, source_target_pairs={{0,2},{1,3},{2,0},{3,1},{4,6},{5,7},{6,4},{7,5},{8,10},{9,11},{10,... | collective-permute-start | bytes 18874376 | tf_op jit(solution)/shard_map/ppermute | solution.py:21
  13.5 57.1 %copy-start.15 = (bf16[24,128,384]{2,1,0:T(8,128)(2,1)}, bf16[24,128,384]{2,1,0:T(8,128)(2,1)S(1)}, u32[]{:S(2)}) copy-start(bf16[24,128,384]{2,1,0:T(8,128)(2,1)S(1)} %get-tuple-element.41) | copy-start | bytes 7077892
  13.5 5.1 %collective-permute-start.4 = (bf16[24,128,384]{2,1,0:T(8,128)(2,1)S(1)}, bf16[24,128,384]{2,1,0:T(8,128)(2,1)S(1)}, u32[]{:S(2)}, u32[]{:S(2)}) collective-permute-start(bf16[24,128,384]{2,1,0:T(8,128)(2,1)S(1)} %get-tuple-element.41), channel_id=1, source_target_pairs={{4,8},{5,9},{6,10},{7,11},{8,4},{9,5},{10,6},{11,7},{20,24},{21,25... | collective-permute-start | bytes 7077896 | tf_op jit(solution)/shard_map/ppermute | solution.py:21
  14.3 55.0 %collective-permute-start.2 = (bf16[18,4,128,128]{3,2,1,0:T(8,128)(2,1)S(1)}, bf16[18,4,128,128]{3,2,1,0:T(8,128)(2,1)S(1)}, u32[]{:S(2)}, u32[]{:S(2)}) collective-permute-start(bf16[18,4,128,128]{3,2,1,0:T(8,128)(2,1)S(1)} %copy-done.25), channel_id=1, source_target_pairs={{0,4},{1,5},{2,6},{3,7},{4,0},{5,1},{6,2},{7,3},{8,12},{9,13},{10,... | collective-permute-start | bytes 7077896 | tf_op jit(solution)/shard_map/ppermute | solution.py:21
  18.7 59.3 %collective-permute-start.5 = (bf16[24,128,384]{2,1,0:T(8,128)(2,1)}, bf16[24,128,384]{2,1,0:T(8,128)(2,1)}, u32[]{:S(2)}, u32[]{:S(2)}) collective-permute-start(bf16[24,128,384]{2,1,0:T(8,128)(2,1)} %get-tuple-element.42), channel_id=1, source_target_pairs={{4,8},{5,9},{6,10},{7,11},{8,4},{9,5},{10,6},{11,7},{20,24},{21,25... | collective-permute-start | bytes 7077896 | tf_op jit(solution)/shard_map/ppermute | solution.py:21
  69.3 120.1 %copy-start.7 = (bf16[18,4,128,128]{3,2,1,0:T(8,128)(2,1)}, bf16[18,4,128,128]{3,2,1,0:T(8,128)(2,1)S(1)}, u32[]{:S(2)}) copy-start(bf16[18,4,128,128]{3,2,1,0:T(8,128)(2,1)S(1)} %collective-permute-done.2.refs_2_) | copy-start | bytes 7077892
  69.3 55.0 %collective-permute-start.7 = (bf16[24,128,384]{2,1,0:T(8,128)(2,1)S(1)}, bf16[24,128,384]{2,1,0:T(8,128)(2,1)S(1)}, u32[]{:S(2)}, u32[]{:S(2)}) collective-permute-start(bf16[24,128,384]{2,1,0:T(8,128)(2,1)S(1)} %collective-permute-done.4), channel_id=1, source_target_pairs={{4,0},{5,1},{6,2},{7,3},{8,12},{9,13},{10,14},{11,15},{20,16},{21,... | collective-permute-start | bytes 7077896 | tf_op jit(solution)/shard_map/ppermute | solution.py:21
  70.6 55.0 %collective-permute-start.3 = (bf16[24,128,384]{2,1,0:T(8,128)(2,1)S(1)}, bf16[24,128,384]{2,1,0:T(8,128)(2,1)}, u32[]{:S(2)}, u32[]{:S(2)}) collective-permute-start(bf16[24,128,384]{2,1,0:T(8,128)(2,1)S(1)} %get-tuple-element.41), channel_id=1, source_target_pairs={{0,4},{1,5},{2,6},{3,7},{12,8},{13,9},{14,10},{15,11},{16,20},{17,... | collective-permute-start | bytes 7077896 | tf_op jit(solution)/shard_map/ppermute | solution.py:21
  125.7 53.3 %collective-permute-start.10 = (bf16[24,128,384]{2,1,0:T(8,128)(2,1)}, bf16[24,128,384]{2,1,0:T(8,128)(2,1)}, u32[]{:S(2)}, u32[]{:S(2)}) collective-permute-start(bf16[24,128,384]{2,1,0:T(8,128)(2,1)} %collective-permute-done.5), channel_id=1, source_target_pairs={{4,0},{5,1},{6,2},{7,3},{8,12},{9,13},{10,14},{11,15},{20,16},{21,... | collective-permute-start | bytes 7077896 | tf_op jit(solution)/shard_map/ppermute | solution.py:21
  127.0 54.6 %collective-permute-start.8 = (bf16[24,128,384]{2,1,0:T(8,128)(2,1)}, bf16[24,128,384]{2,1,0:T(8,128)(2,1)}, u32[]{:S(2)}, u32[]{:S(2)}) collective-permute-start(bf16[24,128,384]{2,1,0:T(8,128)(2,1)} %get-tuple-element.42), channel_id=1, source_target_pairs={{0,4},{1,5},{2,6},{3,7},{12,8},{13,9},{14,10},{15,11},{16,20},{17,... | collective-permute-start | bytes 7077896 | tf_op jit(solution)/shard_map/ppermute | solution.py:21
  134.5 52.9 %collective-permute-start.6 = (bf16[24,128,384]{2,1,0:T(8,128)(2,1)}, bf16[24,128,384]{2,1,0:T(8,128)(2,1)}, u32[]{:S(2)}, u32[]{:S(2)}) collective-permute-start(bf16[24,128,384]{2,1,0:T(8,128)(2,1)} %collective-permute-done.3), channel_id=1, source_target_pairs={{4,8},{5,9},{6,10},{7,11},{8,4},{9,5},{10,6},{11,7},{20,24},{21,25... | collective-permute-start | bytes 7077896 | tf_op jit(solution)/shard_map/ppermute | solution.py:21
  138.5 3.3 collective-permute-start.1
  140.6 3.2 collective-permute-start
  142.8 38.8 %collective-permute-start.14 = (bf16[6,4,128,128]{3,2,1,0:T(8,128)(2,1)}, bf16[6,4,128,128]{3,2,1,0:T(8,128)(2,1)}, u32[]{:S(2)}, u32[]{:S(2)}) collective-permute-start(bf16[6,4,128,128]{3,2,1,0:T(8,128)(2,1)} %slice.71), channel_id=1, source_target_pairs={{0,2},{1,3},{2,0},{3,1},{4,6},{5,7},{6,4},{7,5},{8,10},{9,11},{10,... | collective-permute-start | bytes 2359304 | tf_op jit(solution)/shard_map/ppermute | solution.py:21
  184.9 51.9 %collective-permute-start.19 = (bf16[18,4,128,128]{3,2,1,0:T(8,128)(2,1)}, bf16[18,4,128,128]{3,2,1,0:T(8,128)(2,1)}, u32[]{:S(2)}, u32[]{:S(2)}) collective-permute-start(bf16[18,4,128,128]{3,2,1,0:T(8,128)(2,1)} %slice.53), channel_id=1, source_target_pairs={{0,4},{1,5},{2,6},{3,7},{4,0},{5,1},{6,2},{7,3},{8,12},{9,13},{10,... | collective-permute-start | bytes 7077896 | tf_op jit(solution)/shard_map/ppermute | solution.py:21
  187.4 51.9 %collective-permute-start.9 = (bf16[24,128,384]{2,1,0:T(8,128)(2,1)}, bf16[24,128,384]{2,1,0:T(8,128)(2,1)}, u32[]{:S(2)}, u32[]{:S(2)}) collective-permute-start(bf16[24,128,384]{2,1,0:T(8,128)(2,1)} %collective-permute-done.8), channel_id=1, source_target_pairs={{4,8},{5,9},{6,10},{7,11},{8,4},{9,5},{10,6},{11,7},{20,24},{21,25... | collective-permute-start | bytes 7077896 | tf_op jit(solution)/shard_map/ppermute | solution.py:21
  190.8 33.0 %collective-permute-start.15 = (bf16[12,4,128,128]{3,2,1,0:T(8,128)(2,1)}, bf16[12,4,128,128]{3,2,1,0:T(8,128)(2,1)S(1)}, u32[]{:S(2)}, u32[]{:S(2)}) collective-permute-start(bf16[12,4,128,128]{3,2,1,0:T(8,128)(2,1)} %slice.72), channel_id=1, source_target_pairs={{0,2},{1,3},{2,0},{3,1},{4,6},{5,7},{6,4},{7,5},{8,10},{9,11},{10,... | collective-permute-start | bytes 4718600 | tf_op jit(solution)/shard_map/ppermute | solution.py:21
  194.4 44.9 %copy-start.27 = (bf16[24,128,384]{2,1,0:T(8,128)(2,1)S(1)}, bf16[24,128,384]{2,1,0:T(8,128)(2,1)}, u32[]{:S(2)}) copy-start(bf16[24,128,384]{2,1,0:T(8,128)(2,1)} %copy-done.26) | copy-start | bytes 7077892
  236.8 73.8 %collective-permute-start.24 = (bf16[24,4,128,128]{3,2,1,0:T(8,128)(2,1)}, bf16[24,4,128,128]{3,2,1,0:T(8,128)(2,1)}, u32[]{:S(2)}, u32[]{:S(2)}) collective-permute-start(bf16[24,4,128,128]{3,2,1,0:T(8,128)(2,1)} %pad_maximum_fusion), channel_id=1, source_target_pairs={{0,4},{1,5},{2,6},{3,7},{4,0},{5,1},{6,2},{7,3},{8,12},{9,13},{10,... | collective-permute-start | bytes 9437192 | tf_op jit(solution)/shard_map/ppermute | solution.py:21
  238.8 47.8 %collective-permute-start.20 = (bf16[18,4,128,128]{3,2,1,0:T(8,128)(2,1)}, bf16[18,4,128,128]{3,2,1,0:T(8,128)(2,1)}, u32[]{:S(2)}, u32[]{:S(2)}) collective-permute-start(bf16[18,4,128,128]{3,2,1,0:T(8,128)(2,1)} %collective-permute-done.19.refs_2_), channel_id=1, source_target_pairs={{0,2},{1,3},{2,0},{3,1},{4,6},{5,7},{6,4},{7,5},{8,10},{9,11},{10,... | collective-permute-start | bytes 7077896 | tf_op jit(solution)/shard_map/ppermute | solution.py:21
  242.8 3.2 collective-permute-start.12
  244.4 3.3 collective-permute-start.11
  272.7 31.9 %collective-permute-start.16 = (f32[6,128,384]{2,1,0:T(8,128)}, f32[6,128,384]{2,1,0:T(8,128)S(1)}, u32[]{:S(2)}, u32[]{:S(2)}) collective-permute-start(f32[6,128,384]{2,1,0:T(8,128)} %get-tuple-element.51), channel_id=1, source_target_pairs={{0,1},{1,0},{2,3},{3,2},{4,5},{5,4},{6,7},{7,6},{8,9},{9,8},{10,11... | collective-permute-start | bytes 3538952 | tf_op jit(solution)/shard_map/ppermute | solution.py:21
  273.1 31.5 %collective-permute-start.17 = (f32[6,128,384]{2,1,0:T(8,128)}, f32[6,128,384]{2,1,0:T(8,128)}, u32[]{:S(2)}, u32[]{:S(2)}) collective-permute-start(f32[6,128,384]{2,1,0:T(8,128)} %get-tuple-element.52), channel_id=1, source_target_pairs={{0,1},{1,0},{2,3},{3,2},{4,5},{5,4},{6,7},{7,6},{8,9},{9,8},{10,11... | collective-permute-start | bytes 3538952 | tf_op jit(solution)/shard_map/ppermute | solution.py:21
  273.2 31.2 %copy-start.29 = (s32[48,3]{0,1:T(4,128)S(1)}, s32[48,3]{0,1:T(4,128)}, u32[]{:S(2)}) copy-start(s32[48,3]{0,1:T(4,128)} %param.5) | copy-start | bytes 1732
  273.2 31.4 %collective-permute-start.18 = (f32[6,128,384]{2,1,0:T(8,128)}, f32[6,128,384]{2,1,0:T(8,128)}, u32[]{:S(2)}, u32[]{:S(2)}) collective-permute-start(f32[6,128,384]{2,1,0:T(8,128)} %get-tuple-element.53), channel_id=1, source_target_pairs={{0,1},{1,0},{2,3},{3,2},{4,5},{5,4},{6,7},{7,6},{8,9},{9,8},{10,11... | collective-permute-start | bytes 3538952 | tf_op jit(solution)/shard_map/ppermute | solution.py:21
  304.4 6.2 %collective-permute-start.21 = (f32[6,128,384]{2,1,0:T(8,128)}, f32[6,128,384]{2,1,0:T(8,128)S(1)}, u32[]{:S(2)}, u32[]{:S(2)}) collective-permute-start(f32[6,128,384]{2,1,0:T(8,128)} %get-tuple-element.58), channel_id=1, source_target_pairs={{0,1},{1,0},{2,3},{3,2},{4,5},{5,4},{6,7},{7,6},{8,9},{9,8},{10,11... | collective-permute-start | bytes 3538952 | tf_op jit(solution)/shard_map/ppermute | solution.py:21
  309.9 17.0 %collective-permute-start.22 = (f32[6,128,384]{2,1,0:T(8,128)S(1)}, f32[6,128,384]{2,1,0:T(8,128)S(1)}, u32[]{:S(2)}, u32[]{:S(2)}) collective-permute-start(f32[6,128,384]{2,1,0:T(8,128)S(1)} %copy-done.24), channel_id=1, source_target_pairs={{0,1},{1,0},{2,3},{3,2},{4,5},{5,4},{6,7},{7,6},{8,9},{9,8},{10,11... | collective-permute-start | bytes 3538952 | tf_op jit(solution)/shard_map/ppermute | solution.py:21
  310.5 16.4 %collective-permute-start.23 = (f32[6,128,384]{2,1,0:T(8,128)S(1)}, f32[6,128,384]{2,1,0:T(8,128)S(1)}, u32[]{:S(2)}, u32[]{:S(2)}) collective-permute-start(f32[6,128,384]{2,1,0:T(8,128)S(1)} %copy-done.22), channel_id=1, source_target_pairs={{0,1},{1,0},{2,3},{3,2},{4,5},{5,4},{6,7},{7,6},{8,9},{9,8},{10,11... | collective-permute-start | bytes 3538952 | tf_op jit(solution)/shard_map/ppermute | solution.py:21
  326.3 3.0 collective-permute-start.25
  326.8 4.2 %collective-permute-start.26 = (f32[6,128,384]{2,1,0:T(8,128)S(1)}, f32[6,128,384]{2,1,0:T(8,128)S(1)}, u32[]{:S(2)}, u32[]{:S(2)}) collective-permute-start(f32[6,128,384]{2,1,0:T(8,128)S(1)} %get-tuple-element.67), channel_id=1, source_target_pairs={{0,1},{1,0},{2,3},{3,2},{4,5},{5,4},{6,7},{7,6},{8,9},{9,8},{10,11... | collective-permute-start | bytes 3538952 | tf_op jit(solution)/shard_map/ppermute | solution.py:21
  332.0 4.8 %collective-permute-start.27 = (f32[8,384]{1,0:T(8,128)S(1)}, f32[8,384]{1,0:T(8,128)S(1)}, u32[]{:S(2)}, u32[]{:S(2)}) collective-permute-start(f32[8,384]{1,0:T(8,128)S(1)} %get-tuple-element.69.sums_ref), channel_id=1, source_target_pairs={{0,8},{1,9},{2,10},{3,11},{4,12},{5,13},{6,14},{7,15},{8,0},{9,1},... | collective-permute-start | bytes 36872 | tf_op jit(solution)/shard_map/ppermute | solution.py:21
  (28 other events, 125.7 us)

commit v5 on v4

--- a/solution.py
+++ b/solution.py
@@ -29,10 +29,14 @@
     return not inner(i)
 
 
-def panel_kernel(slot_ref, tiles_ref, *panel_refs):
+def panel_kernel(first_steps, slot_ref, tiles_ref, first_ref, *panel_refs):
     rows, _, width, _ = tiles_ref.shape
     first = pl.program_id(0) * rows
     steps = pl.num_programs(0) // len(panel_refs)
+
+    @pl.when(pl.program_id(0) < first_steps)
+    def _():
+        first_ref[...] = tiles_ref[...]
 
     for n, panel_ref in enumerate(panel_refs):
 
@@ -48,26 +52,34 @@
                     )
 
 
-def make_panel(tile_values, slots, parts):
+def make_panel(tile_values, slots, parts, first_rows):
     block_rows, slots_per_row, width, _ = tile_values.shape
     part_rows = block_rows // parts
-    step = math.gcd(part_rows, 12)
+    step = math.gcd(math.gcd(part_rows, first_rows), 12)
     steps = part_rows // step
+    first_steps = first_rows // step
 
     def part_block(n):
         return pl.BlockSpec(
             (step, width, PC * width), lambda i, s: (jnp.clip(i - n * steps, 0, steps - 1), 0, 0)
         )
 
+    tile_shape = (slots_per_row, width, width)
     return pl.pallas_call(
-        panel_kernel,
+        functools.partial(panel_kernel, first_steps),
         grid_spec=pltpu.PrefetchScalarGridSpec(
             num_scalar_prefetch=1,
             grid=(block_rows // step,),
             in_specs=[pl.BlockSpec((step, slots_per_row, width, width), lambda i, s: (i, 0, 0, 0))],
-            out_specs=[part_block(n) for n in range(parts)],
+            out_specs=[
+                pl.BlockSpec(
+                    (step, *tile_shape), lambda i, s: (jnp.minimum(i, first_steps - 1), 0, 0, 0)
+                )
+            ]
+            + [part_block(n) for n in range(parts)],
         ),
-        out_shape=[jax.ShapeDtypeStruct((part_rows, width, PC * width), jnp.bfloat16)] * parts,
+        out_shape=[jax.ShapeDtypeStruct((first_rows, *tile_shape), jnp.bfloat16)]
+        + [jax.ShapeDtypeStruct((part_rows, width, PC * width), jnp.bfloat16)] * parts,
         compiler_params=pltpu.CompilerParams(vmem_limit_bytes=12 * MIB),
         cost_estimate=SHORT,
         name="panel",
@@ -199,7 +211,7 @@
         out_shape=[jax.ShapeDtypeStruct((len(plan) * rows, width, half), jnp.float32)]
         + [jax.ShapeDtypeStruct((rows, width, half), jnp.float32)] * len(plan),
         in_specs=[smem, smem, vmem, vmem] + [anywhere] * len(arrays),
-        out_specs=[anywhere] * (1 + len(plan)),
+        out_specs=[pl.BlockSpec(memory_space=pltpu.HBM)] * (1 + len(plan)),
         scratch_shapes=[
             pltpu.VMEM((2, STRIPS, rows, slots, width, width), jnp.bfloat16),
             pltpu.VMEM((2, width, 2 * half), jnp.float32),
@@ -264,7 +276,7 @@
             jax.ShapeDtypeStruct((8, half), jnp.float32),
         ),
         input_output_aliases=aliases,
-        compiler_params=pltpu.CompilerParams(vmem_limit_bytes=16 * MIB),
+        compiler_params=pltpu.CompilerParams(vmem_limit_bytes=20 * MIB),
         cost_estimate=SHORT,
         name="square",
     )(*operands)
@@ -343,13 +355,14 @@
         given = [jnp.where(odd, a, b) for a, b in zip(pieces[::2], pieces[1::2])]
         return kept, [swapped(p, 1) for p in given]
 
-    rows = math.gcd(block_rows // 8, 6) if block_rows >= 8 else 1
-    one, two = 3 * block_rows // 8, 2 * (3 * block_rows // 8)
-    few = one // 3 if one >= 3 else one
+    rows = block_rows // 16 or 1
+    one, two = 8 * rows, 13 * rows
+    if block_rows % 16:
+        one, two = block_rows // 3, 2 * (block_rows // 3)
+    few = one // 2 or one
     from_x = swapped(tile_values, 2)
-    own = tile_values[:one]
+    own, *panel = make_panel(tile_values, slot, 2 if relayed else 1, one)
     from_z = [swapped(own, 4)]
-    panel = make_panel(after(tile_values, own), slot, 2 if relayed else 1)
     if relayed:
         across = GC + GC // 2
         near = pack(where, 0, *shared(panel))
@@ -365,20 +378,20 @@
         is_inner = inner(device)
         far = [jnp.where(is_inner, a, b) for a, b in zip(returned, outward)]
         far = pack(where, half // 2, *shared(far))
-        tied = inward[1], outward[1], near
+        tied = inward[1], outward[1]
     else:
-        panels = list(panel)
+        panels = panel
         for bit in range(low_bits, all_bits):
             panels = panels + [swapped(p, 1 << bit) for p in panels]
         others = [swapped(p, 1) for p in panels]
         near = pack(where, 0, panels, others)
         far = pack(where, half // 2, panels, others)
-        tied = (near,)
+        tied = ()
     from_xz = [swapped(after(from_z[0][:few], from_x), 2)]
     if few < one:
         from_xz.append(swapped(after(from_z[0][few:], from_xz[0]), 2))
-    later = after(tile_values, *tied, from_xz[0])
-    from_z.append(swapped(later[one:two], 4))
+    later = after(tile_values, near)
+    from_z.append(swapped(after(later[one:two], *tied, from_xz[0]), 4))
     last = jnp.concatenate([from_x[two:], later[two:]])
     last = swapped(after(last, from_z[1], from_xz[-1]), 4)
     from_xz.append(swapped(after(from_z[1], from_xz[-1]), 2))
@@ -397,7 +410,9 @@
     totals = []
     sums = jnp.zeros((8, PC * width), jnp.float32)
     for lo, hi in ((0, one), (one, two), (two, block_rows)):
-        table = after(index, totals[0], got[0]) if len(totals) == 2 else index
+        table = index
+        if len(totals) == 2:
+            table = after(index, totals[0], got[0])
         pieces = [tiles_at(row) for row in range(lo, hi, rows)]
         mine, other = expand(rows, lo, pieces, order, table, near, far)
         got = [swapped(a, 1) for a in other]

time: 342 us -> 341 us (level)
  local copies, waits for them, and re-layouts: 40.3 us -> 28.3 us
  waiting for transfers between devices: 190 us -> 197 us
  Pallas kernels: 58.3 us -> 63.3 us
    ppermute x28 -> x36, waiting for transfers between devices: 190 us -> 197 us  [swapped(): return lax.ppermute(array, 'grid', pairs)]
    unnamed x65 -> x67, local copies, waits for them, and re-layouts: 26.8 us -> 20.7 us
    slice x3 -> x1, local copies, waits for them, and re-layouts: 7.72 us -> 1.67 us  [shards(): from_z.append(swapped(after(later[one:two], *tied, from_xz[0]), 4))]
    ppermute x28 -> x36, starting transfers between devices: 41.1 us -> 38.7 us  [swapped(): return lax.ppermute(array, 'grid', pairs)]
  transfers between devices with their start and end apart: 28 -> 36, of which waited for: 13 -> 10; matrix products, arithmetic and copies ran while one was open for 7% -> 6% of each run, Pallas kernels for 15% -> 15%
where the time goes in v5:
time: 341 us; the launch traced here: 340 us
  waiting for transfers between devices  197 us (58%)
  Pallas kernels  63.3 us (19%)
  starting transfers between devices  38.7 us (11%)
  local copies, waits for them, and re-layouts  28.3 us (8%)
  other arithmetic  12.2 us (4%)
    ppermute x36, waiting for transfers between devices, swapped(): return lax.ppermute(array, 'grid', pairs)  197 us
    pallas_call x3, Pallas kernels, expand(): pl.pallas_call(functools.partial(expand_kernel, first, plan), out_shape=[...  40.7 us
    ppermute x36, starting transfers between devices, swapped(): return lax.ppermute(array, 'grid', pairs)  38.7 us
    unnamed x67, local copies, waits for them, and re-layouts  20.7 us
    pallas_call x3, Pallas kernels, square(): pl.pallas_call(functools.partial(square_kernel, lo, len(got)), grid_spec=...  6.96 us
  transfers between devices with their start and end apart: 36, of which 10 were waited for; matrix products, arithmetic and copies ran while one was open for 6% of the time, Pallas kernels for 15%

profile of v5, /device:TPU:0, one launch (start us, length us, event | category | flops | bytes accessed | tf_op | source)
XLA Modules:
  0.0 340.1 jit_solution(3700233147838693098)
XLA Ops:
  1.0 6.0 %panel.1 = (bf16[24,4,128,128]{3,2,1,0:T(8,128)(2,1)S(1)}, bf16[24,128,384]{2,1,0:T(8,128)(2,1)S(1)}, bf16[24,128,384]{2,1,0:T(8,128)(2,1)}) custom-call(s32[144]{0:T(256)S(1)} %reshape.160.slot_ref, bf16[48,4,128,128]{3,2,1,0:T(8,128)(2,1)} %refs_0_.5), custom_call_target="tpu_custom_call" | custom-call | bytes 1024 | tf_op jit(solution)/shard_map/panel/pallas_call | solution.py:68
  7.0 3.0 collective-permute-start.2
  12.4 2.1 collective-permute-start.5
  14.6 63.6 %collective-permute-done.2.refs_2_ = bf16[24,4,128,128]{3,2,1,0:T(8,128)(2,1)S(1)} collective-permute-done((bf16[24,4,128,128]{3,2,1,0:T(8,128)(2,1)S(1)}, bf16[24,4,128,128]{3,2,1,0:T(8,128)(2,1)S(1)}, u32[]{:S(2)}, u32[]{:S(2)}) %collective-permute-start.2) | collective-permute-done | bytes 3145760 | tf_op jit(solution)/shard_map/ppermute | solution.py:21
  78.2 5.1 %collective-permute-start.3 = (bf16[24,128,384]{2,1,0:T(8,128)(2,1)S(1)}, bf16[24,128,384]{2,1,0:T(8,128)(2,1)}, u32[]{:S(2)}, u32[]{:S(2)}) collective-permute-start(bf16[24,128,384]{2,1,0:T(8,128)(2,1)S(1)} %get-tuple-element.50), channel_id=1, source_target_pairs={{0,4},{1,5},{2,6},{3,7},{12,8},{13,9},{14,10},{15,11},{16,20},{17,... | collective-permute-start | bytes 7077896 | tf_op jit(solution)/shard_map/ppermute | solution.py:21
  84.6 47.0 %collective-permute-done.3 = bf16[24,128,384]{2,1,0:T(8,128)(2,1)} collective-permute-done((bf16[24,128,384]{2,1,0:T(8,128)(2,1)S(1)}, bf16[24,128,384]{2,1,0:T(8,128)(2,1)}, u32[]{:S(2)}, u32[]{:S(2)}) %collective-permute-start.3) | collective-permute-done | bytes 2359328 | tf_op jit(solution)/shard_map/ppermute | solution.py:21
  131.5 2.1 collective-permute-start.6
  133.6 3.6 %collective-permute-done.7 = bf16[24,128,384]{2,1,0:T(8,128)(2,1)} collective-permute-done((bf16[24,128,384]{2,1,0:T(8,128)(2,1)S(1)}, bf16[24,128,384]{2,1,0:T(8,128)(2,1)}, u32[]{:S(2)}, u32[]{:S(2)}) %collective-permute-start.7) | collective-permute-done | bytes 2359328 | tf_op jit(solution)/shard_map/ppermute | solution.py:21
  137.2 3.7 %collective-permute-start.8 = (bf16[24,128,384]{2,1,0:T(8,128)(2,1)}, bf16[24,128,384]{2,1,0:T(8,128)(2,1)}, u32[]{:S(2)}, u32[]{:S(2)}) collective-permute-start(bf16[24,128,384]{2,1,0:T(8,128)(2,1)} %get-tuple-element.51), channel_id=1, source_target_pairs={{0,4},{1,5},{2,6},{3,7},{12,8},{13,9},{14,10},{15,11},{16,20},{17,... | collective-permute-start | bytes 7077896 | tf_op jit(solution)/shard_map/ppermute | solution.py:21
  142.3 1.9 fusion.3
  144.2 4.1 %collective-permute-done.13.refs_1_ = bf16[48,4,128,128]{3,2,1,0:T(8,128)(2,1)} collective-permute-done((bf16[48,4,128,128]{3,2,1,0:T(8,128)(2,1)}, bf16[48,4,128,128]{3,2,1,0:T(8,128)(2,1)}, u32[]{:S(2)}, u32[]{:S(2)}) %collective-permute-start.13) | collective-permute-done | bytes 6291488 | tf_op jit(solution)/shard_map/ppermute | solution.py:21
  151.0 2.9 broadcast_select_fusion.6
  154.4 34.0 %collective-permute-done.8 = bf16[24,128,384]{2,1,0:T(8,128)(2,1)} collective-permute-done((bf16[24,128,384]{2,1,0:T(8,128)(2,1)}, bf16[24,128,384]{2,1,0:T(8,128)(2,1)}, u32[]{:S(2)}, u32[]{:S(2)}) %collective-permute-start.8) | collective-permute-done | bytes 2359328 | tf_op jit(solution)/shard_map/ppermute | solution.py:21
  188.4 2.0 collective-permute-start.9
  190.6 2.2 pack.2.near_ref
  192.8 2.2 copy-done
  195.0 1.7 slice.49
  196.7 3.3 collective-permute-start.24
  201.2 32.8 %collective-permute-done.15.refs_4_ = bf16[12,4,128,128]{3,2,1,0:T(8,128)(2,1)S(1)} collective-permute-done((bf16[12,4,128,128]{3,2,1,0:T(8,128)(2,1)}, bf16[12,4,128,128]{3,2,1,0:T(8,128)(2,1)S(1)}, u32[]{:S(2)}, u32[]{:S(2)}) %collective-permute-start.15) | collective-permute-done | bytes 1572896 | tf_op jit(solution)/shard_map/ppermute | solution.py:21
  234.0 6.9 %collective-permute-done.24.refs_2_ = bf16[15,4,128,128]{3,2,1,0:T(8,128)(2,1)} collective-permute-done((bf16[15,4,128,128]{3,2,1,0:T(8,128)(2,1)S(1)}, bf16[15,4,128,128]{3,2,1,0:T(8,128)(2,1)}, u32[]{:S(2)}, u32[]{:S(2)}) %collective-permute-start.24) | collective-permute-done | bytes 1966112 | tf_op jit(solution)/shard_map/ppermute | solution.py:21
  242.1 2.9 broadcast_select_fusion
  252.5 1.7 collective-permute-start.31
  255.2 2.6 pack.3.far_ref
  259.5 20.8 %expand.3 = (f32[24,128,384]{2,1,0:T(8,128)S(1)}, f32[3,128,384]{2,1,0:T(8,128)S(1)}, f32[3,128,384]{2,1,0:T(8,128)S(1)}, f32[3,128,384]{2,1,0:T(8,128)S(1)}, f3...) custom-call(s32[4]{0:T(128)S(1)} %iota_xor_fusion.order_ref, ...), custom_call_target="tpu_custom_call" | custom-call | bytes 1024 | tf_op jit(solution)/shard_map/expand/pallas_call | solution.py:209
  281.0 2.0 collective-permute-done.25.refs_3_
  287.3 11.7 %expand.4 = (f32[15,128,384]{2,1,0:T(8,128)S(1)}, f32[3,128,384]{2,1,0:T(8,128)}, f32[3,128,384]{2,1,0:T(8,128)}, f32[3,128,384]{2,1,0:T(8,128)}, f32[3,128,384]...) custom-call(s32[4]{0:T(128)S(1)} %iota_xor_fusion.order_ref, s32[768]{0:T(1024)S(1)} %add.104.index_ref, ...), custom_call_target="tpu_custom_call" | custom-call | bytes 1024 | tf_op jit(solution)/shard_map/expand/pallas_call | solution.py:209
  303.8 2.5 copy-done.6
  313.9 3.2 square.3
  317.7 8.1 %expand.5 = (f32[9,128,384]{2,1,0:T(8,128)S(1)}, f32[3,128,384]{2,1,0:T(8,128)S(1)}, f32[3,128,384]{2,1,0:T(8,128)S(1)}, f32[3,128,384]{2,1,0:T(8,128)S(1)}) custom-call(s32[4]{0:T(128)S(1)} %iota_xor_fusion.order_ref, s32[768]{0:T(1024)S(1)} %add.104.index_ref, bf16[24,128,768]{2,1,0:T(8,128)(2,1)S(1)} %bitcast.11, bf16[24,128,768]{2,1,0:T(8,128)(2,1)S(1)} %copy-done.2, ...), custom_call_target="tpu_custom_call" | custom-call | bytes 1024 | tf_op jit(solution)/shard_map/expand/pallas_call | solution.py:209
  326.5 2.8 square.4
  332.3 3.0 collective-permute-done.35.got_ref
  335.3 4.8 %scale.1 = f32[48,3,128,128]{3,2,1,0:T(8,128)} custom-call(f32[8,384]{1,0:T(8,128)S(1)} %get-tuple-element.87.sums_ref, f32[8,384]{1,0:T(8,128)S(1)} %collective-permute-done.35.got_ref, f32[48,128,384]{2,1,0:T(8,128)S(1)} %get-tuple-element.88.squared_ref), custom_call_target="tpu_custom_call" | custom-call | bytes 1024 | tf_op jit(solution)/shard_map/scale/pallas_call | solution.py:298
  (148 shorter events, 43.4 us)
Async XLA Ops:
  7.0 71.1 %collective-permute-start.2 = (bf16[24,4,128,128]{3,2,1,0:T(8,128)(2,1)S(1)}, bf16[24,4,128,128]{3,2,1,0:T(8,128)(2,1)S(1)}, u32[]{:S(2)}, u32[]{:S(2)}) collective-permute-start(bf16[24,4,128,128]{3,2,1,0:T(8,128)(2,1)S(1)} %get-tuple-element.49), channel_id=1, source_target_pairs={{0,4},{1,5},{2,6},{3,7},{4,0},{5,1},{6,2},{7,3},{8,12},{9,13},{10,... | collective-permute-start | bytes 9437192 | tf_op jit(solution)/shard_map/ppermute | solution.py:21
  10.9 137.4 %collective-permute-start.13 = (bf16[48,4,128,128]{3,2,1,0:T(8,128)(2,1)}, bf16[48,4,128,128]{3,2,1,0:T(8,128)(2,1)}, u32[]{:S(2)}, u32[]{:S(2)}) collective-permute-start(bf16[48,4,128,128]{3,2,1,0:T(8,128)(2,1)} %refs_0_.5), channel_id=1, source_target_pairs={{0,2},{1,3},{2,0},{3,1},{4,6},{5,7},{6,4},{7,5},{8,10},{9,11},{10,... | collective-permute-start | bytes 18874376 | tf_op jit(solution)/shard_map/ppermute | solution.py:21
  12.4 72.1 %collective-permute-start.5 = (bf16[24,128,384]{2,1,0:T(8,128)(2,1)}, bf16[24,128,384]{2,1,0:T(8,128)(2,1)}, u32[]{:S(2)}, u32[]{:S(2)}) collective-permute-start(bf16[24,128,384]{2,1,0:T(8,128)(2,1)} %get-tuple-element.51), channel_id=1, source_target_pairs={{4,8},{5,9},{6,10},{7,11},{8,4},{9,5},{10,6},{11,7},{20,24},{21,25... | collective-permute-start | bytes 7077896 | tf_op jit(solution)/shard_map/ppermute | solution.py:21
  78.2 53.4 %collective-permute-start.3 = (bf16[24,128,384]{2,1,0:T(8,128)(2,1)S(1)}, bf16[24,128,384]{2,1,0:T(8,128)(2,1)}, u32[]{:S(2)}, u32[]{:S(2)}) collective-permute-start(bf16[24,128,384]{2,1,0:T(8,128)(2,1)S(1)} %get-tuple-element.50), channel_id=1, source_target_pairs={{0,4},{1,5},{2,6},{3,7},{12,8},{13,9},{14,10},{15,11},{16,20},{17,... | collective-permute-start | bytes 7077896 | tf_op jit(solution)/shard_map/ppermute | solution.py:21
  83.3 53.9 %collective-permute-start.7 = (bf16[24,128,384]{2,1,0:T(8,128)(2,1)S(1)}, bf16[24,128,384]{2,1,0:T(8,128)(2,1)}, u32[]{:S(2)}, u32[]{:S(2)}) collective-permute-start(bf16[24,128,384]{2,1,0:T(8,128)(2,1)S(1)} %collective-permute-done.4), channel_id=1, source_target_pairs={{4,0},{5,1},{6,2},{7,3},{8,12},{9,13},{10,14},{11,15},{20,16},{21,... | collective-permute-start | bytes 7077896 | tf_op jit(solution)/shard_map/ppermute | solution.py:21
  131.5 22.3 %collective-permute-start.6 = (bf16[24,128,384]{2,1,0:T(8,128)(2,1)}, bf16[24,128,384]{2,1,0:T(8,128)(2,1)}, u32[]{:S(2)}, u32[]{:S(2)}) collective-permute-start(bf16[24,128,384]{2,1,0:T(8,128)(2,1)} %collective-permute-done.3), channel_id=1, source_target_pairs={{4,8},{5,9},{6,10},{7,11},{8,4},{9,5},{10,6},{11,7},{20,24},{21,25... | collective-permute-start | bytes 7077896 | tf_op jit(solution)/shard_map/ppermute | solution.py:21
  137.2 51.2 %collective-permute-start.8 = (bf16[24,128,384]{2,1,0:T(8,128)(2,1)}, bf16[24,128,384]{2,1,0:T(8,128)(2,1)}, u32[]{:S(2)}, u32[]{:S(2)}) collective-permute-start(bf16[24,128,384]{2,1,0:T(8,128)(2,1)} %get-tuple-element.51), channel_id=1, source_target_pairs={{0,4},{1,5},{2,6},{3,7},{12,8},{13,9},{14,10},{15,11},{16,20},{17,... | collective-permute-start | bytes 7077896 | tf_op jit(solution)/shard_map/ppermute | solution.py:21
  141.0 55.7 %collective-permute-start.10 = (bf16[24,128,384]{2,1,0:T(8,128)(2,1)}, bf16[24,128,384]{2,1,0:T(8,128)(2,1)}, u32[]{:S(2)}, u32[]{:S(2)}) collective-permute-start(bf16[24,128,384]{2,1,0:T(8,128)(2,1)} %collective-permute-done.5), channel_id=1, source_target_pairs={{4,0},{5,1},{6,2},{7,3},{8,12},{9,13},{10,14},{11,15},{20,16},{21,... | collective-permute-start | bytes 7077896 | tf_op jit(solution)/shard_map/ppermute | solution.py:21
  148.2 48.5 %collective-permute-start.14 = (bf16[12,4,128,128]{3,2,1,0:T(8,128)(2,1)}, bf16[12,4,128,128]{3,2,1,0:T(8,128)(2,1)}, u32[]{:S(2)}, u32[]{:S(2)}) collective-permute-start(bf16[12,4,128,128]{3,2,1,0:T(8,128)(2,1)} %get-tuple-element.57), channel_id=1, source_target_pairs={{0,2},{1,3},{2,0},{3,1},{4,6},{5,7},{6,4},{7,5},{8,10},{9,11},{10,... | collective-permute-start | bytes 4718600 | tf_op jit(solution)/shard_map/ppermute | solution.py:21
  151.0 39.6 %collective-permute-start = (bf16[12,128,384]{2,1,0:T(8,128)(2,1)}, bf16[12,128,384]{2,1,0:T(8,128)(2,1)S(1)}, u32[]{:S(2)}, u32[]{:S(2)}) collective-permute-start(bf16[12,128,384]{2,1,0:T(8,128)(2,1)} %get-tuple-element.108), channel_id=1, source_target_pairs={{0,1},{1,0},{2,3},{3,2},{4,5},{5,4},{6,7},{7,6},{8,9},{9,8},{10,11... | collective-permute-start | bytes 3538952 | tf_op jit(solution)/shard_map/ppermute | solution.py:21
  153.9 36.7 %collective-permute-start.1 = (bf16[12,128,384]{2,1,0:T(8,128)(2,1)}, bf16[12,128,384]{2,1,0:T(8,128)(2,1)}, u32[]{:S(2)}, u32[]{:S(2)}) collective-permute-start(bf16[12,128,384]{2,1,0:T(8,128)(2,1)} %get-tuple-element.106), channel_id=1, source_target_pairs={{0,1},{1,0},{2,3},{3,2},{4,5},{5,4},{6,7},{7,6},{8,9},{9,8},{10,11... | collective-permute-start | bytes 3538952 | tf_op jit(solution)/shard_map/ppermute | solution.py:21
  188.4 53.7 %collective-permute-start.9 = (bf16[24,128,384]{2,1,0:T(8,128)(2,1)}, bf16[24,128,384]{2,1,0:T(8,128)(2,1)}, u32[]{:S(2)}, u32[]{:S(2)}) collective-permute-start(bf16[24,128,384]{2,1,0:T(8,128)(2,1)} %collective-permute-done.8), channel_id=1, source_target_pairs={{4,8},{5,9},{6,10},{7,11},{8,4},{9,5},{10,6},{11,7},{20,24},{21,25... | collective-permute-start | bytes 7077896 | tf_op jit(solution)/shard_map/ppermute | solution.py:21
  196.7 44.1 %collective-permute-start.24 = (bf16[15,4,128,128]{3,2,1,0:T(8,128)(2,1)S(1)}, bf16[15,4,128,128]{3,2,1,0:T(8,128)(2,1)}, u32[]{:S(2)}, u32[]{:S(2)}) collective-permute-start(bf16[15,4,128,128]{3,2,1,0:T(8,128)(2,1)S(1)} %slice.49), channel_id=1, source_target_pairs={{0,4},{1,5},{2,6},{3,7},{4,0},{5,1},{6,2},{7,3},{8,12},{9,13},{10,... | collective-permute-start | bytes 5898248 | tf_op jit(solution)/shard_map/ppermute | solution.py:21
  200.0 34.0 %collective-permute-start.15 = (bf16[12,4,128,128]{3,2,1,0:T(8,128)(2,1)}, bf16[12,4,128,128]{3,2,1,0:T(8,128)(2,1)S(1)}, u32[]{:S(2)}, u32[]{:S(2)}) collective-permute-start(bf16[12,4,128,128]{3,2,1,0:T(8,128)(2,1)} %get-tuple-element.58), channel_id=1, source_target_pairs={{0,2},{1,3},{2,0},{3,1},{4,6},{5,7},{6,4},{7,5},{8,10},{9,11},{10,... | collective-permute-start | bytes 4718600 | tf_op jit(solution)/shard_map/ppermute | solution.py:21
  240.8 42.2 %collective-permute-start.25 = (bf16[15,4,128,128]{3,2,1,0:T(8,128)(2,1)}, bf16[15,4,128,128]{3,2,1,0:T(8,128)(2,1)}, u32[]{:S(2)}, u32[]{:S(2)}) collective-permute-start(bf16[15,4,128,128]{3,2,1,0:T(8,128)(2,1)} %collective-permute-done.24.refs_2_), channel_id=1, source_target_pairs={{0,2},{1,3},{2,0},{3,1},{4,6},{5,7},{6,4},{7,5},{8,10},{9,11},{10,... | collective-permute-start | bytes 5898248 | tf_op jit(solution)/shard_map/ppermute | solution.py:21
  246.3 8.9 %collective-permute-start.12 = (bf16[12,128,384]{2,1,0:T(8,128)(2,1)}, bf16[12,128,384]{2,1,0:T(8,128)(2,1)}, u32[]{:S(2)}, u32[]{:S(2)}) collective-permute-start(bf16[12,128,384]{2,1,0:T(8,128)(2,1)} %get-tuple-element.102), channel_id=1, source_target_pairs={{0,1},{1,0},{2,3},{3,2},{4,5},{5,4},{6,7},{7,6},{8,9},{9,8},{10,11... | collective-permute-start | bytes 3538952 | tf_op jit(solution)/shard_map/ppermute | solution.py:21
  247.6 7.6 %collective-permute-start.11 = (bf16[12,128,384]{2,1,0:T(8,128)(2,1)}, bf16[12,128,384]{2,1,0:T(8,128)(2,1)}, u32[]{:S(2)}, u32[]{:S(2)}) collective-permute-start(bf16[12,128,384]{2,1,0:T(8,128)(2,1)} %get-tuple-element.104), channel_id=1, source_target_pairs={{0,1},{1,0},{2,3},{3,2},{4,5},{5,4},{6,7},{7,6},{8,9},{9,8},{10,11... | collective-permute-start | bytes 3538952 | tf_op jit(solution)/shard_map/ppermute | solution.py:21
  252.5 65.2 %collective-permute-start.31 = (bf16[18,4,128,128]{3,2,1,0:T(8,128)(2,1)}, bf16[18,4,128,128]{3,2,1,0:T(8,128)(2,1)}, u32[]{:S(2)}, u32[]{:S(2)}) collective-permute-start(bf16[18,4,128,128]{3,2,1,0:T(8,128)(2,1)} %pad_maximum_fusion), channel_id=1, source_target_pairs={{0,4},{1,5},{2,6},{3,7},{4,0},{5,1},{6,2},{7,3},{8,12},{9,13},{10,... | collective-permute-start | bytes 7077896 | tf_op jit(solution)/shard_map/ppermute | solution.py:21
  280.4 3.9 %collective-permute-start.17 = (f32[3,128,384]{2,1,0:T(8,128)S(1)}, f32[3,128,384]{2,1,0:T(8,128)S(1)}, u32[]{:S(2)}, u32[]{:S(2)}) collective-permute-start(f32[3,128,384]{2,1,0:T(8,128)S(1)} %get-tuple-element.61), channel_id=1, source_target_pairs={{0,1},{1,0},{2,3},{3,2},{4,5},{5,4},{6,7},{7,6},{8,9},{9,8},{10,11... | collective-permute-start | bytes 1769480 | tf_op jit(solution)/shard_map/ppermute | solution.py:21
  280.9 4.2 %collective-permute-start.18 = (f32[3,128,384]{2,1,0:T(8,128)S(1)}, f32[3,128,384]{2,1,0:T(8,128)S(1)}, u32[]{:S(2)}, u32[]{:S(2)}) collective-permute-start(f32[3,128,384]{2,1,0:T(8,128)S(1)} %get-tuple-element.62), channel_id=1, source_target_pairs={{0,1},{1,0},{2,3},{3,2},{4,5},{5,4},{6,7},{7,6},{8,9},{9,8},{10,11... | collective-permute-start | bytes 1769480 | tf_op jit(solution)/shard_map/ppermute | solution.py:21
  283.0 3.5 %collective-permute-start.19 = (f32[3,128,384]{2,1,0:T(8,128)S(1)}, f32[3,128,384]{2,1,0:T(8,128)S(1)}, u32[]{:S(2)}, u32[]{:S(2)}) collective-permute-start(f32[3,128,384]{2,1,0:T(8,128)S(1)} %get-tuple-element.63), channel_id=1, source_target_pairs={{0,1},{1,0},{2,3},{3,2},{4,5},{5,4},{6,7},{7,6},{8,9},{9,8},{10,11... | collective-permute-start | bytes 1769480 | tf_op jit(solution)/shard_map/ppermute | solution.py:21
  283.8 16.1 %collective-permute-start.20 = (f32[3,128,384]{2,1,0:T(8,128)S(1)}, f32[3,128,384]{2,1,0:T(8,128)S(1)}, u32[]{:S(2)}, u32[]{:S(2)}) collective-permute-start(f32[3,128,384]{2,1,0:T(8,128)S(1)} %get-tuple-element.64), channel_id=1, source_target_pairs={{0,1},{1,0},{2,3},{3,2},{4,5},{5,4},{6,7},{7,6},{8,9},{9,8},{10,11... | collective-permute-start | bytes 1769480 | tf_op jit(solution)/shard_map/ppermute | solution.py:21
  285.1 16.1 %collective-permute-start.21 = (f32[3,128,384]{2,1,0:T(8,128)S(1)}, f32[3,128,384]{2,1,0:T(8,128)S(1)}, u32[]{:S(2)}, u32[]{:S(2)}) collective-permute-start(f32[3,128,384]{2,1,0:T(8,128)S(1)} %get-tuple-element.65), channel_id=1, source_target_pairs={{0,1},{1,0},{2,3},{3,2},{4,5},{5,4},{6,7},{7,6},{8,9},{9,8},{10,11... | collective-permute-start | bytes 1769480 | tf_op jit(solution)/shard_map/ppermute | solution.py:21
  286.0 16.1 %collective-permute-start.22 = (f32[3,128,384]{2,1,0:T(8,128)S(1)}, f32[3,128,384]{2,1,0:T(8,128)S(1)}, u32[]{:S(2)}, u32[]{:S(2)}) collective-permute-start(f32[3,128,384]{2,1,0:T(8,128)S(1)} %get-tuple-element.66), channel_id=1, source_target_pairs={{0,1},{1,0},{2,3},{3,2},{4,5},{5,4},{6,7},{7,6},{8,9},{9,8},{10,11... | collective-permute-start | bytes 1769480 | tf_op jit(solution)/shard_map/ppermute | solution.py:21
  287.3 16.4 %collective-permute-start.23 = (f32[3,128,384]{2,1,0:T(8,128)}, f32[3,128,384]{2,1,0:T(8,128)}, u32[]{:S(2)}, u32[]{:S(2)}) collective-permute-start(f32[3,128,384]{2,1,0:T(8,128)} %get-tuple-element.67), channel_id=1, source_target_pairs={{0,1},{1,0},{2,3},{3,2},{4,5},{5,4},{6,7},{7,6},{8,9},{9,8},{10,11... | collective-permute-start | bytes 1769480 | tf_op jit(solution)/shard_map/ppermute | solution.py:21
  300.8 16.3 %collective-permute-start.26 = (f32[3,128,384]{2,1,0:T(8,128)}, f32[3,128,384]{2,1,0:T(8,128)}, u32[]{:S(2)}, u32[]{:S(2)}) collective-permute-start(f32[3,128,384]{2,1,0:T(8,128)} %get-tuple-element.73), channel_id=1, source_target_pairs={{0,1},{1,0},{2,3},{3,2},{4,5},{5,4},{6,7},{7,6},{8,9},{9,8},{10,11... | collective-permute-start | bytes 1769480 | tf_op jit(solution)/shard_map/ppermute | solution.py:21
  302.1 23.9 %collective-permute-start.27 = (f32[3,128,384]{2,1,0:T(8,128)}, f32[3,128,384]{2,1,0:T(8,128)}, u32[]{:S(2)}, u32[]{:S(2)}) collective-permute-start(f32[3,128,384]{2,1,0:T(8,128)} %get-tuple-element.74), channel_id=1, source_target_pairs={{0,1},{1,0},{2,3},{3,2},{4,5},{5,4},{6,7},{7,6},{8,9},{9,8},{10,11... | collective-permute-start | bytes 1769480 | tf_op jit(solution)/shard_map/ppermute | solution.py:21
  303.0 23.5 %collective-permute-start.28 = (f32[3,128,384]{2,1,0:T(8,128)}, f32[3,128,384]{2,1,0:T(8,128)}, u32[]{:S(2)}, u32[]{:S(2)}) collective-permute-start(f32[3,128,384]{2,1,0:T(8,128)} %get-tuple-element.75), channel_id=1, source_target_pairs={{0,1},{1,0},{2,3},{3,2},{4,5},{5,4},{6,7},{7,6},{8,9},{9,8},{10,11... | collective-permute-start | bytes 1769480 | tf_op jit(solution)/shard_map/ppermute | solution.py:21
  303.7 22.8 %collective-permute-start.29 = (f32[3,128,384]{2,1,0:T(8,128)}, f32[3,128,384]{2,1,0:T(8,128)S(1)}, u32[]{:S(2)}, u32[]{:S(2)}) collective-permute-start(f32[3,128,384]{2,1,0:T(8,128)} %copy-done.26), channel_id=1, source_target_pairs={{0,1},{1,0},{2,3},{3,2},{4,5},{5,4},{6,7},{7,6},{8,9},{9,8},{10,11... | collective-permute-start | bytes 1769480 | tf_op jit(solution)/shard_map/ppermute | solution.py:21
  317.1 9.4 %collective-permute-start.30 = (f32[3,128,384]{2,1,0:T(8,128)}, f32[3,128,384]{2,1,0:T(8,128)S(1)}, u32[]{:S(2)}, u32[]{:S(2)}) collective-permute-start(f32[3,128,384]{2,1,0:T(8,128)} %copy-done.25), channel_id=1, source_target_pairs={{0,1},{1,0},{2,3},{3,2},{4,5},{5,4},{6,7},{7,6},{8,9},{9,8},{10,11... | collective-permute-start | bytes 1769480 | tf_op jit(solution)/shard_map/ppermute | solution.py:21
  325.9 3.4 %collective-permute-start.32 = (f32[3,128,384]{2,1,0:T(8,128)S(1)}, f32[3,128,384]{2,1,0:T(8,128)S(1)}, u32[]{:S(2)}, u32[]{:S(2)}) collective-permute-start(f32[3,128,384]{2,1,0:T(8,128)S(1)} %get-tuple-element.83), channel_id=1, source_target_pairs={{0,1},{1,0},{2,3},{3,2},{4,5},{5,4},{6,7},{7,6},{8,9},{9,8},{10,11... | collective-permute-start | bytes 1769480 | tf_op jit(solution)/shard_map/ppermute | solution.py:21
  330.6 4.7 %collective-permute-start.35 = (f32[8,384]{1,0:T(8,128)S(1)}, f32[8,384]{1,0:T(8,128)S(1)}, u32[]{:S(2)}, u32[]{:S(2)}) collective-permute-start(f32[8,384]{1,0:T(8,128)S(1)} %get-tuple-element.87.sums_ref), channel_id=1, source_target_pairs={{0,8},{1,9},{2,10},{3,11},{4,12},{5,13},{6,14},{7,15},{8,0},{9,1},... | collective-permute-start | bytes 36872 | tf_op jit(solution)/shard_map/ppermute | solution.py:21
  (37 other events, 289.1 us)

commit v6 on v5

--- a/solution.py
+++ b/solution.py
@@ -376,9 +376,13 @@
         returned = [swapped(after(inward[0], crossed[1]), across, inner)]
         returned.append(swapped(after(inward[1], returned[0]), across, inner))
         is_inner = inner(device)
-        far = [jnp.where(is_inner, a, b) for a, b in zip(returned, outward)]
-        far = pack(where, half // 2, *shared(far))
-        tied = inward[1], outward[1]
+        kept, received = [], []
+        for a, b in zip(returned, outward):
+            k, r = shared([jnp.where(is_inner, a, b)])
+            kept += k
+            received += r
+        far = pack(where, half // 2, kept, received)
+        tied = [inward[1], outward[1]]
     else:
         panels = panel
         for bit in range(low_bits, all_bits):
@@ -386,13 +390,14 @@
         others = [swapped(p, 1) for p in panels]
         near = pack(where, 0, panels, others)
         far = pack(where, half // 2, panels, others)
-        tied = ()
+        tied = []
     from_xz = [swapped(after(from_z[0][:few], from_x), 2)]
     if few < one:
         from_xz.append(swapped(after(from_z[0][few:], from_xz[0]), 2))
     later = after(tile_values, near)
-    from_z.append(swapped(after(later[one:two], *tied, from_xz[0]), 4))
     last = jnp.concatenate([from_x[two:], later[two:]])
+    tied = tied + [from_xz[0], last, keep, index]
+    from_z.append(swapped(after(later[one:two], *tied), 4))
     last = swapped(after(last, from_z[1], from_xz[-1]), 4)
     from_xz.append(swapped(after(from_z[1], from_xz[-1]), 2))
 
@@ -407,6 +412,7 @@
         return [(tile_values, row), (from_x, row)] + far_tiles
 
     squared = None
+    keep, index = lax.optimization_barrier((keep, index, from_z[1]))[:2]
     totals = []
     sums = jnp.zeros((8, PC * width), jnp.float32)
     for lo, hi in ((0, one), (one, two), (two, block_rows)):

time: 341 us -> 335 us (0.982)
  local copies, waits for them, and re-layouts: 28.3 us -> 13.9 us
  waiting for transfers between devices: 197 us -> 211 us
  Pallas kernels: 63.3 us -> 58.9 us
    unnamed x67 -> x17, local copies, waits for them, and re-layouts: 20.7 us -> 4.83 us
    ppermute x36, waiting for transfers between devices: 197 us -> 211 us  [swapped(): return lax.ppermute(array, 'grid', pairs)]
  transfers between devices with their start and end apart: 36 -> 36, of which waited for: 10 -> 14; matrix products, arithmetic and copies ran while one was open for 6% -> 6% of each run, Pallas kernels for 15% -> 14%
where the time goes in v6:
time: 335 us
  waiting for transfers between devices  211 us (63%)
  Pallas kernels  58.9 us (18%)
  starting transfers between devices  37.7 us (11%)
  local copies, waits for them, and re-layouts  13.9 us (4%)
  other arithmetic  12.5 us (4%)
    ppermute x36, waiting for transfers between devices, swapped(): return lax.ppermute(array, 'grid', pairs)  211 us
    pallas_call x3, Pallas kernels, expand(): pl.pallas_call(functools.partial(expand_kernel, first, plan), out_shape=[...  40.3 us
    ppermute x36, starting transfers between devices, swapped(): return lax.ppermute(array, 'grid', pairs)  37.7 us
    select_n x4, other arithmetic, shared(): given = [jnp.where(odd, a, b) for a, b in zip(pieces[::2], pieces[1::2])]  7 us
  transfers between devices with their start and end apart: 36, of which 14 were waited for; matrix products, arithmetic and copies ran while one was open for 6% of the time, Pallas kernels for 14%

profile of v6, /device:TPU:0, one launch (start us, length us, event | category | flops | bytes accessed | tf_op | source)
XLA Modules:
  0.0 334.6 jit_solution(13672279863016605561)
XLA Ops:
  1.0 6.0 %panel.1 = (bf16[24,4,128,128]{3,2,1,0:T(8,128)(2,1)S(1)}, bf16[24,128,384]{2,1,0:T(8,128)(2,1)S(1)}, bf16[24,128,384]{2,1,0:T(8,128)(2,1)}) custom-call(s32[144]{0:T(256)S(1)} %reshape.160.slot_ref, bf16[48,4,128,128]{3,2,1,0:T(8,128)(2,1)} %refs_0_.5), custom_call_target="tpu_custom_call" | custom-call | bytes 1024 | tf_op jit(solution)/shard_map/panel/pallas_call | solution.py:68
  7.0 3.0 collective-permute-start.2
  10.9 1.6 collective-permute-start.9
  12.4 2.1 collective-permute-start.7
  14.5 63.6 %collective-permute-done.2.refs_2_ = bf16[24,4,128,128]{3,2,1,0:T(8,128)(2,1)S(1)} collective-permute-done((bf16[24,4,128,128]{3,2,1,0:T(8,128)(2,1)S(1)}, bf16[24,4,128,128]{3,2,1,0:T(8,128)(2,1)S(1)}, u32[]{:S(2)}, u32[]{:S(2)}) %collective-permute-start.2) | collective-permute-done | bytes 3145760 | tf_op jit(solution)/shard_map/ppermute | solution.py:21
  78.2 5.1 %collective-permute-start.3 = (bf16[24,128,384]{2,1,0:T(8,128)(2,1)S(1)}, bf16[24,128,384]{2,1,0:T(8,128)(2,1)}, u32[]{:S(2)}, u32[]{:S(2)}) collective-permute-start(bf16[24,128,384]{2,1,0:T(8,128)(2,1)S(1)} %get-tuple-element.53), channel_id=1, source_target_pairs={{0,4},{1,5},{2,6},{3,7},{12,8},{13,9},{14,10},{15,11},{16,20},{17,... | collective-permute-start | bytes 7077896 | tf_op jit(solution)/shard_map/ppermute | solution.py:21
  84.5 47.0 %collective-permute-done.3 = bf16[24,128,384]{2,1,0:T(8,128)(2,1)} collective-permute-done((bf16[24,128,384]{2,1,0:T(8,128)(2,1)S(1)}, bf16[24,128,384]{2,1,0:T(8,128)(2,1)}, u32[]{:S(2)}, u32[]{:S(2)}) %collective-permute-start.3) | collective-permute-done | bytes 2359328 | tf_op jit(solution)/shard_map/ppermute | solution.py:21
  131.5 2.1 collective-permute-start.12
  133.7 3.5 %collective-permute-done.5 = bf16[24,128,384]{2,1,0:T(8,128)(2,1)} collective-permute-done((bf16[24,128,384]{2,1,0:T(8,128)(2,1)S(1)}, bf16[24,128,384]{2,1,0:T(8,128)(2,1)}, u32[]{:S(2)}, u32[]{:S(2)}) %collective-permute-start.5) | collective-permute-done | bytes 2359328 | tf_op jit(solution)/shard_map/ppermute | solution.py:21
  137.2 3.8 %collective-permute-start.6 = (bf16[24,128,384]{2,1,0:T(8,128)(2,1)}, bf16[24,128,384]{2,1,0:T(8,128)(2,1)}, u32[]{:S(2)}, u32[]{:S(2)}) collective-permute-start(bf16[24,128,384]{2,1,0:T(8,128)(2,1)} %get-tuple-element.56), channel_id=1, source_target_pairs={{0,4},{1,5},{2,6},{3,7},{12,8},{13,9},{14,10},{15,11},{16,20},{17,... | collective-permute-start | bytes 7077896 | tf_op jit(solution)/shard_map/ppermute | solution.py:21
  142.2 3.2 broadcast_select_fusion.7
  145.5 1.9 fusion.3
  149.7 3.3 broadcast_select_fusion.6
  154.2 34.2 %collective-permute-done.6 = bf16[24,128,384]{2,1,0:T(8,128)(2,1)} collective-permute-done((bf16[24,128,384]{2,1,0:T(8,128)(2,1)}, bf16[24,128,384]{2,1,0:T(8,128)(2,1)}, u32[]{:S(2)}, u32[]{:S(2)}) %collective-permute-start.6) | collective-permute-done | bytes 2359328 | tf_op jit(solution)/shard_map/ppermute | solution.py:21
  188.4 2.1 collective-permute-start.13
  193.3 2.3 pack.2.near_ref
  195.7 2.2 copy-done
  199.2 3.1 slice.43
  203.7 1.6 pad_maximum_fusion
  205.3 3.1 collective-permute-start.11
  209.9 33.8 %collective-permute-done.16.refs_4_ = bf16[12,4,128,128]{3,2,1,0:T(8,128)(2,1)} collective-permute-done((bf16[12,4,128,128]{3,2,1,0:T(8,128)(2,1)}, bf16[12,4,128,128]{3,2,1,0:T(8,128)(2,1)}, u32[]{:S(2)}, u32[]{:S(2)}) %collective-permute-start.16) | collective-permute-done | bytes 1572896 | tf_op jit(solution)/shard_map/ppermute | solution.py:21
  243.7 7.0 %collective-permute-done.11.refs_2_ = bf16[15,4,128,128]{3,2,1,0:T(8,128)(2,1)} collective-permute-done((bf16[15,4,128,128]{3,2,1,0:T(8,128)(2,1)}, bf16[15,4,128,128]{3,2,1,0:T(8,128)(2,1)}, u32[]{:S(2)}, u32[]{:S(2)}) %collective-permute-start.11) | collective-permute-done | bytes 1966112 | tf_op jit(solution)/shard_map/ppermute | solution.py:21
  252.2 2.9 broadcast_select_fusion
  256.2 1.7 collective-permute-start.31
  258.3 1.7 collective-permute-done.14.refs_2_
  261.2 19.5 %expand.3 = (f32[24,128,384]{2,1,0:T(8,128)S(1)}, f32[3,128,384]{2,1,0:T(8,128)S(1)}, f32[3,128,384]{2,1,0:T(8,128)S(1)}, f32[3,128,384]{2,1,0:T(8,128)S(1)}, f3...) custom-call(s32[4]{0:T(128)S(1)} %iota_xor_fusion.order_ref, ...), custom_call_target="tpu_custom_call" | custom-call | bytes 1024 | tf_op jit(solution)/shard_map/expand/pallas_call | solution.py:209
  281.4 12.5 %collective-permute-done.25.refs_3_ = bf16[15,4,128,128]{3,2,1,0:T(8,128)(2,1)S(1)} collective-permute-done((bf16[15,4,128,128]{3,2,1,0:T(8,128)(2,1)}, bf16[15,4,128,128]{3,2,1,0:T(8,128)(2,1)S(1)}, u32[]{:S(2)}, u32[]{:S(2)}) %collective-permute-start.25) | collective-permute-done | bytes 1966112 | tf_op jit(solution)/shard_map/ppermute | solution.py:21
  296.1 12.7 %expand.4 = (f32[15,128,384]{2,1,0:T(8,128)S(1)}, f32[3,128,384]{2,1,0:T(8,128)S(1)}, f32[3,128,384]{2,1,0:T(8,128)S(1)}, f32[3,128,384]{2,1,0:T(8,128)S(1)}, f3...) custom-call(s32[4]{0:T(128)S(1)} %iota_xor_fusion.order_ref, s32[768]{0:T(1024)S(1)} %add.105.index_ref, ...), custom_call_target="tpu_custom_call" | custom-call | bytes 1024 | tf_op jit(solution)/shard_map/expand/pallas_call | solution.py:209
  309.9 1.9 square.3
  312.2 8.1 %expand.5 = (f32[9,128,384]{2,1,0:T(8,128)S(1)}, f32[3,128,384]{2,1,0:T(8,128)S(1)}, f32[3,128,384]{2,1,0:T(8,128)S(1)}, f32[3,128,384]{2,1,0:T(8,128)S(1)}) custom-call(s32[4]{0:T(128)S(1)} %iota_xor_fusion.order_ref, s32[768]{0:T(1024)S(1)} %add.105.index_ref, bf16[24,128,768]{2,1,0:T(8,128)(2,1)S(1)} %bitcast.9, bf16[24,128,768]{2,1,0:T(8,128)(2,1)S(1)} %pack.3.far_ref, ...), custom_call_target="tpu_custom_call" | custom-call | bytes 1024 | tf_op jit(solution)/shard_map/expand/pallas_call | solution.py:209
  325.7 4.1 %collective-permute-done.35.got_ref = f32[8,384]{1,0:T(8,128)S(1)} collective-permute-done((f32[8,384]{1,0:T(8,128)S(1)}, f32[8,384]{1,0:T(8,128)S(1)}, u32[]{:S(2)}, u32[]{:S(2)}) %collective-permute-start.35) | collective-permute-done | bytes 12320 | tf_op jit(solution)/shard_map/ppermute | solution.py:21
  329.8 4.8 %scale.1 = f32[48,3,128,128]{3,2,1,0:T(8,128)} custom-call(f32[8,384]{1,0:T(8,128)S(1)} %get-tuple-element.91.sums_ref, f32[8,384]{1,0:T(8,128)S(1)} %collective-permute-done.35.got_ref, f32[48,128,384]{2,1,0:T(8,128)S(1)} %get-tuple-element.92.squared_ref), custom_call_target="tpu_custom_call" | custom-call | bytes 1024 | tf_op jit(solution)/shard_map/scale/pallas_call | solution.py:298
  (97 shorter events, 28.7 us)
Async XLA Ops:
  7.0 71.1 %collective-permute-start.2 = (bf16[24,4,128,128]{3,2,1,0:T(8,128)(2,1)S(1)}, bf16[24,4,128,128]{3,2,1,0:T(8,128)(2,1)S(1)}, u32[]{:S(2)}, u32[]{:S(2)}) collective-permute-start(bf16[24,4,128,128]{3,2,1,0:T(8,128)(2,1)S(1)} %get-tuple-element.52), channel_id=1, source_target_pairs={{0,4},{1,5},{2,6},{3,7},{4,0},{5,1},{6,2},{7,3},{8,12},{9,13},{10,... | collective-permute-start | bytes 9437192 | tf_op jit(solution)/shard_map/ppermute | solution.py:21
  10.9 137.4 %collective-permute-start.9 = (bf16[48,4,128,128]{3,2,1,0:T(8,128)(2,1)}, bf16[48,4,128,128]{3,2,1,0:T(8,128)(2,1)}, u32[]{:S(2)}, u32[]{:S(2)}) collective-permute-start(bf16[48,4,128,128]{3,2,1,0:T(8,128)(2,1)} %refs_0_.5), channel_id=1, source_target_pairs={{0,2},{1,3},{2,0},{3,1},{4,6},{5,7},{6,4},{7,5},{8,10},{9,11},{10,... | collective-permute-start | bytes 18874376 | tf_op jit(solution)/shard_map/ppermute | solution.py:21
  12.4 72.1 %collective-permute-start.7 = (bf16[24,128,384]{2,1,0:T(8,128)(2,1)}, bf16[24,128,384]{2,1,0:T(8,128)(2,1)}, u32[]{:S(2)}, u32[]{:S(2)}) collective-permute-start(bf16[24,128,384]{2,1,0:T(8,128)(2,1)} %get-tuple-element.56), channel_id=1, source_target_pairs={{4,8},{5,9},{6,10},{7,11},{8,4},{9,5},{10,6},{11,7},{20,24},{21,25... | collective-permute-start | bytes 7077896 | tf_op jit(solution)/shard_map/ppermute | solution.py:21
  78.2 53.4 %collective-permute-start.3 = (bf16[24,128,384]{2,1,0:T(8,128)(2,1)S(1)}, bf16[24,128,384]{2,1,0:T(8,128)(2,1)}, u32[]{:S(2)}, u32[]{:S(2)}) collective-permute-start(bf16[24,128,384]{2,1,0:T(8,128)(2,1)S(1)} %get-tuple-element.53), channel_id=1, source_target_pairs={{0,4},{1,5},{2,6},{3,7},{12,8},{13,9},{14,10},{15,11},{16,20},{17,... | collective-permute-start | bytes 7077896 | tf_op jit(solution)/shard_map/ppermute | solution.py:21
  83.2 53.9 %collective-permute-start.5 = (bf16[24,128,384]{2,1,0:T(8,128)(2,1)S(1)}, bf16[24,128,384]{2,1,0:T(8,128)(2,1)}, u32[]{:S(2)}, u32[]{:S(2)}) collective-permute-start(bf16[24,128,384]{2,1,0:T(8,128)(2,1)S(1)} %collective-permute-done.4), channel_id=1, source_target_pairs={{4,0},{5,1},{6,2},{7,3},{8,12},{9,13},{10,14},{11,15},{20,16},{21,... | collective-permute-start | bytes 7077896 | tf_op jit(solution)/shard_map/ppermute | solution.py:21
  131.5 21.5 %collective-permute-start.12 = (bf16[24,128,384]{2,1,0:T(8,128)(2,1)}, bf16[24,128,384]{2,1,0:T(8,128)(2,1)}, u32[]{:S(2)}, u32[]{:S(2)}) collective-permute-start(bf16[24,128,384]{2,1,0:T(8,128)(2,1)} %collective-permute-done.3), channel_id=1, source_target_pairs={{4,8},{5,9},{6,10},{7,11},{8,4},{9,5},{10,6},{11,7},{20,24},{21,25... | collective-permute-start | bytes 7077896 | tf_op jit(solution)/shard_map/ppermute | solution.py:21
  137.2 51.2 %collective-permute-start.6 = (bf16[24,128,384]{2,1,0:T(8,128)(2,1)}, bf16[24,128,384]{2,1,0:T(8,128)(2,1)}, u32[]{:S(2)}, u32[]{:S(2)}) collective-permute-start(bf16[24,128,384]{2,1,0:T(8,128)(2,1)} %get-tuple-element.56), channel_id=1, source_target_pairs={{0,4},{1,5},{2,6},{3,7},{12,8},{13,9},{14,10},{15,11},{16,20},{17,... | collective-permute-start | bytes 7077896 | tf_op jit(solution)/shard_map/ppermute | solution.py:21
  140.9 64.4 %collective-permute-start.8 = (bf16[24,128,384]{2,1,0:T(8,128)(2,1)}, bf16[24,128,384]{2,1,0:T(8,128)(2,1)}, u32[]{:S(2)}, u32[]{:S(2)}) collective-permute-start(bf16[24,128,384]{2,1,0:T(8,128)(2,1)} %collective-permute-done.7), channel_id=1, source_target_pairs={{4,0},{5,1},{6,2},{7,3},{8,12},{9,13},{10,14},{11,15},{20,16},{21,... | collective-permute-start | bytes 7077896 | tf_op jit(solution)/shard_map/ppermute | solution.py:21
  145.5 45.3 %collective-permute-start = (bf16[12,128,384]{2,1,0:T(8,128)(2,1)}, bf16[12,128,384]{2,1,0:T(8,128)(2,1)}, u32[]{:S(2)}, u32[]{:S(2)}) collective-permute-start(bf16[12,128,384]{2,1,0:T(8,128)(2,1)} %get-tuple-element.112), channel_id=1, source_target_pairs={{0,1},{1,0},{2,3},{3,2},{4,5},{5,4},{6,7},{7,6},{8,9},{9,8},{10,11... | collective-permute-start | bytes 3538952 | tf_op jit(solution)/shard_map/ppermute | solution.py:21
  148.2 57.1 %collective-permute-start.10 = (bf16[12,4,128,128]{3,2,1,0:T(8,128)(2,1)}, bf16[12,4,128,128]{3,2,1,0:T(8,128)(2,1)}, u32[]{:S(2)}, u32[]{:S(2)}) collective-permute-start(bf16[12,4,128,128]{3,2,1,0:T(8,128)(2,1)} %get-tuple-element.58), channel_id=1, source_target_pairs={{0,2},{1,3},{2,0},{3,1},{4,6},{5,7},{6,4},{7,5},{8,10},{9,11},{10,... | collective-permute-start | bytes 4718600 | tf_op jit(solution)/shard_map/ppermute | solution.py:21
  153.0 37.8 %collective-permute-start.1 = (bf16[12,128,384]{2,1,0:T(8,128)(2,1)}, bf16[12,128,384]{2,1,0:T(8,128)(2,1)}, u32[]{:S(2)}, u32[]{:S(2)}) collective-permute-start(bf16[12,128,384]{2,1,0:T(8,128)(2,1)} %get-tuple-element.110), channel_id=1, source_target_pairs={{0,1},{1,0},{2,3},{3,2},{4,5},{5,4},{6,7},{7,6},{8,9},{9,8},{10,11... | collective-permute-start | bytes 3538952 | tf_op jit(solution)/shard_map/ppermute | solution.py:21
  188.4 63.8 %collective-permute-start.13 = (bf16[24,128,384]{2,1,0:T(8,128)(2,1)}, bf16[24,128,384]{2,1,0:T(8,128)(2,1)}, u32[]{:S(2)}, u32[]{:S(2)}) collective-permute-start(bf16[24,128,384]{2,1,0:T(8,128)(2,1)} %collective-permute-done.6), channel_id=1, source_target_pairs={{4,8},{5,9},{6,10},{7,11},{8,4},{9,5},{10,6},{11,7},{20,24},{21,25... | collective-permute-start | bytes 7077896 | tf_op jit(solution)/shard_map/ppermute | solution.py:21
  205.3 45.3 %collective-permute-start.11 = (bf16[15,4,128,128]{3,2,1,0:T(8,128)(2,1)}, bf16[15,4,128,128]{3,2,1,0:T(8,128)(2,1)}, u32[]{:S(2)}, u32[]{:S(2)}) collective-permute-start(bf16[15,4,128,128]{3,2,1,0:T(8,128)(2,1)} %slice.43), channel_id=1, source_target_pairs={{0,4},{1,5},{2,6},{3,7},{4,0},{5,1},{6,2},{7,3},{8,12},{9,13},{10,... | collective-permute-start | bytes 5898248 | tf_op jit(solution)/shard_map/ppermute | solution.py:21
  208.4 35.3 %collective-permute-start.16 = (bf16[12,4,128,128]{3,2,1,0:T(8,128)(2,1)}, bf16[12,4,128,128]{3,2,1,0:T(8,128)(2,1)}, u32[]{:S(2)}, u32[]{:S(2)}) collective-permute-start(bf16[12,4,128,128]{3,2,1,0:T(8,128)(2,1)} %get-tuple-element.64), channel_id=1, source_target_pairs={{0,2},{1,3},{2,0},{3,1},{4,6},{5,7},{6,4},{7,5},{8,10},{9,11},{10,... | collective-permute-start | bytes 4718600 | tf_op jit(solution)/shard_map/ppermute | solution.py:21
  250.7 43.3 %collective-permute-start.25 = (bf16[15,4,128,128]{3,2,1,0:T(8,128)(2,1)}, bf16[15,4,128,128]{3,2,1,0:T(8,128)(2,1)S(1)}, u32[]{:S(2)}, u32[]{:S(2)}) collective-permute-start(bf16[15,4,128,128]{3,2,1,0:T(8,128)(2,1)} %collective-permute-done.11.refs_2_), channel_id=1, source_target_pairs={{0,2},{1,3},{2,0},{3,1},{4,6},{5,7},{6,4},{7,5},{8,10},{9,11},{10,... | collective-permute-start | bytes 5898248 | tf_op jit(solution)/shard_map/ppermute | solution.py:21
  255.3 2.9 collective-permute-start.15
  255.7 4.3 %collective-permute-start.14 = (bf16[12,128,384]{2,1,0:T(8,128)(2,1)S(1)}, bf16[12,128,384]{2,1,0:T(8,128)(2,1)S(1)}, u32[]{:S(2)}, u32[]{:S(2)}) collective-permute-start(bf16[12,128,384]{2,1,0:T(8,128)(2,1)S(1)} %get-tuple-element.108), channel_id=1, source_target_pairs={{0,1},{1,0},{2,3},{3,2},{4,5},{5,4},{6,7},{7,6},{8,9},{9,8},{10,11... | collective-permute-start | bytes 3538952 | tf_op jit(solution)/shard_map/ppermute | solution.py:21
  256.2 56.0 %collective-permute-start.31 = (bf16[18,4,128,128]{3,2,1,0:T(8,128)(2,1)}, bf16[18,4,128,128]{3,2,1,0:T(8,128)(2,1)}, u32[]{:S(2)}, u32[]{:S(2)}) collective-permute-start(bf16[18,4,128,128]{3,2,1,0:T(8,128)(2,1)} %pad_maximum_fusion), channel_id=1, source_target_pairs={{0,4},{1,5},{2,6},{3,7},{4,0},{5,1},{6,2},{7,3},{8,12},{9,13},{10,... | collective-permute-start | bytes 7077896 | tf_op jit(solution)/shard_map/ppermute | solution.py:21
  280.7 13.2 %collective-permute-start.17 = (f32[3,128,384]{2,1,0:T(8,128)S(1)}, f32[3,128,384]{2,1,0:T(8,128)S(1)}, u32[]{:S(2)}, u32[]{:S(2)}) collective-permute-start(f32[3,128,384]{2,1,0:T(8,128)S(1)} %get-tuple-element.66), channel_id=1, source_target_pairs={{0,1},{1,0},{2,3},{3,2},{4,5},{5,4},{6,7},{7,6},{8,9},{9,8},{10,11... | collective-permute-start | bytes 1769480 | tf_op jit(solution)/shard_map/ppermute | solution.py:21
  280.9 13.6 %collective-permute-start.18 = (f32[3,128,384]{2,1,0:T(8,128)S(1)}, f32[3,128,384]{2,1,0:T(8,128)S(1)}, u32[]{:S(2)}, u32[]{:S(2)}) collective-permute-start(f32[3,128,384]{2,1,0:T(8,128)S(1)} %get-tuple-element.67), channel_id=1, source_target_pairs={{0,1},{1,0},{2,3},{3,2},{4,5},{5,4},{6,7},{7,6},{8,9},{9,8},{10,11... | collective-permute-start | bytes 1769480 | tf_op jit(solution)/shard_map/ppermute | solution.py:21
  281.3 13.3 %collective-permute-start.19 = (f32[3,128,384]{2,1,0:T(8,128)S(1)}, f32[3,128,384]{2,1,0:T(8,128)S(1)}, u32[]{:S(2)}, u32[]{:S(2)}) collective-permute-start(f32[3,128,384]{2,1,0:T(8,128)S(1)} %get-tuple-element.68), channel_id=1, source_target_pairs={{0,1},{1,0},{2,3},{3,2},{4,5},{5,4},{6,7},{7,6},{8,9},{9,8},{10,11... | collective-permute-start | bytes 1769480 | tf_op jit(solution)/shard_map/ppermute | solution.py:21
  293.9 14.8 %collective-permute-start.21 = (f32[3,128,384]{2,1,0:T(8,128)S(1)}, f32[3,128,384]{2,1,0:T(8,128)S(1)}, u32[]{:S(2)}, u32[]{:S(2)}) collective-permute-start(f32[3,128,384]{2,1,0:T(8,128)S(1)} %get-tuple-element.70), channel_id=1, source_target_pairs={{0,1},{1,0},{2,3},{3,2},{4,5},{5,4},{6,7},{7,6},{8,9},{9,8},{10,11... | collective-permute-start | bytes 1769480 | tf_op jit(solution)/shard_map/ppermute | solution.py:21
  294.5 14.8 %collective-permute-start.22 = (f32[3,128,384]{2,1,0:T(8,128)S(1)}, f32[3,128,384]{2,1,0:T(8,128)S(1)}, u32[]{:S(2)}, u32[]{:S(2)}) collective-permute-start(f32[3,128,384]{2,1,0:T(8,128)S(1)} %get-tuple-element.71), channel_id=1, source_target_pairs={{0,1},{1,0},{2,3},{3,2},{4,5},{5,4},{6,7},{7,6},{8,9},{9,8},{10,11... | collective-permute-start | bytes 1769480 | tf_op jit(solution)/shard_map/ppermute | solution.py:21
  294.5 14.8 %collective-permute-start.23 = (f32[3,128,384]{2,1,0:T(8,128)S(1)}, f32[3,128,384]{2,1,0:T(8,128)S(1)}, u32[]{:S(2)}, u32[]{:S(2)}) collective-permute-start(f32[3,128,384]{2,1,0:T(8,128)S(1)} %get-tuple-element.72), channel_id=1, source_target_pairs={{0,1},{1,0},{2,3},{3,2},{4,5},{5,4},{6,7},{7,6},{8,9},{9,8},{10,11... | collective-permute-start | bytes 1769480 | tf_op jit(solution)/shard_map/ppermute | solution.py:21
  295.9 13.8 %collective-permute-start.24 = (f32[3,128,384]{2,1,0:T(8,128)S(1)}, f32[3,128,384]{2,1,0:T(8,128)S(1)}, u32[]{:S(2)}, u32[]{:S(2)}) collective-permute-start(f32[3,128,384]{2,1,0:T(8,128)S(1)} %get-tuple-element.73), channel_id=1, source_target_pairs={{0,1},{1,0},{2,3},{3,2},{4,5},{5,4},{6,7},{7,6},{8,9},{9,8},{10,11... | collective-permute-start | bytes 1769480 | tf_op jit(solution)/shard_map/ppermute | solution.py:21
  308.8 3.0 collective-permute-start.26
  309.2 11.3 %collective-permute-start.27 = (f32[3,128,384]{2,1,0:T(8,128)S(1)}, f32[3,128,384]{2,1,0:T(8,128)S(1)}, u32[]{:S(2)}, u32[]{:S(2)}) collective-permute-start(f32[3,128,384]{2,1,0:T(8,128)S(1)} %get-tuple-element.78), channel_id=1, source_target_pairs={{0,1},{1,0},{2,3},{3,2},{4,5},{5,4},{6,7},{7,6},{8,9},{9,8},{10,11... | collective-permute-start | bytes 1769480 | tf_op jit(solution)/shard_map/ppermute | solution.py:21
  309.4 11.6 %collective-permute-start.28 = (f32[3,128,384]{2,1,0:T(8,128)S(1)}, f32[3,128,384]{2,1,0:T(8,128)S(1)}, u32[]{:S(2)}, u32[]{:S(2)}) collective-permute-start(f32[3,128,384]{2,1,0:T(8,128)S(1)} %get-tuple-element.79), channel_id=1, source_target_pairs={{0,1},{1,0},{2,3},{3,2},{4,5},{5,4},{6,7},{7,6},{8,9},{9,8},{10,11... | collective-permute-start | bytes 1769480 | tf_op jit(solution)/shard_map/ppermute | solution.py:21
  309.7 11.3 %collective-permute-start.29 = (f32[3,128,384]{2,1,0:T(8,128)S(1)}, f32[3,128,384]{2,1,0:T(8,128)S(1)}, u32[]{:S(2)}, u32[]{:S(2)}) collective-permute-start(f32[3,128,384]{2,1,0:T(8,128)S(1)} %get-tuple-element.80), channel_id=1, source_target_pairs={{0,1},{1,0},{2,3},{3,2},{4,5},{5,4},{6,7},{7,6},{8,9},{9,8},{10,11... | collective-permute-start | bytes 1769480 | tf_op jit(solution)/shard_map/ppermute | solution.py:21
  311.8 9.3 %collective-permute-start.30 = (f32[3,128,384]{2,1,0:T(8,128)S(1)}, f32[3,128,384]{2,1,0:T(8,128)S(1)}, u32[]{:S(2)}, u32[]{:S(2)}) collective-permute-start(f32[3,128,384]{2,1,0:T(8,128)S(1)} %get-tuple-element.81), channel_id=1, source_target_pairs={{0,1},{1,0},{2,3},{3,2},{4,5},{5,4},{6,7},{7,6},{8,9},{9,8},{10,11... | collective-permute-start | bytes 1769480 | tf_op jit(solution)/shard_map/ppermute | solution.py:21
  320.9 3.2 collective-permute-start.34
  325.1 4.7 %collective-permute-start.35 = (f32[8,384]{1,0:T(8,128)S(1)}, f32[8,384]{1,0:T(8,128)S(1)}, u32[]{:S(2)}, u32[]{:S(2)}) collective-permute-start(f32[8,384]{1,0:T(8,128)S(1)} %get-tuple-element.91.sums_ref), channel_id=1, source_target_pairs={{0,8},{1,9},{2,10},{3,11},{4,12},{5,13},{6,14},{7,15},{8,0},{9,1},... | collective-permute-start | bytes 36872 | tf_op jit(solution)/shard_map/ppermute | solution.py:21
  (12 other events, 102.3 us)

commit v7 on v6

--- a/solution.py
+++ b/solution.py
@@ -369,12 +369,15 @@
         crossed = [swapped(panel[0], across, inner)]
         crossed.append(swapped(after(panel[1], crossed[0]), across, inner))
         inward, outward = [], []
+        middle_rows = tile_values[one:two]
+        early = [near, middle_rows]
         for got, piece in zip(crossed, panel):
-            ready = from_z + inward + outward
+            ready = from_z + inward + outward + (early if inward else [])
             inward.append(swapped(after(piece, *ready), 4, outer))
             outward.append(swapped(after(got, *ready), 4, inner))
         returned = [swapped(after(inward[0], crossed[1]), across, inner)]
-        returned.append(swapped(after(inward[1], returned[0]), across, inner))
+        last = jnp.concatenate([from_x[two:], tile_values[two:]])
+        returned.append(swapped(after(inward[1], returned[0], last), across, inner))
         is_inner = inner(device)
         kept, received = [], []
         for a, b in zip(returned, outward):
@@ -391,13 +394,13 @@
         near = pack(where, 0, panels, others)
         far = pack(where, half // 2, panels, others)
         tied = []
+        middle_rows = tile_values[one:two]
+        last = jnp.concatenate([from_x[two:], tile_values[two:]])
     from_xz = [swapped(after(from_z[0][:few], from_x), 2)]
     if few < one:
         from_xz.append(swapped(after(from_z[0][few:], from_xz[0]), 2))
-    later = after(tile_values, near)
-    last = jnp.concatenate([from_x[two:], later[two:]])
     tied = tied + [from_xz[0], last, keep, index]
-    from_z.append(swapped(after(later[one:two], *tied), 4))
+    from_z.append(swapped(after(middle_rows, *tied), 4))
     last = swapped(after(last, from_z[1], from_xz[-1]), 4)
     from_xz.append(swapped(after(from_z[1], from_xz[-1]), 2))
 

time: 335 us -> 323 us (0.964)
  waiting for transfers between devices: 211 us -> 188 us
  local copies, waits for them, and re-layouts: 13.9 us -> 20.3 us
    ppermute x36, waiting for transfers between devices: 211 us -> 188 us  [swapped(): return lax.ppermute(array, 'grid', pairs)]
    unnamed x17 -> x25, local copies, waits for them, and re-layouts: 4.83 us -> 10.2 us
  transfers between devices with their start and end apart: 36 -> 36, of which waited for: 14 -> 13; matrix products, arithmetic and copies ran while one was open for 6% -> 7% of each run, Pallas kernels for 14% -> 14%
where the time goes in v7:
time: 323 us; the launch traced here: 322 us
  waiting for transfers between devices  188 us (58%)
  Pallas kernels  60.4 us (19%)
  starting transfers between devices  40.8 us (13%)
  local copies, waits for them, and re-layouts  20.3 us (6%)
  other arithmetic  13.1 us (4%)
    ppermute x36, waiting for transfers between devices, swapped(): return lax.ppermute(array, 'grid', pairs)  188 us
    ppermute x36, starting transfers between devices, swapped(): return lax.ppermute(array, 'grid', pairs)  40.8 us
    pallas_call x3, Pallas kernels, expand(): pl.pallas_call(functools.partial(expand_kernel, first, plan), out_shape=[...  40.2 us
    unnamed x25, local copies, waits for them, and re-layouts  10.2 us
    pallas_call x1, Pallas kernels, make_panel(): pl.pallas_call(functools.partial(panel_kernel, first_steps), grid_spec=pl...  7.99 us
    select_n x4, other arithmetic, shared(): given = [jnp.where(odd, a, b) for a, b in zip(pieces[::2], pieces[1::2])]  6.64 us
  transfers between devices with their start and end apart: 36, of which 13 were waited for; matrix products, arithmetic and copies ran while one was open for 7% of the time, Pallas kernels for 14%

profile of v7, /device:TPU:0, one launch (start us, length us, event | category | flops | bytes accessed | tf_op | source)
XLA Modules:
  0.0 322.5 jit_solution(12770350963686478941)
XLA Ops:
  1.0 8.0 %panel.1 = (bf16[24,4,128,128]{3,2,1,0:T(8,128)(2,1)}, bf16[24,128,384]{2,1,0:T(8,128)(2,1)}, bf16[24,128,384]{2,1,0:T(8,128)(2,1)}) custom-call(s32[144]{0:T(256)S(1)} %reshape.159.slot_ref, bf16[48,4,128,128]{3,2,1,0:T(8,128)(2,1)} %refs_0_.5), custom_call_target="tpu_custom_call" | custom-call | bytes 1024 | tf_op jit(solution)/shard_map/panel/pallas_call | solution.py:68
  9.0 3.0 collective-permute-start
  13.5 2.0 collective-permute-start.2
  15.5 2.9 broadcast_select_fusion.6
  18.5 2.1 collective-permute-start.7
  20.6 59.7 %collective-permute-done.refs_2_ = bf16[24,4,128,128]{3,2,1,0:T(8,128)(2,1)S(1)} collective-permute-done((bf16[24,4,128,128]{3,2,1,0:T(8,128)(2,1)}, bf16[24,4,128,128]{3,2,1,0:T(8,128)(2,1)S(1)}, u32[]{:S(2)}, u32[]{:S(2)}) %collective-permute-start) | collective-permute-done | bytes 3145760 | tf_op jit(solution)/shard_map/ppermute | solution.py:21
  80.3 5.1 %collective-permute-start.1 = (bf16[24,128,384]{2,1,0:T(8,128)(2,1)}, bf16[24,128,384]{2,1,0:T(8,128)(2,1)}, u32[]{:S(2)}, u32[]{:S(2)}) collective-permute-start(bf16[24,128,384]{2,1,0:T(8,128)(2,1)} %get-tuple-element.51), channel_id=1, source_target_pairs={{0,4},{1,5},{2,6},{3,7},{12,8},{13,9},{14,10},{15,11},{16,20},{17,... | collective-permute-start | bytes 7077896 | tf_op jit(solution)/shard_map/ppermute | solution.py:21
  86.7 3.3 %broadcast_select_fusion.7 = (bf16[12,128,384]{2,1,0:T(8,128)(2,1)}, bf16[12,128,384]{2,1,0:T(8,128)(2,1)}) fusion(pred[]{:T(512)S(6)} %eq.31, bf16[24,128,384]{2,1,0:T(8,128)(2,1)} %get-tuple-element.51), kind=kLoop, calls=%fused_computation.9 | loop fusion | flops 1179648 | bytes 4718593 | tf_op jit(solution)/shard_map/jit(_where)/select_n | solution.py:355
  91.1 3.0 slice.39
  98.1 2.0 pack.2.near_ref
  100.1 2.2 copy-done
  102.3 31.7 %collective-permute-done.1 = bf16[24,128,384]{2,1,0:T(8,128)(2,1)} collective-permute-done((bf16[24,128,384]{2,1,0:T(8,128)(2,1)}, bf16[24,128,384]{2,1,0:T(8,128)(2,1)}, u32[]{:S(2)}, u32[]{:S(2)}) %collective-permute-start.1) | collective-permute-done | bytes 2359328 | tf_op jit(solution)/shard_map/ppermute | solution.py:21
  134.0 2.1 collective-permute-start.12
  136.1 3.4 %collective-permute-done.3 = bf16[24,128,384]{2,1,0:T(8,128)(2,1)} collective-permute-done((bf16[24,128,384]{2,1,0:T(8,128)(2,1)}, bf16[24,128,384]{2,1,0:T(8,128)(2,1)}, u32[]{:S(2)}, u32[]{:S(2)}) %collective-permute-start.3) | collective-permute-done | bytes 2359328 | tf_op jit(solution)/shard_map/ppermute | solution.py:21
  139.5 3.7 %collective-permute-start.6 = (bf16[24,128,384]{2,1,0:T(8,128)(2,1)}, bf16[24,128,384]{2,1,0:T(8,128)(2,1)}, u32[]{:S(2)}, u32[]{:S(2)}) collective-permute-start(bf16[24,128,384]{2,1,0:T(8,128)(2,1)} %get-tuple-element.54), channel_id=1, source_target_pairs={{0,4},{1,5},{2,6},{3,7},{12,8},{13,9},{14,10},{15,11},{16,20},{17,... | collective-permute-start | bytes 7077896 | tf_op jit(solution)/shard_map/ppermute | solution.py:21
  146.4 2.9 collective-permute-done.9.refs_1_
  150.8 2.4 slice.46
  157.4 33.4 %collective-permute-done.6 = bf16[24,128,384]{2,1,0:T(8,128)(2,1)} collective-permute-done((bf16[24,128,384]{2,1,0:T(8,128)(2,1)}, bf16[24,128,384]{2,1,0:T(8,128)(2,1)}, u32[]{:S(2)}, u32[]{:S(2)}) %collective-permute-start.6) | collective-permute-done | bytes 2359328 | tf_op jit(solution)/shard_map/ppermute | solution.py:21
  190.7 2.1 collective-permute-start.13
  193.2 3.3 %collective-permute-done.8 = bf16[24,128,384]{2,1,0:T(8,128)(2,1)} collective-permute-done((bf16[24,128,384]{2,1,0:T(8,128)(2,1)}, bf16[24,128,384]{2,1,0:T(8,128)(2,1)}, u32[]{:S(2)}, u32[]{:S(2)}) %collective-permute-start.8) | collective-permute-done | bytes 2359328 | tf_op jit(solution)/shard_map/ppermute | solution.py:21
  198.1 1.9 broadcast_select_fusion.1
  200.3 29.2 %collective-permute-done.16.refs_4_ = bf16[12,4,128,128]{3,2,1,0:T(8,128)(2,1)} collective-permute-done((bf16[12,4,128,128]{3,2,1,0:T(8,128)(2,1)}, bf16[12,4,128,128]{3,2,1,0:T(8,128)(2,1)}, u32[]{:S(2)}, u32[]{:S(2)}) %collective-permute-start.16) | collective-permute-done | bytes 1572896 | tf_op jit(solution)/shard_map/ppermute | solution.py:21
  229.5 8.8 %collective-permute-done.11.refs_2_ = bf16[15,4,128,128]{3,2,1,0:T(8,128)(2,1)} collective-permute-done((bf16[15,4,128,128]{3,2,1,0:T(8,128)(2,1)}, bf16[15,4,128,128]{3,2,1,0:T(8,128)(2,1)}, u32[]{:S(2)}, u32[]{:S(2)}) %collective-permute-start.11) | collective-permute-done | bytes 1966112 | tf_op jit(solution)/shard_map/ppermute | solution.py:21
  239.8 1.9 broadcast_select_fusion
  242.1 5.7 %collective-permute-start.31 = (bf16[18,4,128,128]{3,2,1,0:T(8,128)(2,1)}, bf16[18,4,128,128]{3,2,1,0:T(8,128)(2,1)}, u32[]{:S(2)}, u32[]{:S(2)}) collective-permute-start(bf16[18,4,128,128]{3,2,1,0:T(8,128)(2,1)} %pad_maximum_fusion), channel_id=1, source_target_pairs={{0,4},{1,5},{2,6},{3,7},{4,0},{5,1},{6,2},{7,3},{8,12},{9,13},{10,... | collective-permute-start | bytes 7077896 | tf_op jit(solution)/shard_map/ppermute | solution.py:21
  249.1 19.5 %expand.3 = (f32[24,128,384]{2,1,0:T(8,128)S(1)}, f32[3,128,384]{2,1,0:T(8,128)S(1)}, f32[3,128,384]{2,1,0:T(8,128)S(1)}, f32[3,128,384]{2,1,0:T(8,128)S(1)}, f3...) custom-call(s32[4]{0:T(128)S(1)} %iota_xor_fusion.order_ref, ...), custom_call_target="tpu_custom_call" | custom-call | bytes 1024 | tf_op jit(solution)/shard_map/expand/pallas_call | solution.py:209
  269.4 9.7 %collective-permute-done.25.refs_3_ = bf16[15,4,128,128]{3,2,1,0:T(8,128)(2,1)S(1)} collective-permute-done((bf16[15,4,128,128]{3,2,1,0:T(8,128)(2,1)}, bf16[15,4,128,128]{3,2,1,0:T(8,128)(2,1)S(1)}, u32[]{:S(2)}, u32[]{:S(2)}) %collective-permute-start.25) | collective-permute-done | bytes 1966112 | tf_op jit(solution)/shard_map/ppermute | solution.py:21
  284.1 12.6 %expand.4 = (f32[15,128,384]{2,1,0:T(8,128)S(1)}, f32[3,128,384]{2,1,0:T(8,128)S(1)}, f32[3,128,384]{2,1,0:T(8,128)}, f32[3,128,384]{2,1,0:T(8,128)}, f32[3,128,...) custom-call(s32[4]{0:T(128)S(1)} %iota_xor_fusion.order_ref, s32[768]{0:T(1024)S(1)} %add.105.index_ref, ...), custom_call_target="tpu_custom_call" | custom-call | bytes 1024 | tf_op jit(solution)/shard_map/expand/pallas_call | solution.py:209
  300.1 8.1 %expand.5 = (f32[9,128,384]{2,1,0:T(8,128)S(1)}, f32[3,128,384]{2,1,0:T(8,128)S(1)}, f32[3,128,384]{2,1,0:T(8,128)S(1)}, f32[3,128,384]{2,1,0:T(8,128)S(1)}) custom-call(s32[4]{0:T(128)S(1)} %iota_xor_fusion.order_ref, s32[768]{0:T(1024)S(1)} %add.105.index_ref, bf16[24,128,768]{2,1,0:T(8,128)(2,1)S(1)} %bitcast.9, bf16[24,128,768]{2,1,0:T(8,128)(2,1)S(1)} %pack.3.far_ref, ...), custom_call_target="tpu_custom_call" | custom-call | bytes 1024 | tf_op jit(solution)/shard_map/expand/pallas_call | solution.py:209
  313.0 2.0 collective-permute-start.35
  315.0 2.6 collective-permute-done.35.got_ref
  317.7 4.8 %scale.1 = f32[48,3,128,128]{3,2,1,0:T(8,128)} custom-call(f32[8,384]{1,0:T(8,128)S(1)} %get-tuple-element.89.sums_ref, f32[8,384]{1,0:T(8,128)S(1)} %collective-permute-done.35.got_ref, f32[48,128,384]{2,1,0:T(8,128)S(1)} %get-tuple-element.90.squared_ref), custom_call_target="tpu_custom_call" | custom-call | bytes 1024 | tf_op jit(solution)/shard_map/scale/pallas_call | solution.py:298
  (106 shorter events, 36.7 us)
Async XLA Ops:
  9.0 71.3 %collective-permute-start = (bf16[24,4,128,128]{3,2,1,0:T(8,128)(2,1)}, bf16[24,4,128,128]{3,2,1,0:T(8,128)(2,1)S(1)}, u32[]{:S(2)}, u32[]{:S(2)}) collective-permute-start(bf16[24,4,128,128]{3,2,1,0:T(8,128)(2,1)} %get-tuple-element.49), channel_id=1, source_target_pairs={{0,4},{1,5},{2,6},{3,7},{4,0},{5,1},{6,2},{7,3},{8,12},{9,13},{10,... | collective-permute-start | bytes 9437192 | tf_op jit(solution)/shard_map/ppermute | solution.py:21
  12.0 137.3 %collective-permute-start.9 = (bf16[48,4,128,128]{3,2,1,0:T(8,128)(2,1)}, bf16[48,4,128,128]{3,2,1,0:T(8,128)(2,1)}, u32[]{:S(2)}, u32[]{:S(2)}) collective-permute-start(bf16[48,4,128,128]{3,2,1,0:T(8,128)(2,1)} %refs_0_.5), channel_id=1, source_target_pairs={{0,2},{1,3},{2,0},{3,1},{4,6},{5,7},{6,4},{7,5},{8,10},{9,11},{10,... | collective-permute-start | bytes 18874376 | tf_op jit(solution)/shard_map/ppermute | solution.py:21
  13.5 5.0 %collective-permute-start.2 = (bf16[24,128,384]{2,1,0:T(8,128)(2,1)}, bf16[24,128,384]{2,1,0:T(8,128)(2,1)}, u32[]{:S(2)}, u32[]{:S(2)}) collective-permute-start(bf16[24,128,384]{2,1,0:T(8,128)(2,1)} %get-tuple-element.51), channel_id=1, source_target_pairs={{4,8},{5,9},{6,10},{7,11},{8,4},{9,5},{10,6},{11,7},{20,24},{21,25... | collective-permute-start | bytes 7077896 | tf_op jit(solution)/shard_map/ppermute | solution.py:21
  18.5 71.5 %collective-permute-start.5 = (bf16[12,128,384]{2,1,0:T(8,128)(2,1)S(1)}, bf16[12,128,384]{2,1,0:T(8,128)(2,1)S(1)}, u32[]{:S(2)}, u32[]{:S(2)}) collective-permute-start(bf16[12,128,384]{2,1,0:T(8,128)(2,1)S(1)} %get-tuple-element.108), channel_id=1, source_target_pairs={{0,1},{1,0},{2,3},{3,2},{4,5},{5,4},{6,7},{7,6},{8,9},{9,8},{10,11... | collective-permute-start | bytes 3538952 | tf_op jit(solution)/shard_map/ppermute | solution.py:21
  18.5 83.8 %collective-permute-start.7 = (bf16[24,128,384]{2,1,0:T(8,128)(2,1)}, bf16[24,128,384]{2,1,0:T(8,128)(2,1)}, u32[]{:S(2)}, u32[]{:S(2)}) collective-permute-start(bf16[24,128,384]{2,1,0:T(8,128)(2,1)} %get-tuple-element.54), channel_id=1, source_target_pairs={{4,8},{5,9},{6,10},{7,11},{8,4},{9,5},{10,6},{11,7},{20,24},{21,25... | collective-permute-start | bytes 7077896 | tf_op jit(solution)/shard_map/ppermute | solution.py:21
  80.3 53.7 %collective-permute-start.1 = (bf16[24,128,384]{2,1,0:T(8,128)(2,1)}, bf16[24,128,384]{2,1,0:T(8,128)(2,1)}, u32[]{:S(2)}, u32[]{:S(2)}) collective-permute-start(bf16[24,128,384]{2,1,0:T(8,128)(2,1)} %get-tuple-element.51), channel_id=1, source_target_pairs={{0,4},{1,5},{2,6},{3,7},{12,8},{13,9},{14,10},{15,11},{16,20},{17,... | collective-permute-start | bytes 7077896 | tf_op jit(solution)/shard_map/ppermute | solution.py:21
  85.4 54.1 %collective-permute-start.3 = (bf16[24,128,384]{2,1,0:T(8,128)(2,1)}, bf16[24,128,384]{2,1,0:T(8,128)(2,1)}, u32[]{:S(2)}, u32[]{:S(2)}) collective-permute-start(bf16[24,128,384]{2,1,0:T(8,128)(2,1)} %collective-permute-done.2), channel_id=1, source_target_pairs={{4,0},{5,1},{6,2},{7,3},{8,12},{9,13},{10,14},{11,15},{20,16},{21,... | collective-permute-start | bytes 7077896 | tf_op jit(solution)/shard_map/ppermute | solution.py:21
  91.0 3.2 %collective-permute-start.4 = (bf16[12,128,384]{2,1,0:T(8,128)(2,1)}, bf16[12,128,384]{2,1,0:T(8,128)(2,1)}, u32[]{:S(2)}, u32[]{:S(2)}) collective-permute-start(bf16[12,128,384]{2,1,0:T(8,128)(2,1)} %get-tuple-element.110), channel_id=1, source_target_pairs={{0,1},{1,0},{2,3},{3,2},{4,5},{5,4},{6,7},{7,6},{8,9},{9,8},{10,11... | collective-permute-start | bytes 3538952 | tf_op jit(solution)/shard_map/ppermute | solution.py:21
  134.0 23.4 %collective-permute-start.12 = (bf16[24,128,384]{2,1,0:T(8,128)(2,1)}, bf16[24,128,384]{2,1,0:T(8,128)(2,1)}, u32[]{:S(2)}, u32[]{:S(2)}) collective-permute-start(bf16[24,128,384]{2,1,0:T(8,128)(2,1)} %collective-permute-done.1), channel_id=1, source_target_pairs={{4,8},{5,9},{6,10},{7,11},{8,4},{9,5},{10,6},{11,7},{20,24},{21,25... | collective-permute-start | bytes 7077896 | tf_op jit(solution)/shard_map/ppermute | solution.py:21
  139.5 51.2 %collective-permute-start.6 = (bf16[24,128,384]{2,1,0:T(8,128)(2,1)}, bf16[24,128,384]{2,1,0:T(8,128)(2,1)}, u32[]{:S(2)}, u32[]{:S(2)}) collective-permute-start(bf16[24,128,384]{2,1,0:T(8,128)(2,1)} %get-tuple-element.54), channel_id=1, source_target_pairs={{0,4},{1,5},{2,6},{3,7},{12,8},{13,9},{14,10},{15,11},{16,20},{17,... | collective-permute-start | bytes 7077896 | tf_op jit(solution)/shard_map/ppermute | solution.py:21
  143.3 53.3 %collective-permute-start.8 = (bf16[24,128,384]{2,1,0:T(8,128)(2,1)}, bf16[24,128,384]{2,1,0:T(8,128)(2,1)}, u32[]{:S(2)}, u32[]{:S(2)}) collective-permute-start(bf16[24,128,384]{2,1,0:T(8,128)(2,1)} %collective-permute-done.7), channel_id=1, source_target_pairs={{4,0},{5,1},{6,2},{7,3},{8,12},{9,13},{10,14},{11,15},{20,16},{21,... | collective-permute-start | bytes 7077896 | tf_op jit(solution)/shard_map/ppermute | solution.py:21
  149.3 47.3 %collective-permute-start.10 = (bf16[12,4,128,128]{3,2,1,0:T(8,128)(2,1)}, bf16[12,4,128,128]{3,2,1,0:T(8,128)(2,1)}, u32[]{:S(2)}, u32[]{:S(2)}) collective-permute-start(bf16[12,4,128,128]{3,2,1,0:T(8,128)(2,1)} %get-tuple-element.56), channel_id=1, source_target_pairs={{0,2},{1,3},{2,0},{3,1},{4,6},{5,7},{6,4},{7,5},{8,10},{9,11},{10,... | collective-permute-start | bytes 4718600 | tf_op jit(solution)/shard_map/ppermute | solution.py:21
  190.7 49.1 %collective-permute-start.13 = (bf16[24,128,384]{2,1,0:T(8,128)(2,1)}, bf16[24,128,384]{2,1,0:T(8,128)(2,1)}, u32[]{:S(2)}, u32[]{:S(2)}) collective-permute-start(bf16[24,128,384]{2,1,0:T(8,128)(2,1)} %collective-permute-done.6), channel_id=1, source_target_pairs={{4,8},{5,9},{6,10},{7,11},{8,4},{9,5},{10,6},{11,7},{20,24},{21,25... | collective-permute-start | bytes 7077896 | tf_op jit(solution)/shard_map/ppermute | solution.py:21
  196.6 41.8 %collective-permute-start.11 = (bf16[15,4,128,128]{3,2,1,0:T(8,128)(2,1)}, bf16[15,4,128,128]{3,2,1,0:T(8,128)(2,1)}, u32[]{:S(2)}, u32[]{:S(2)}) collective-permute-start(bf16[15,4,128,128]{3,2,1,0:T(8,128)(2,1)} %slice.39), channel_id=1, source_target_pairs={{0,4},{1,5},{2,6},{3,7},{4,0},{5,1},{6,2},{7,3},{8,12},{9,13},{10,... | collective-permute-start | bytes 5898248 | tf_op jit(solution)/shard_map/ppermute | solution.py:21
  196.6 32.9 %collective-permute-start.16 = (bf16[12,4,128,128]{3,2,1,0:T(8,128)(2,1)}, bf16[12,4,128,128]{3,2,1,0:T(8,128)(2,1)}, u32[]{:S(2)}, u32[]{:S(2)}) collective-permute-start(bf16[12,4,128,128]{3,2,1,0:T(8,128)(2,1)} %get-tuple-element.62), channel_id=1, source_target_pairs={{0,2},{1,3},{2,0},{3,1},{4,6},{5,7},{6,4},{7,5},{8,10},{9,11},{10,... | collective-permute-start | bytes 4718600 | tf_op jit(solution)/shard_map/ppermute | solution.py:21
  200.2 47.6 %collective-permute-start.14 = (bf16[12,128,384]{2,1,0:T(8,128)(2,1)S(1)}, bf16[12,128,384]{2,1,0:T(8,128)(2,1)S(1)}, u32[]{:S(2)}, u32[]{:S(2)}) collective-permute-start(bf16[12,128,384]{2,1,0:T(8,128)(2,1)S(1)} %get-tuple-element.106), channel_id=1, source_target_pairs={{0,1},{1,0},{2,3},{3,2},{4,5},{5,4},{6,7},{7,6},{8,9},{9,8},{10,11... | collective-permute-start | bytes 3538952 | tf_op jit(solution)/shard_map/ppermute | solution.py:21
  238.3 40.8 %collective-permute-start.25 = (bf16[15,4,128,128]{3,2,1,0:T(8,128)(2,1)}, bf16[15,4,128,128]{3,2,1,0:T(8,128)(2,1)S(1)}, u32[]{:S(2)}, u32[]{:S(2)}) collective-permute-start(bf16[15,4,128,128]{3,2,1,0:T(8,128)(2,1)} %collective-permute-done.11.refs_2_), channel_id=1, source_target_pairs={{0,2},{1,3},{2,0},{3,1},{4,6},{5,7},{6,4},{7,5},{8,10},{9,11},{10,... | collective-permute-start | bytes 5898248 | tf_op jit(solution)/shard_map/ppermute | solution.py:21
  242.0 5.8 %collective-permute-start.15 = (bf16[12,128,384]{2,1,0:T(8,128)(2,1)S(1)}, bf16[12,128,384]{2,1,0:T(8,128)(2,1)S(1)}, u32[]{:S(2)}, u32[]{:S(2)}) collective-permute-start(bf16[12,128,384]{2,1,0:T(8,128)(2,1)S(1)} %get-tuple-element.104), channel_id=1, source_target_pairs={{0,1},{1,0},{2,3},{3,2},{4,5},{5,4},{6,7},{7,6},{8,9},{9,8},{10,11... | collective-permute-start | bytes 3538952 | tf_op jit(solution)/shard_map/ppermute | solution.py:21
  242.1 58.0 %collective-permute-start.31 = (bf16[18,4,128,128]{3,2,1,0:T(8,128)(2,1)}, bf16[18,4,128,128]{3,2,1,0:T(8,128)(2,1)}, u32[]{:S(2)}, u32[]{:S(2)}) collective-permute-start(bf16[18,4,128,128]{3,2,1,0:T(8,128)(2,1)} %pad_maximum_fusion), channel_id=1, source_target_pairs={{0,4},{1,5},{2,6},{3,7},{4,0},{5,1},{6,2},{7,3},{8,12},{9,13},{10,... | collective-permute-start | bytes 7077896 | tf_op jit(solution)/shard_map/ppermute | solution.py:21
  268.6 11.8 %collective-permute-start.17 = (f32[3,128,384]{2,1,0:T(8,128)S(1)}, f32[3,128,384]{2,1,0:T(8,128)S(1)}, u32[]{:S(2)}, u32[]{:S(2)}) collective-permute-start(f32[3,128,384]{2,1,0:T(8,128)S(1)} %get-tuple-element.64), channel_id=1, source_target_pairs={{0,1},{1,0},{2,3},{3,2},{4,5},{5,4},{6,7},{7,6},{8,9},{9,8},{10,11... | collective-permute-start | bytes 1769480 | tf_op jit(solution)/shard_map/ppermute | solution.py:21
  268.8 12.0 %collective-permute-start.18 = (f32[3,128,384]{2,1,0:T(8,128)S(1)}, f32[3,128,384]{2,1,0:T(8,128)S(1)}, u32[]{:S(2)}, u32[]{:S(2)}) collective-permute-start(f32[3,128,384]{2,1,0:T(8,128)S(1)} %get-tuple-element.65), channel_id=1, source_target_pairs={{0,1},{1,0},{2,3},{3,2},{4,5},{5,4},{6,7},{7,6},{8,9},{9,8},{10,11... | collective-permute-start | bytes 1769480 | tf_op jit(solution)/shard_map/ppermute | solution.py:21
  269.2 11.8 %collective-permute-start.19 = (f32[3,128,384]{2,1,0:T(8,128)S(1)}, f32[3,128,384]{2,1,0:T(8,128)S(1)}, u32[]{:S(2)}, u32[]{:S(2)}) collective-permute-start(f32[3,128,384]{2,1,0:T(8,128)S(1)} %get-tuple-element.66), channel_id=1, source_target_pairs={{0,1},{1,0},{2,3},{3,2},{4,5},{5,4},{6,7},{7,6},{8,9},{9,8},{10,11... | collective-permute-start | bytes 1769480 | tf_op jit(solution)/shard_map/ppermute | solution.py:21
  280.4 16.3 %collective-permute-start.21 = (f32[3,128,384]{2,1,0:T(8,128)S(1)}, f32[3,128,384]{2,1,0:T(8,128)S(1)}, u32[]{:S(2)}, u32[]{:S(2)}) collective-permute-start(f32[3,128,384]{2,1,0:T(8,128)S(1)} %get-tuple-element.68), channel_id=1, source_target_pairs={{0,1},{1,0},{2,3},{3,2},{4,5},{5,4},{6,7},{7,6},{8,9},{9,8},{10,11... | collective-permute-start | bytes 1769480 | tf_op jit(solution)/shard_map/ppermute | solution.py:21
  280.9 16.2 %collective-permute-start.22 = (f32[3,128,384]{2,1,0:T(8,128)S(1)}, f32[3,128,384]{2,1,0:T(8,128)S(1)}, u32[]{:S(2)}, u32[]{:S(2)}) collective-permute-start(f32[3,128,384]{2,1,0:T(8,128)S(1)} %get-tuple-element.69), channel_id=1, source_target_pairs={{0,1},{1,0},{2,3},{3,2},{4,5},{5,4},{6,7},{7,6},{8,9},{9,8},{10,11... | collective-permute-start | bytes 1769480 | tf_op jit(solution)/shard_map/ppermute | solution.py:21
  281.0 16.3 %collective-permute-start.23 = (f32[3,128,384]{2,1,0:T(8,128)S(1)}, f32[3,128,384]{2,1,0:T(8,128)S(1)}, u32[]{:S(2)}, u32[]{:S(2)}) collective-permute-start(f32[3,128,384]{2,1,0:T(8,128)S(1)} %get-tuple-element.70), channel_id=1, source_target_pairs={{0,1},{1,0},{2,3},{3,2},{4,5},{5,4},{6,7},{7,6},{8,9},{9,8},{10,11... | collective-permute-start | bytes 1769480 | tf_op jit(solution)/shard_map/ppermute | solution.py:21
  282.4 15.2 %collective-permute-start.24 = (f32[3,128,384]{2,1,0:T(8,128)S(1)}, f32[3,128,384]{2,1,0:T(8,128)S(1)}, u32[]{:S(2)}, u32[]{:S(2)}) collective-permute-start(f32[3,128,384]{2,1,0:T(8,128)S(1)} %get-tuple-element.71), channel_id=1, source_target_pairs={{0,1},{1,0},{2,3},{3,2},{4,5},{5,4},{6,7},{7,6},{8,9},{9,8},{10,11... | collective-permute-start | bytes 1769480 | tf_op jit(solution)/shard_map/ppermute | solution.py:21
  297.1 11.4 %collective-permute-start.27 = (f32[3,128,384]{2,1,0:T(8,128)}, f32[3,128,384]{2,1,0:T(8,128)S(1)}, u32[]{:S(2)}, u32[]{:S(2)}) collective-permute-start(f32[3,128,384]{2,1,0:T(8,128)} %get-tuple-element.76), channel_id=1, source_target_pairs={{0,1},{1,0},{2,3},{3,2},{4,5},{5,4},{6,7},{7,6},{8,9},{9,8},{10,11... | collective-permute-start | bytes 1769480 | tf_op jit(solution)/shard_map/ppermute | solution.py:21
  297.2 11.6 %collective-permute-start.28 = (f32[3,128,384]{2,1,0:T(8,128)}, f32[3,128,384]{2,1,0:T(8,128)S(1)}, u32[]{:S(2)}, u32[]{:S(2)}) collective-permute-start(f32[3,128,384]{2,1,0:T(8,128)} %get-tuple-element.77), channel_id=1, source_target_pairs={{0,1},{1,0},{2,3},{3,2},{4,5},{5,4},{6,7},{7,6},{8,9},{9,8},{10,11... | collective-permute-start | bytes 1769480 | tf_op jit(solution)/shard_map/ppermute | solution.py:21
  297.6 11.4 %collective-permute-start.29 = (f32[3,128,384]{2,1,0:T(8,128)S(1)}, f32[3,128,384]{2,1,0:T(8,128)S(1)}, u32[]{:S(2)}, u32[]{:S(2)}) collective-permute-start(f32[3,128,384]{2,1,0:T(8,128)S(1)} %get-tuple-element.78), channel_id=1, source_target_pairs={{0,1},{1,0},{2,3},{3,2},{4,5},{5,4},{6,7},{7,6},{8,9},{9,8},{10,11... | collective-permute-start | bytes 1769480 | tf_op jit(solution)/shard_map/ppermute | solution.py:21
  299.7 9.3 %collective-permute-start.30 = (f32[3,128,384]{2,1,0:T(8,128)S(1)}, f32[3,128,384]{2,1,0:T(8,128)S(1)}, u32[]{:S(2)}, u32[]{:S(2)}) collective-permute-start(f32[3,128,384]{2,1,0:T(8,128)S(1)} %get-tuple-element.79), channel_id=1, source_target_pairs={{0,1},{1,0},{2,3},{3,2},{4,5},{5,4},{6,7},{7,6},{8,9},{9,8},{10,11... | collective-permute-start | bytes 1769480 | tf_op jit(solution)/shard_map/ppermute | solution.py:21
  308.8 3.2 collective-permute-start.34
  313.0 4.7 %collective-permute-start.35 = (f32[8,384]{1,0:T(8,128)S(1)}, f32[8,384]{1,0:T(8,128)S(1)}, u32[]{:S(2)}, u32[]{:S(2)}) collective-permute-start(f32[8,384]{1,0:T(8,128)S(1)} %get-tuple-element.89.sums_ref), channel_id=1, source_target_pairs={{0,8},{1,9},{2,10},{3,11},{4,12},{5,13},{6,14},{7,15},{8,0},{9,1},... | collective-permute-start | bytes 36872 | tf_op jit(solution)/shard_map/ppermute | solution.py:21
  (16 other events, 43.8 us)

commit v8 on v7

--- a/solution.py
+++ b/solution.py
@@ -55,7 +55,7 @@
 def make_panel(tile_values, slots, parts, first_rows):
     block_rows, slots_per_row, width, _ = tile_values.shape
     part_rows = block_rows // parts
-    step = math.gcd(math.gcd(part_rows, first_rows), 12)
+    step = math.gcd(math.gcd(part_rows, first_rows), 6)
     steps = part_rows // step
     first_steps = first_rows // step
 

time: 323 us -> 325 us (level)
  no operation moved by 1% of the time
where the time goes in v8:
time: 325 us; the launch traced here: 324 us
  waiting for transfers between devices  188 us (58%)
  Pallas kernels  61.8 us (19%)
  starting transfers between devices  40.8 us (13%)
  local copies, waits for them, and re-layouts  20.3 us (6%)
  other arithmetic  13.1 us (4%)
    ppermute x36, waiting for transfers between devices, swapped(): return lax.ppermute(array, 'grid', pairs)  188 us
    ppermute x36, starting transfers between devices, swapped(): return lax.ppermute(array, 'grid', pairs)  40.8 us
    pallas_call x3, Pallas kernels, expand(): pl.pallas_call(functools.partial(expand_kernel, first, plan), out_shape=[...  40.2 us
    unnamed x25, local copies, waits for them, and re-layouts  10.2 us
    pallas_call x1, Pallas kernels, make_panel(): pl.pallas_call(functools.partial(panel_kernel, first_steps), grid_spec=pl...  9.47 us
    select_n x4, other arithmetic, shared(): given = [jnp.where(odd, a, b) for a, b in zip(pieces[::2], pieces[1::2])]  6.64 us
  transfers between devices with their start and end apart: 36, of which 13 were waited for; matrix products, arithmetic and copies ran while one was open for 7% of the time, Pallas kernels for 14%

profile of v8, /device:TPU:0, one launch (start us, length us, event | category | flops | bytes accessed | tf_op | source)
XLA Modules:
  0.0 324.0 jit_solution(9864713553025773224)
XLA Ops:
  1.0 9.5 %panel.1 = (bf16[24,4,128,128]{3,2,1,0:T(8,128)(2,1)}, bf16[24,128,384]{2,1,0:T(8,128)(2,1)}, bf16[24,128,384]{2,1,0:T(8,128)(2,1)}) custom-call(s32[144]{0:T(256)S(1)} %reshape.159.slot_ref, bf16[48,4,128,128]{3,2,1,0:T(8,128)(2,1)} %refs_0_.5), custom_call_target="tpu_custom_call" | custom-call | bytes 1024 | tf_op jit(solution)/shard_map/panel/pallas_call | solution.py:68
  10.5 3.0 collective-permute-start
  15.0 2.0 collective-permute-start.2
  17.0 2.9 broadcast_select_fusion.6
  19.9 2.1 collective-permute-start.7
  22.1 59.7 %collective-permute-done.refs_2_ = bf16[24,4,128,128]{3,2,1,0:T(8,128)(2,1)S(1)} collective-permute-done((bf16[24,4,128,128]{3,2,1,0:T(8,128)(2,1)}, bf16[24,4,128,128]{3,2,1,0:T(8,128)(2,1)S(1)}, u32[]{:S(2)}, u32[]{:S(2)}) %collective-permute-start) | collective-permute-done | bytes 3145760 | tf_op jit(solution)/shard_map/ppermute | solution.py:21
  81.8 5.1 %collective-permute-start.1 = (bf16[24,128,384]{2,1,0:T(8,128)(2,1)}, bf16[24,128,384]{2,1,0:T(8,128)(2,1)}, u32[]{:S(2)}, u32[]{:S(2)}) collective-permute-start(bf16[24,128,384]{2,1,0:T(8,128)(2,1)} %get-tuple-element.51), channel_id=1, source_target_pairs={{0,4},{1,5},{2,6},{3,7},{12,8},{13,9},{14,10},{15,11},{16,20},{17,... | collective-permute-start | bytes 7077896 | tf_op jit(solution)/shard_map/ppermute | solution.py:21
  88.2 3.3 %broadcast_select_fusion.7 = (bf16[12,128,384]{2,1,0:T(8,128)(2,1)}, bf16[12,128,384]{2,1,0:T(8,128)(2,1)}) fusion(pred[]{:T(512)S(6)} %eq.31, bf16[24,128,384]{2,1,0:T(8,128)(2,1)} %get-tuple-element.51), kind=kLoop, calls=%fused_computation.9 | loop fusion | flops 1179648 | bytes 4718593 | tf_op jit(solution)/shard_map/jit(_where)/select_n | solution.py:355
  92.5 3.0 slice.39
  99.6 2.0 pack.2.near_ref
  101.5 2.2 copy-done
  103.7 31.7 %collective-permute-done.1 = bf16[24,128,384]{2,1,0:T(8,128)(2,1)} collective-permute-done((bf16[24,128,384]{2,1,0:T(8,128)(2,1)}, bf16[24,128,384]{2,1,0:T(8,128)(2,1)}, u32[]{:S(2)}, u32[]{:S(2)}) %collective-permute-start.1) | collective-permute-done | bytes 2359328 | tf_op jit(solution)/shard_map/ppermute | solution.py:21
  135.5 2.1 collective-permute-start.12
  137.6 3.4 %collective-permute-done.3 = bf16[24,128,384]{2,1,0:T(8,128)(2,1)} collective-permute-done((bf16[24,128,384]{2,1,0:T(8,128)(2,1)}, bf16[24,128,384]{2,1,0:T(8,128)(2,1)}, u32[]{:S(2)}, u32[]{:S(2)}) %collective-permute-start.3) | collective-permute-done | bytes 2359328 | tf_op jit(solution)/shard_map/ppermute | solution.py:21
  141.0 3.7 %collective-permute-start.6 = (bf16[24,128,384]{2,1,0:T(8,128)(2,1)}, bf16[24,128,384]{2,1,0:T(8,128)(2,1)}, u32[]{:S(2)}, u32[]{:S(2)}) collective-permute-start(bf16[24,128,384]{2,1,0:T(8,128)(2,1)} %get-tuple-element.54), channel_id=1, source_target_pairs={{0,4},{1,5},{2,6},{3,7},{12,8},{13,9},{14,10},{15,11},{16,20},{17,... | collective-permute-start | bytes 7077896 | tf_op jit(solution)/shard_map/ppermute | solution.py:21
  147.9 2.9 collective-permute-done.9.refs_1_
  152.3 2.4 slice.46
  158.8 33.4 %collective-permute-done.6 = bf16[24,128,384]{2,1,0:T(8,128)(2,1)} collective-permute-done((bf16[24,128,384]{2,1,0:T(8,128)(2,1)}, bf16[24,128,384]{2,1,0:T(8,128)(2,1)}, u32[]{:S(2)}, u32[]{:S(2)}) %collective-permute-start.6) | collective-permute-done | bytes 2359328 | tf_op jit(solution)/shard_map/ppermute | solution.py:21
  192.2 2.1 collective-permute-start.13
  194.7 3.3 %collective-permute-done.8 = bf16[24,128,384]{2,1,0:T(8,128)(2,1)} collective-permute-done((bf16[24,128,384]{2,1,0:T(8,128)(2,1)}, bf16[24,128,384]{2,1,0:T(8,128)(2,1)}, u32[]{:S(2)}, u32[]{:S(2)}) %collective-permute-start.8) | collective-permute-done | bytes 2359328 | tf_op jit(solution)/shard_map/ppermute | solution.py:21
  199.5 1.9 broadcast_select_fusion.1
  201.8 29.2 %collective-permute-done.16.refs_4_ = bf16[12,4,128,128]{3,2,1,0:T(8,128)(2,1)} collective-permute-done((bf16[12,4,128,128]{3,2,1,0:T(8,128)(2,1)}, bf16[12,4,128,128]{3,2,1,0:T(8,128)(2,1)}, u32[]{:S(2)}, u32[]{:S(2)}) %collective-permute-start.16) | collective-permute-done | bytes 1572896 | tf_op jit(solution)/shard_map/ppermute | solution.py:21
  231.0 8.8 %collective-permute-done.11.refs_2_ = bf16[15,4,128,128]{3,2,1,0:T(8,128)(2,1)} collective-permute-done((bf16[15,4,128,128]{3,2,1,0:T(8,128)(2,1)}, bf16[15,4,128,128]{3,2,1,0:T(8,128)(2,1)}, u32[]{:S(2)}, u32[]{:S(2)}) %collective-permute-start.11) | collective-permute-done | bytes 1966112 | tf_op jit(solution)/shard_map/ppermute | solution.py:21
  241.3 1.9 broadcast_select_fusion
  243.6 5.7 %collective-permute-start.31 = (bf16[18,4,128,128]{3,2,1,0:T(8,128)(2,1)}, bf16[18,4,128,128]{3,2,1,0:T(8,128)(2,1)}, u32[]{:S(2)}, u32[]{:S(2)}) collective-permute-start(bf16[18,4,128,128]{3,2,1,0:T(8,128)(2,1)} %pad_maximum_fusion), channel_id=1, source_target_pairs={{0,4},{1,5},{2,6},{3,7},{4,0},{5,1},{6,2},{7,3},{8,12},{9,13},{10,... | collective-permute-start | bytes 7077896 | tf_op jit(solution)/shard_map/ppermute | solution.py:21
  250.6 19.5 %expand.3 = (f32[24,128,384]{2,1,0:T(8,128)S(1)}, f32[3,128,384]{2,1,0:T(8,128)S(1)}, f32[3,128,384]{2,1,0:T(8,128)S(1)}, f32[3,128,384]{2,1,0:T(8,128)S(1)}, f3...) custom-call(s32[4]{0:T(128)S(1)} %iota_xor_fusion.order_ref, ...), custom_call_target="tpu_custom_call" | custom-call | bytes 1024 | tf_op jit(solution)/shard_map/expand/pallas_call | solution.py:209
  270.8 9.7 %collective-permute-done.25.refs_3_ = bf16[15,4,128,128]{3,2,1,0:T(8,128)(2,1)S(1)} collective-permute-done((bf16[15,4,128,128]{3,2,1,0:T(8,128)(2,1)}, bf16[15,4,128,128]{3,2,1,0:T(8,128)(2,1)S(1)}, u32[]{:S(2)}, u32[]{:S(2)}) %collective-permute-start.25) | collective-permute-done | bytes 1966112 | tf_op jit(solution)/shard_map/ppermute | solution.py:21
  285.5 12.6 %expand.4 = (f32[15,128,384]{2,1,0:T(8,128)S(1)}, f32[3,128,384]{2,1,0:T(8,128)S(1)}, f32[3,128,384]{2,1,0:T(8,128)}, f32[3,128,384]{2,1,0:T(8,128)}, f32[3,128,...) custom-call(s32[4]{0:T(128)S(1)} %iota_xor_fusion.order_ref, s32[768]{0:T(1024)S(1)} %add.105.index_ref, ...), custom_call_target="tpu_custom_call" | custom-call | bytes 1024 | tf_op jit(solution)/shard_map/expand/pallas_call | solution.py:209
  301.6 8.1 %expand.5 = (f32[9,128,384]{2,1,0:T(8,128)S(1)}, f32[3,128,384]{2,1,0:T(8,128)S(1)}, f32[3,128,384]{2,1,0:T(8,128)S(1)}, f32[3,128,384]{2,1,0:T(8,128)S(1)}) custom-call(s32[4]{0:T(128)S(1)} %iota_xor_fusion.order_ref, s32[768]{0:T(1024)S(1)} %add.105.index_ref, bf16[24,128,768]{2,1,0:T(8,128)(2,1)S(1)} %bitcast.9, bf16[24,128,768]{2,1,0:T(8,128)(2,1)S(1)} %pack.3.far_ref, ...), custom_call_target="tpu_custom_call" | custom-call | bytes 1024 | tf_op jit(solution)/shard_map/expand/pallas_call | solution.py:209
  314.5 2.0 collective-permute-start.35
  316.5 2.6 collective-permute-done.35.got_ref
  319.1 4.8 %scale.1 = f32[48,3,128,128]{3,2,1,0:T(8,128)} custom-call(f32[8,384]{1,0:T(8,128)S(1)} %get-tuple-element.89.sums_ref, f32[8,384]{1,0:T(8,128)S(1)} %collective-permute-done.35.got_ref, f32[48,128,384]{2,1,0:T(8,128)S(1)} %get-tuple-element.90.squared_ref), custom_call_target="tpu_custom_call" | custom-call | bytes 1024 | tf_op jit(solution)/shard_map/scale/pallas_call | solution.py:298
  (106 shorter events, 36.7 us)
Async XLA Ops:
  10.5 71.3 %collective-permute-start = (bf16[24,4,128,128]{3,2,1,0:T(8,128)(2,1)}, bf16[24,4,128,128]{3,2,1,0:T(8,128)(2,1)S(1)}, u32[]{:S(2)}, u32[]{:S(2)}) collective-permute-start(bf16[24,4,128,128]{3,2,1,0:T(8,128)(2,1)} %get-tuple-element.49), channel_id=1, source_target_pairs={{0,4},{1,5},{2,6},{3,7},{4,0},{5,1},{6,2},{7,3},{8,12},{9,13},{10,... | collective-permute-start | bytes 9437192 | tf_op jit(solution)/shard_map/ppermute | solution.py:21
  13.5 137.3 %collective-permute-start.9 = (bf16[48,4,128,128]{3,2,1,0:T(8,128)(2,1)}, bf16[48,4,128,128]{3,2,1,0:T(8,128)(2,1)}, u32[]{:S(2)}, u32[]{:S(2)}) collective-permute-start(bf16[48,4,128,128]{3,2,1,0:T(8,128)(2,1)} %refs_0_.5), channel_id=1, source_target_pairs={{0,2},{1,3},{2,0},{3,1},{4,6},{5,7},{6,4},{7,5},{8,10},{9,11},{10,... | collective-permute-start | bytes 18874376 | tf_op jit(solution)/shard_map/ppermute | solution.py:21
  15.0 5.0 %collective-permute-start.2 = (bf16[24,128,384]{2,1,0:T(8,128)(2,1)}, bf16[24,128,384]{2,1,0:T(8,128)(2,1)}, u32[]{:S(2)}, u32[]{:S(2)}) collective-permute-start(bf16[24,128,384]{2,1,0:T(8,128)(2,1)} %get-tuple-element.51), channel_id=1, source_target_pairs={{4,8},{5,9},{6,10},{7,11},{8,4},{9,5},{10,6},{11,7},{20,24},{21,25... | collective-permute-start | bytes 7077896 | tf_op jit(solution)/shard_map/ppermute | solution.py:21
  19.9 71.5 %collective-permute-start.5 = (bf16[12,128,384]{2,1,0:T(8,128)(2,1)S(1)}, bf16[12,128,384]{2,1,0:T(8,128)(2,1)S(1)}, u32[]{:S(2)}, u32[]{:S(2)}) collective-permute-start(bf16[12,128,384]{2,1,0:T(8,128)(2,1)S(1)} %get-tuple-element.108), channel_id=1, source_target_pairs={{0,1},{1,0},{2,3},{3,2},{4,5},{5,4},{6,7},{7,6},{8,9},{9,8},{10,11... | collective-permute-start | bytes 3538952 | tf_op jit(solution)/shard_map/ppermute | solution.py:21
  19.9 83.8 %collective-permute-start.7 = (bf16[24,128,384]{2,1,0:T(8,128)(2,1)}, bf16[24,128,384]{2,1,0:T(8,128)(2,1)}, u32[]{:S(2)}, u32[]{:S(2)}) collective-permute-start(bf16[24,128,384]{2,1,0:T(8,128)(2,1)} %get-tuple-element.54), channel_id=1, source_target_pairs={{4,8},{5,9},{6,10},{7,11},{8,4},{9,5},{10,6},{11,7},{20,24},{21,25... | collective-permute-start | bytes 7077896 | tf_op jit(solution)/shard_map/ppermute | solution.py:21
  81.8 53.7 %collective-permute-start.1 = (bf16[24,128,384]{2,1,0:T(8,128)(2,1)}, bf16[24,128,384]{2,1,0:T(8,128)(2,1)}, u32[]{:S(2)}, u32[]{:S(2)}) collective-permute-start(bf16[24,128,384]{2,1,0:T(8,128)(2,1)} %get-tuple-element.51), channel_id=1, source_target_pairs={{0,4},{1,5},{2,6},{3,7},{12,8},{13,9},{14,10},{15,11},{16,20},{17,... | collective-permute-start | bytes 7077896 | tf_op jit(solution)/shard_map/ppermute | solution.py:21
  86.9 54.1 %collective-permute-start.3 = (bf16[24,128,384]{2,1,0:T(8,128)(2,1)}, bf16[24,128,384]{2,1,0:T(8,128)(2,1)}, u32[]{:S(2)}, u32[]{:S(2)}) collective-permute-start(bf16[24,128,384]{2,1,0:T(8,128)(2,1)} %collective-permute-done.2), channel_id=1, source_target_pairs={{4,0},{5,1},{6,2},{7,3},{8,12},{9,13},{10,14},{11,15},{20,16},{21,... | collective-permute-start | bytes 7077896 | tf_op jit(solution)/shard_map/ppermute | solution.py:21
  92.5 3.2 collective-permute-start.4
  135.5 23.4 %collective-permute-start.12 = (bf16[24,128,384]{2,1,0:T(8,128)(2,1)}, bf16[24,128,384]{2,1,0:T(8,128)(2,1)}, u32[]{:S(2)}, u32[]{:S(2)}) collective-permute-start(bf16[24,128,384]{2,1,0:T(8,128)(2,1)} %collective-permute-done.1), channel_id=1, source_target_pairs={{4,8},{5,9},{6,10},{7,11},{8,4},{9,5},{10,6},{11,7},{20,24},{21,25... | collective-permute-start | bytes 7077896 | tf_op jit(solution)/shard_map/ppermute | solution.py:21
  141.0 51.2 %collective-permute-start.6 = (bf16[24,128,384]{2,1,0:T(8,128)(2,1)}, bf16[24,128,384]{2,1,0:T(8,128)(2,1)}, u32[]{:S(2)}, u32[]{:S(2)}) collective-permute-start(bf16[24,128,384]{2,1,0:T(8,128)(2,1)} %get-tuple-element.54), channel_id=1, source_target_pairs={{0,4},{1,5},{2,6},{3,7},{12,8},{13,9},{14,10},{15,11},{16,20},{17,... | collective-permute-start | bytes 7077896 | tf_op jit(solution)/shard_map/ppermute | solution.py:21
  144.8 53.3 %collective-permute-start.8 = (bf16[24,128,384]{2,1,0:T(8,128)(2,1)}, bf16[24,128,384]{2,1,0:T(8,128)(2,1)}, u32[]{:S(2)}, u32[]{:S(2)}) collective-permute-start(bf16[24,128,384]{2,1,0:T(8,128)(2,1)} %collective-permute-done.7), channel_id=1, source_target_pairs={{4,0},{5,1},{6,2},{7,3},{8,12},{9,13},{10,14},{11,15},{20,16},{21,... | collective-permute-start | bytes 7077896 | tf_op jit(solution)/shard_map/ppermute | solution.py:21
  150.8 47.3 %collective-permute-start.10 = (bf16[12,4,128,128]{3,2,1,0:T(8,128)(2,1)}, bf16[12,4,128,128]{3,2,1,0:T(8,128)(2,1)}, u32[]{:S(2)}, u32[]{:S(2)}) collective-permute-start(bf16[12,4,128,128]{3,2,1,0:T(8,128)(2,1)} %get-tuple-element.56), channel_id=1, source_target_pairs={{0,2},{1,3},{2,0},{3,1},{4,6},{5,7},{6,4},{7,5},{8,10},{9,11},{10,... | collective-permute-start | bytes 4718600 | tf_op jit(solution)/shard_map/ppermute | solution.py:21
  192.2 49.1 %collective-permute-start.13 = (bf16[24,128,384]{2,1,0:T(8,128)(2,1)}, bf16[24,128,384]{2,1,0:T(8,128)(2,1)}, u32[]{:S(2)}, u32[]{:S(2)}) collective-permute-start(bf16[24,128,384]{2,1,0:T(8,128)(2,1)} %collective-permute-done.6), channel_id=1, source_target_pairs={{4,8},{5,9},{6,10},{7,11},{8,4},{9,5},{10,6},{11,7},{20,24},{21,25... | collective-permute-start | bytes 7077896 | tf_op jit(solution)/shard_map/ppermute | solution.py:21
  198.0 41.8 %collective-permute-start.11 = (bf16[15,4,128,128]{3,2,1,0:T(8,128)(2,1)}, bf16[15,4,128,128]{3,2,1,0:T(8,128)(2,1)}, u32[]{:S(2)}, u32[]{:S(2)}) collective-permute-start(bf16[15,4,128,128]{3,2,1,0:T(8,128)(2,1)} %slice.39), channel_id=1, source_target_pairs={{0,4},{1,5},{2,6},{3,7},{4,0},{5,1},{6,2},{7,3},{8,12},{9,13},{10,... | collective-permute-start | bytes 5898248 | tf_op jit(solution)/shard_map/ppermute | solution.py:21
  198.0 32.9 %collective-permute-start.16 = (bf16[12,4,128,128]{3,2,1,0:T(8,128)(2,1)}, bf16[12,4,128,128]{3,2,1,0:T(8,128)(2,1)}, u32[]{:S(2)}, u32[]{:S(2)}) collective-permute-start(bf16[12,4,128,128]{3,2,1,0:T(8,128)(2,1)} %get-tuple-element.62), channel_id=1, source_target_pairs={{0,2},{1,3},{2,0},{3,1},{4,6},{5,7},{6,4},{7,5},{8,10},{9,11},{10,... | collective-permute-start | bytes 4718600 | tf_op jit(solution)/shard_map/ppermute | solution.py:21
  201.7 47.6 %collective-permute-start.14 = (bf16[12,128,384]{2,1,0:T(8,128)(2,1)S(1)}, bf16[12,128,384]{2,1,0:T(8,128)(2,1)S(1)}, u32[]{:S(2)}, u32[]{:S(2)}) collective-permute-start(bf16[12,128,384]{2,1,0:T(8,128)(2,1)S(1)} %get-tuple-element.106), channel_id=1, source_target_pairs={{0,1},{1,0},{2,3},{3,2},{4,5},{5,4},{6,7},{7,6},{8,9},{9,8},{10,11... | collective-permute-start | bytes 3538952 | tf_op jit(solution)/shard_map/ppermute | solution.py:21
  239.8 40.8 %collective-permute-start.25 = (bf16[15,4,128,128]{3,2,1,0:T(8,128)(2,1)}, bf16[15,4,128,128]{3,2,1,0:T(8,128)(2,1)S(1)}, u32[]{:S(2)}, u32[]{:S(2)}) collective-permute-start(bf16[15,4,128,128]{3,2,1,0:T(8,128)(2,1)} %collective-permute-done.11.refs_2_), channel_id=1, source_target_pairs={{0,2},{1,3},{2,0},{3,1},{4,6},{5,7},{6,4},{7,5},{8,10},{9,11},{10,... | collective-permute-start | bytes 5898248 | tf_op jit(solution)/shard_map/ppermute | solution.py:21
  243.5 5.8 %collective-permute-start.15 = (bf16[12,128,384]{2,1,0:T(8,128)(2,1)S(1)}, bf16[12,128,384]{2,1,0:T(8,128)(2,1)S(1)}, u32[]{:S(2)}, u32[]{:S(2)}) collective-permute-start(bf16[12,128,384]{2,1,0:T(8,128)(2,1)S(1)} %get-tuple-element.104), channel_id=1, source_target_pairs={{0,1},{1,0},{2,3},{3,2},{4,5},{5,4},{6,7},{7,6},{8,9},{9,8},{10,11... | collective-permute-start | bytes 3538952 | tf_op jit(solution)/shard_map/ppermute | solution.py:21
  243.6 58.0 %collective-permute-start.31 = (bf16[18,4,128,128]{3,2,1,0:T(8,128)(2,1)}, bf16[18,4,128,128]{3,2,1,0:T(8,128)(2,1)}, u32[]{:S(2)}, u32[]{:S(2)}) collective-permute-start(bf16[18,4,128,128]{3,2,1,0:T(8,128)(2,1)} %pad_maximum_fusion), channel_id=1, source_target_pairs={{0,4},{1,5},{2,6},{3,7},{4,0},{5,1},{6,2},{7,3},{8,12},{9,13},{10,... | collective-permute-start | bytes 7077896 | tf_op jit(solution)/shard_map/ppermute | solution.py:21
  270.1 11.8 %collective-permute-start.17 = (f32[3,128,384]{2,1,0:T(8,128)S(1)}, f32[3,128,384]{2,1,0:T(8,128)S(1)}, u32[]{:S(2)}, u32[]{:S(2)}) collective-permute-start(f32[3,128,384]{2,1,0:T(8,128)S(1)} %get-tuple-element.64), channel_id=1, source_target_pairs={{0,1},{1,0},{2,3},{3,2},{4,5},{5,4},{6,7},{7,6},{8,9},{9,8},{10,11... | collective-permute-start | bytes 1769480 | tf_op jit(solution)/shard_map/ppermute | solution.py:21
  270.3 12.0 %collective-permute-start.18 = (f32[3,128,384]{2,1,0:T(8,128)S(1)}, f32[3,128,384]{2,1,0:T(8,128)S(1)}, u32[]{:S(2)}, u32[]{:S(2)}) collective-permute-start(f32[3,128,384]{2,1,0:T(8,128)S(1)} %get-tuple-element.65), channel_id=1, source_target_pairs={{0,1},{1,0},{2,3},{3,2},{4,5},{5,4},{6,7},{7,6},{8,9},{9,8},{10,11... | collective-permute-start | bytes 1769480 | tf_op jit(solution)/shard_map/ppermute | solution.py:21
  270.7 11.8 %collective-permute-start.19 = (f32[3,128,384]{2,1,0:T(8,128)S(1)}, f32[3,128,384]{2,1,0:T(8,128)S(1)}, u32[]{:S(2)}, u32[]{:S(2)}) collective-permute-start(f32[3,128,384]{2,1,0:T(8,128)S(1)} %get-tuple-element.66), channel_id=1, source_target_pairs={{0,1},{1,0},{2,3},{3,2},{4,5},{5,4},{6,7},{7,6},{8,9},{9,8},{10,11... | collective-permute-start | bytes 1769480 | tf_op jit(solution)/shard_map/ppermute | solution.py:21
  281.9 16.3 %collective-permute-start.21 = (f32[3,128,384]{2,1,0:T(8,128)S(1)}, f32[3,128,384]{2,1,0:T(8,128)S(1)}, u32[]{:S(2)}, u32[]{:S(2)}) collective-permute-start(f32[3,128,384]{2,1,0:T(8,128)S(1)} %get-tuple-element.68), channel_id=1, source_target_pairs={{0,1},{1,0},{2,3},{3,2},{4,5},{5,4},{6,7},{7,6},{8,9},{9,8},{10,11... | collective-permute-start | bytes 1769480 | tf_op jit(solution)/shard_map/ppermute | solution.py:21
  282.4 16.2 %collective-permute-start.22 = (f32[3,128,384]{2,1,0:T(8,128)S(1)}, f32[3,128,384]{2,1,0:T(8,128)S(1)}, u32[]{:S(2)}, u32[]{:S(2)}) collective-permute-start(f32[3,128,384]{2,1,0:T(8,128)S(1)} %get-tuple-element.69), channel_id=1, source_target_pairs={{0,1},{1,0},{2,3},{3,2},{4,5},{5,4},{6,7},{7,6},{8,9},{9,8},{10,11... | collective-permute-start | bytes 1769480 | tf_op jit(solution)/shard_map/ppermute | solution.py:21
  282.4 16.3 %collective-permute-start.23 = (f32[3,128,384]{2,1,0:T(8,128)S(1)}, f32[3,128,384]{2,1,0:T(8,128)S(1)}, u32[]{:S(2)}, u32[]{:S(2)}) collective-permute-start(f32[3,128,384]{2,1,0:T(8,128)S(1)} %get-tuple-element.70), channel_id=1, source_target_pairs={{0,1},{1,0},{2,3},{3,2},{4,5},{5,4},{6,7},{7,6},{8,9},{9,8},{10,11... | collective-permute-start | bytes 1769480 | tf_op jit(solution)/shard_map/ppermute | solution.py:21
  283.9 15.2 %collective-permute-start.24 = (f32[3,128,384]{2,1,0:T(8,128)S(1)}, f32[3,128,384]{2,1,0:T(8,128)S(1)}, u32[]{:S(2)}, u32[]{:S(2)}) collective-permute-start(f32[3,128,384]{2,1,0:T(8,128)S(1)} %get-tuple-element.71), channel_id=1, source_target_pairs={{0,1},{1,0},{2,3},{3,2},{4,5},{5,4},{6,7},{7,6},{8,9},{9,8},{10,11... | collective-permute-start | bytes 1769480 | tf_op jit(solution)/shard_map/ppermute | solution.py:21
  298.6 11.4 %collective-permute-start.27 = (f32[3,128,384]{2,1,0:T(8,128)}, f32[3,128,384]{2,1,0:T(8,128)S(1)}, u32[]{:S(2)}, u32[]{:S(2)}) collective-permute-start(f32[3,128,384]{2,1,0:T(8,128)} %get-tuple-element.76), channel_id=1, source_target_pairs={{0,1},{1,0},{2,3},{3,2},{4,5},{5,4},{6,7},{7,6},{8,9},{9,8},{10,11... | collective-permute-start | bytes 1769480 | tf_op jit(solution)/shard_map/ppermute | solution.py:21
  298.7 11.6 %collective-permute-start.28 = (f32[3,128,384]{2,1,0:T(8,128)}, f32[3,128,384]{2,1,0:T(8,128)S(1)}, u32[]{:S(2)}, u32[]{:S(2)}) collective-permute-start(f32[3,128,384]{2,1,0:T(8,128)} %get-tuple-element.77), channel_id=1, source_target_pairs={{0,1},{1,0},{2,3},{3,2},{4,5},{5,4},{6,7},{7,6},{8,9},{9,8},{10,11... | collective-permute-start | bytes 1769480 | tf_op jit(solution)/shard_map/ppermute | solution.py:21
  299.1 11.4 %collective-permute-start.29 = (f32[3,128,384]{2,1,0:T(8,128)S(1)}, f32[3,128,384]{2,1,0:T(8,128)S(1)}, u32[]{:S(2)}, u32[]{:S(2)}) collective-permute-start(f32[3,128,384]{2,1,0:T(8,128)S(1)} %get-tuple-element.78), channel_id=1, source_target_pairs={{0,1},{1,0},{2,3},{3,2},{4,5},{5,4},{6,7},{7,6},{8,9},{9,8},{10,11... | collective-permute-start | bytes 1769480 | tf_op jit(solution)/shard_map/ppermute | solution.py:21
  301.2 9.3 %collective-permute-start.30 = (f32[3,128,384]{2,1,0:T(8,128)S(1)}, f32[3,128,384]{2,1,0:T(8,128)S(1)}, u32[]{:S(2)}, u32[]{:S(2)}) collective-permute-start(f32[3,128,384]{2,1,0:T(8,128)S(1)} %get-tuple-element.79), channel_id=1, source_target_pairs={{0,1},{1,0},{2,3},{3,2},{4,5},{5,4},{6,7},{7,6},{8,9},{9,8},{10,11... | collective-permute-start | bytes 1769480 | tf_op jit(solution)/shard_map/ppermute | solution.py:21
  310.3 3.2 collective-permute-start.34
  314.5 4.7 %collective-permute-start.35 = (f32[8,384]{1,0:T(8,128)S(1)}, f32[8,384]{1,0:T(8,128)S(1)}, u32[]{:S(2)}, u32[]{:S(2)}) collective-permute-start(f32[8,384]{1,0:T(8,128)S(1)} %get-tuple-element.89.sums_ref), channel_id=1, source_target_pairs={{0,8},{1,9},{2,10},{3,11},{4,12},{5,13},{6,14},{7,15},{8,0},{9,1},... | collective-permute-start | bytes 36872 | tf_op jit(solution)/shard_map/ppermute | solution.py:21
  (16 other events, 43.7 us)
